TPU v7x, 128 devices: a whole 4x4x4 slice. The times are simulated.
128 devices in a mesh: ctx: 16 (over y, z), tp: 8 (over x, core).
Axes of the slice: x: 4, y: 4, z: 4, core: 2. Of those that a mesh axis runs over, the one named last changes fastest.
Arguments:
- queries: bfloat16 [16384, 4096], P('ctx', 'tp'), may hold values from -15 to 15
- keys: bfloat16 [16384, 256], P('ctx'), may hold values from -6 to 6
- values: bfloat16 [16384, 256], P('ctx'), may hold values from -6 to 6
- out_proj: bfloat16 [4096, 4096], P('tp', 'ctx'), may hold values from -0.09375 to 0.09375
- residual: bfloat16 [16384, 4096], P(('ctx', 'tp')), may hold values from -6 to 6
- norm_gain: float32 [4096], replicated, may hold values from 0.1 to 1.9
- expert_ids: int32 [16384, 4], P(('ctx', 'tp')), may hold values from 0 to 127, all different within a row; in each aligned block of 128 rows (0 to 127, 128 to 255, ...) at most 6 rows name the same one
- route_weights: float32 [16384, 4], P(('ctx', 'tp')), may hold values from 0.05 to 1
- w_in: bfloat16 [128, 4096, 1536], P(('ctx', 'tp')), may hold values from -0.09375 to 0.09375
- w_out: bfloat16 [128, 768, 4096], P(('ctx', 'tp')), may hold values from -0.21875 to 0.21875
Outputs:
- layer_out: bfloat16 [16384, 4096], P(('ctx', 'tp'))
Inputs may be any that keep to these rules, and one draw needn't show every extreme that they name: `expert_ids`: each token names 4 different experts. Among the 128 tokens of one device (aligned blocks of rows) no expert is named by more than 6 of them, and in every draw some expert is named by exactly 6 in some block.
All inputs are finite; a program needn't handle non-finite values.
Results may differ from a plain program's by a relative error of at most 0.015.
Values may be sent and summed in bfloat16 or wider, within the bound.
No kernel may reach another device: no remote copies, remote signals or barrier semaphores. Data moves between devices by JAX's collectives and lax.ppermute only.
A program may use at most 128 MiB of HBM per device.

v0:
```python
import math

import jax
import jax.numpy as jnp
from jax import lax
from jax.sharding import PartitionSpec as P

HEADS = 32
KV_HEADS = 2
HEAD_DIM = 128
FF = 768
SEQS = 1


def body(
    queries, keys, values, out_proj, residual, norm_gain, expert_ids, route_weights, w_in, w_out
):
    ctx_count = lax.axis_size("ctx")
    tp_count = lax.axis_size("tp")
    dev_count = ctx_count * tp_count
    ctx_index = lax.axis_index("ctx")
    tp_index = lax.axis_index("tp")
    query_rows = queries.shape[0]
    heads_here = queries.shape[1] // HEAD_DIM
    head_group = HEADS // KV_HEADS
    kv_index = tp_index * heads_here // head_group
    own_keys = lax.dynamic_slice_in_dim(keys, kv_index * HEAD_DIM, HEAD_DIM, 1)
    own_values = lax.dynamic_slice_in_dim(values, kv_index * HEAD_DIM, HEAD_DIM, 1)
    seq_len = query_rows * ctx_count // SEQS
    query_first = ctx_index * query_rows
    query_pos = query_first + jnp.arange(query_rows, dtype=jnp.int32)
    seq_start = query_first // seq_len * seq_len
    score_scale = HEAD_DIM ** (-0.5)
    groups = (queries, query_pos)
    prepared = []
    group_rows, group_pos = groups
    row_total = group_rows.shape[0]
    prepared.append(
        (group_rows.reshape(row_total, heads_here, HEAD_DIM), group_pos, jnp.max(group_pos))
    )
    initial = tuple(
        (
            (
                jnp.full((heads_here, item[0].shape[0]), -1e30, jnp.float32),
                jnp.zeros((heads_here, item[0].shape[0]), jnp.float32),
                jnp.zeros((heads_here, item[0].shape[0], HEAD_DIM), jnp.float32),
            )
            for item in prepared
        )
    )
    piece_keys = lax.all_gather(own_keys, "ctx", axis=0, tiled=True)
    piece_values = lax.all_gather(own_values, "ctx", axis=0, tiled=True)
    key_rows = piece_keys.shape[0]
    block_width = math.gcd(key_rows, 512)
    block_count = key_rows // block_width

    def one_block(block_index, running):
        offset = block_index * block_width
        block_keys = lax.dynamic_slice_in_dim(piece_keys, offset, block_width, 0)
        block_values = lax.dynamic_slice_in_dim(piece_values, offset, block_width, 0)
        key_pos = offset + jnp.arange(block_width, dtype=jnp.int32)
        results = []
        for state, (query_heads, group_pos, group_last) in zip(running, prepared):

            def update(current, query_heads=query_heads, group_pos=group_pos):
                run_max, run_sum, run_acc = current
                scores = (
                    jnp.einsum(
                        "qhd,kd->hqk", query_heads, block_keys, preferred_element_type=jnp.float32
                    )
                    * score_scale
                )
                allowed = (key_pos[None, :] <= group_pos[:, None]) & (key_pos[None, :] >= seq_start)
                scores = jnp.where(allowed[None], scores, -1e30)
                new_max = jnp.maximum(run_max, jnp.max(scores, axis=-1))
                factor = jnp.exp(run_max - new_max)
                weights_now = jnp.where(allowed[None], jnp.exp(scores - new_max[..., None]), 0.0)
                new_sum = run_sum * factor + jnp.sum(weights_now, axis=-1)
                new_acc = run_acc * factor[..., None] + jnp.einsum(
                    "hqk,kd->hqd",
                    weights_now.astype(jnp.bfloat16),
                    block_values,
                    preferred_element_type=jnp.float32,
                )
                return (new_max, new_sum, new_acc)

            needed = (offset <= group_last) & (offset + block_width > seq_start)
            results.append(lax.cond(needed, update, lambda kept: kept, state))
        return tuple(results)

    finals = lax.fori_loop(0, block_count, one_block, initial)
    outputs_list = []
    for run_max, run_sum, run_acc in finals:
        row_total = run_acc.shape[1]
        outputs_list.append(
            (run_acc / run_sum[..., None])
            .transpose(1, 0, 2)
            .reshape(row_total, heads_here * HEAD_DIM)
            .astype(jnp.bfloat16)
        )
    attended = outputs_list[0]
    full_proj = lax.all_gather(out_proj, "ctx", axis=1, tiled=True)
    attn_out = lax.psum_scatter(
        jnp.dot(attended, full_proj, preferred_element_type=jnp.float32).astype(jnp.bfloat16),
        "tp",
        scatter_dimension=0,
        tiled=True,
    ).astype(jnp.float32)
    hidden_state = (residual.astype(jnp.float32) + attn_out).astype(jnp.bfloat16)
    hidden_wide = hidden_state.astype(jnp.float32)
    variance = jnp.mean(hidden_wide * hidden_wide, axis=-1, keepdims=True)
    normed = (hidden_wide * lax.rsqrt(variance + 1e-06) * norm_gain).astype(jnp.bfloat16)
    mixing = route_weights / jnp.sum(route_weights, axis=-1, keepdims=True)
    route_count = expert_ids.shape[0] * expert_ids.shape[1]
    capacity = route_count * 3 // (2 * dev_count)
    flat_ids = expert_ids.reshape(-1)
    one_hot = (flat_ids[:, None] == jnp.arange(dev_count, dtype=jnp.int32)[None, :]).astype(
        jnp.int32
    )
    earlier = jnp.cumsum(one_hot, axis=0) - one_hot
    slot_number = jnp.sum(earlier * one_hot, axis=1)
    target = flat_ids * capacity + slot_number
    source_rows = normed[jnp.arange(route_count, dtype=jnp.int32) // expert_ids.shape[1]]
    outgoing = (
        jnp.zeros((dev_count * capacity, normed.shape[1]), jnp.bfloat16).at[target].set(source_rows)
    )
    gate_up = w_in[0]
    down_weight = w_out[0]
    packed = outgoing.reshape(dev_count, capacity, -1)
    arrived = lax.all_to_all(packed, ("ctx", "tp"), split_axis=0, concat_axis=0, tiled=True)
    flat_rows = arrived.reshape(-1, arrived.shape[-1])
    gate_up_out = jnp.dot(flat_rows, gate_up, preferred_element_type=jnp.float32)
    active = (jax.nn.silu(gate_up_out[:, :FF]) * gate_up_out[:, FF:]).astype(jnp.bfloat16)
    result = jnp.dot(active, down_weight, preferred_element_type=jnp.float32).astype(jnp.bfloat16)
    processed = result.reshape(arrived.shape[0], arrived.shape[1], -1)
    returned = lax.all_to_all(processed, ("ctx", "tp"), split_axis=0, concat_axis=0, tiled=True)
    back_rows = returned.reshape(dev_count * capacity, -1)[target]
    combined = jnp.sum(
        mixing[:, :, None]
        * back_rows.astype(jnp.float32).reshape(expert_ids.shape[0], expert_ids.shape[1], -1),
        axis=1,
    )
    return (hidden_wide + combined).astype(jnp.bfloat16)


def solution(mesh):
    return jax.shard_map(
        body,
        mesh=mesh,
        in_specs=(
            P("ctx", "tp"),
            P("ctx", None),
            P("ctx", None),
            P("tp", "ctx"),
            P(("ctx", "tp"), None),
            P(),
            P(("ctx", "tp"), None),
            P(("ctx", "tp"), None),
            P(("ctx", "tp"), None, None),
            P(("ctx", "tp"), None, None),
        ),
        out_specs=P(("ctx", "tp"), None),
        check_vma=False,
    )
```

profile of v0, /device:TPU:6, one launch (start us, length us, event | category | flops | bytes accessed | tf_op | source)
XLA Modules:
  0.0 891.5 jit_solution(2232171572734104127)
XLA Ops:
  6.5 1.0 copy-done
  7.6 0.7 constant_dynamic-slice_fusion.1
  8.4 1.7 constant_dynamic-slice_fusion
  10.1 0.7 all-gather.8.cloned.1.call-update
  10.9 0.7 add_reduce_fusion
  11.6 1.5 copy.14
  13.1 0.7 copy.15
  13.8 49.8 %all-gather.4.cloned.1.call-done = bf16[16384,128]{1,0:T(8,128)(2,1)} async-done(((bf16[1024,128]{1,0:T(8,128)(2,1)}), bf16[16384,128]{1,0:T(8,128)(2,1)}) %all-gather.4.cloned.1.call-update) | async-done | bytes 4194320 | tf_op jit(solution)/shard_map/all_gather | solution.py:51
  63.5 53.4 %all-gather.6.cloned.1.call-done = bf16[16384,128]{1,0:T(8,128)(2,1)} async-done(((bf16[1024,128]{1,0:T(8,128)(2,1)}), bf16[16384,128]{1,0:T(8,128)(2,1)}) %all-gather.6.cloned.1.call-update) | async-done | bytes 4194320 | tf_op jit(solution)/shard_map/all_gather | solution.py:52
  116.9 1.5 broadcast_in_dim.58
  118.4 45.6 %while.18 = (s32[]{:T(128)}, f32[4,1024]{1,0:T(4,128)S(1)}, f32[4,1024]{1,0:T(4,128)S(1)}, f32[4,1024,128]{2,1,0:T(8,128)}, s32[]{:T(128)}, /*index=5*/s32[]{:T(...) while((s32[]{:T(128)}, f32[4,1024]{1,0:T(4,128)S(1)}, ...), condition=%wide.region_6.7_spmd.clone, body=%wide.region_1.6_spmd.clone.sunk | while | flops 1103112192 | bytes 49833376 | solution.py:91
  119.1 10.6 %conditional.3 = ((f32[4,1024]{1,0:T(4,128)S(1)}, f32[4,1024]{1,0:T(4,128)S(1)}, f32[4,1024,128]{2,1,0:T(8,128)})) conditional(s32[]{:T(128)} %convert_element_type.128, (f32[4,1024]{1,0:T(4,128)S(1)}, f32[4,1024]{1,0:T(4,128)S(1)}, f32[4,1024,128]{2,1,0:T(8,128)}) %tuple.55, (s32[]{:T(128)}, s32[512]{0:T(512)S(1)}, s32[]{:T(128)}, s32[]{:T(128)}, ...), branch_computations={%region_2.2_spmd, %region_3.5_spmd} | conditional | flops 1103112192 | bytes 49826956 | solution.py:88
  119.2 0.4 compare_and_fusion
  119.6 2.5 fusion.2
  122.2 2.1 fusion.4
  124.3 4.1 multiply_add_fusion
  128.4 1.4 copy-done.5
  130.5 10.6 %conditional.3 = ((f32[4,1024]{1,0:T(4,128)S(1)}, f32[4,1024]{1,0:T(4,128)S(1)}, f32[4,1024,128]{2,1,0:T(8,128)})) conditional(s32[]{:T(128)} %convert_element_type.128, (f32[4,1024]{1,0:T(4,128)S(1)}, f32[4,1024]{1,0:T(4,128)S(1)}, f32[4,1024,128]{2,1,0:T(8,128)}) %tuple.55, (s32[]{:T(128)}, s32[512]{0:T(512)S(1)}, s32[]{:T(128)}, s32[]{:T(128)}, ...), branch_computations={%region_2.2_spmd, %region_3.5_spmd} | conditional | flops 1103112192 | bytes 49826956 | solution.py:88
  130.5 0.4 compare_and_fusion
  131.0 2.5 fusion.2
  133.5 2.1 fusion.4
  135.7 4.1 multiply_add_fusion
  139.8 1.4 copy-done.5
  164.0 2.1 copy.16
  166.1 1.2 divide_convert_fusion
  167.4 9.0 %all-gather.8.cloned.1.call-done = bf16[512,4096]{1,0:T(8,128)(2,1)} async-done(((bf16[512,256]{1,0:T(8,128)(2,1)}), bf16[512,4096]{1,0:T(8,128)(2,1)}) %all-gather.8.cloned.1.call-update) | async-done | bytes 4194320 | tf_op jit(solution)/shard_map/all_gather | solution.py:102
  176.4 10.3 %convolution_convert_fusion = bf16[1024,4096]{1,0:T(8,128)(2,1)} fusion(bf16[1024,512]{0,1:T(8,128)(2,1)} %bitcast.53, bf16[512,4096]{1,0:T(8,128)(2,1)} %all-gather.8.cloned.1.call-done), kind=kOutput, calls=%fused_computation.31 | convolution fusion | flops 4299161600 | bytes 13631488 | tf_op jit(solution)/shard_map/dot_general | solution.py:104
  186.7 0.7 copy-done.7
  187.8 0.2 fusion.35
  188.4 0.2 fusion.34
  188.6 356.0 %reduce-scatter.2.cloned.1.call-done = bf16[128,4096]{1,0:T(8,128)(2,1)} async-done(((bf16[1024,4096]{1,0:T(8,128)(2,1)}), bf16[128,4096]{1,0:T(8,128)(2,1)}) %reduce-scatter.2.cloned.1.call-update) | async-done | bytes 1048592 | tf_op jit(solution)/shard_map/reduce_scatter | solution.py:103
  544.7 1.6 fusion.27
  546.3 1.6 fusion.29
  548.0 22.6 %scatter_custom_fusion = bf16[768,4096]{1,0:T(8,128)(2,1)} fusion(s32[512]{0:T(512)S(1)} %bitcast.57, bf16[128,4096]{1,0:T(8,128)(2,1)S(1)} %fusion.29, s32[1024]{0:T(1024)S(1)} %pad_clamp_fusion.1, bf16[]{:T(256)} %constant.138.clone.1), kind=kCustom, calls=%fused_computation.34 | custom fusion | bytes 6291458 | tf_op jit(solution)/shard_map/scatter | solution.py:125
  570.6 10.1 %reshape.170 = bf16[128,6,4096]{2,1,0:T(8,128)(2,1)} reshape(bf16[768,4096]{1,0:T(8,128)(2,1)} %scatter_custom_fusion) | data formatting | bytes 12582912 | tf_op jit(solution)/shard_map/reshape | solution.py:129
  580.7 107.0 %all_to_all.10 = bf16[128,6,4096]{2,1,0:T(8,128)(2,1)} all-to-all(bf16[128,6,4096]{2,1,0:T(8,128)(2,1)} %reshape.170), channel_id=1, replica_groups=mesh['ctx'=16,'tp'=8] {'ctx','tp'}, dimensions={0} | all-to-all | bytes 12582912 | tf_op jit(solution)/shard_map/all_to_all | solution.py:130
  687.7 10.3 %reshape.171 = bf16[768,4096]{1,0:T(8,128)(2,1)} reshape(bf16[128,6,4096]{2,1,0:T(8,128)(2,1)} %all_to_all.10) | data formatting | bytes 12582912 | tf_op jit(solution)/shard_map/reshape | solution.py:131
  698.0 13.9 %fusion.20 = f32[768,1536]{1,0:T(8,128)S(1)} fusion(bf16[768,4096]{1,0:T(8,128)(2,1)} %reshape.171, bf16[1,4096,1536]{2,1,0:T(8,128)(2,1)} %param.22), kind=kOutput, calls=%fused_computation.28 | convolution fusion | flops 9663676416 | bytes 23592960 | tf_op jit(solution)/shard_map/dot_general | solution.py:132
  711.9 9.9 %convolution_convert_fusion.1 = bf16[768,4096]{1,0:T(8,128)(2,1)} fusion(bf16[1,768,4096]{2,1,0:T(8,128)(2,1)} %param.23, f32[768,1536]{1,0:T(8,128)S(1)} %fusion.20), kind=kOutput, calls=%fused_computation.32 | convolution fusion | flops 4838522880 | bytes 17301504 | tf_op jit(solution)/shard_map/dot_general | solution.py:134
  721.8 10.1 %reshape.172 = bf16[128,6,4096]{2,1,0:T(8,128)(2,1)} reshape(bf16[768,4096]{1,0:T(8,128)(2,1)} %convolution_convert_fusion.1) | data formatting | bytes 12582912 | tf_op jit(solution)/shard_map/reshape | solution.py:135
  731.9 8.1 all-to-all-start.1
  740.0 0.1 copy.17
  740.1 99.5 %all-to-all-done.1 = bf16[128,6,4096]{2,1,0:T(8,128)(2,1)} async-done(((bf16[128,6,4096]{2,1,0:T(8,128)(2,1)}), bf16[128,6,4096]{2,1,0:T(8,128)(2,1)}, u32[]{:S(2)}, u32[]{:S(2)}) %all-to-all-start.1) | async-done | bytes 6291488 | tf_op jit(solution)/shard_map/all_to_all | solution.py:136
  839.6 10.2 %reshape.173 = bf16[768,4096]{1,0:T(8,128)(2,1)} reshape(bf16[128,6,4096]{2,1,0:T(8,128)(2,1)} %all-to-all-done.1) | data formatting | bytes 12582912 | tf_op jit(solution)/shard_map/reshape | solution.py:137
  849.8 12.2 %gather_fusion = bf16[512,4096]{1,0:T(8,128)(2,1)} fusion(bf16[768,4096]{1,0:T(8,128)(2,1)} %reshape.173, s32[1024]{0:T(1024)S(1)} %pad_clamp_fusion), kind=kCustom, calls=%fused_computation.1 | custom fusion | bytes 8390656 | tf_op jit(solution)/shard_map/gather | solution.py:137
  862.0 8.5 reshape.174
  870.5 11.2 %multiply_reduce_fusion = f32[128,4096]{1,0:T(8,128)} fusion(f32[128,4,4096]{2,1,0:T(4,128)} %reshape.174, f32[128,4]{1,0:T(8,128)S(1)} %copy.17), kind=kLoop, calls=%fused_computation.30 | loop fusion | flops 3670016 | bytes 10487808 | tf_op jit(solution)/shard_map/reduce_sum | solution.py:138
  881.8 2.9 fusion.30
  (151 shorter events, 1.7 us)
Async XLA Ops:
  6.5 1.0 copy-start
  6.5 57.0 %all-gather.4.cloned.1.call-start = ((), (), s32[]{:S(2)}) async-start(), calls=%async_computation.3 | async-start | bytes 4456448 | tf_op jit(solution)/shard_map/all_gather | solution.py:51
  8.3 108.6 %all-gather.6.cloned.1.call-start = ((), (), s32[]{:S(2)}) async-start(), calls=%async_computation.4 | async-start | bytes 4456448 | tf_op jit(solution)/shard_map/all_gather | solution.py:52
  10.1 166.3 %all-gather.8.cloned.1.call-start = ((), (), s32[]{:S(2)}) async-start(), calls=%async_computation.5 | async-start | bytes 4456448 | tf_op jit(solution)/shard_map/all_gather | solution.py:102
  10.8 533.8 %reduce-scatter.2.cloned.1.call-start = ((), (), s32[]{:S(2)}) async-start(), calls=%async_computation.6 | async-start | bytes 9437184 | tf_op jit(solution)/shard_map/reduce_scatter | solution.py:103
  122.1 2.2 copy-start.4
  128.4 1.4 copy-start.5
  133.5 2.2 copy-start.4
  139.8 1.4 copy-start.5
  186.7 0.7 copy-start.7
  186.7 358.0 %copy-start.2 = (bf16[128,4096]{1,0:T(8,128)(2,1)S(1)}, bf16[128,4096]{1,0:T(8,128)(2,1)}, u32[]{:S(2)}) copy-start(bf16[128,4096]{1,0:T(8,128)(2,1)} %param.18) | copy-start | bytes 3145732
  187.4 358.9 %copy-start.6 = (f32[4096]{0:T(1024)S(1)}, f32[4096]{0:T(1024)}, u32[]{:S(2)}) copy-start(f32[4096]{0:T(1024)} %param.19) | copy-start | bytes 49156
  731.9 8.1 copy-start.8
  731.9 107.7 %all-to-all-start.1 = ((bf16[128,6,4096]{2,1,0:T(8,128)(2,1)}), bf16[128,6,4096]{2,1,0:T(8,128)(2,1)}, u32[]{:S(2)}, u32[]{:S(2)}) async-start(bf16[128,6,4096]{2,1,0:T(8,128)(2,1)} %reshape.172), calls=%async_computation.2 | async-start | bytes 16777216 | tf_op jit(solution)/shard_map/all_to_all | solution.py:136
  870.5 11.3 %copy-start.3 = (bf16[128,4096]{1,0:T(8,128)(2,1)S(1)}, bf16[128,4096]{1,0:T(8,128)(2,1)}, u32[]{:S(2)}) copy-start(bf16[128,4096]{1,0:T(8,128)(2,1)} %reduce-scatter.2.cloned.1.call-done) | copy-start | bytes 3145732
  870.5 14.2 %copy-start.1 = (bf16[1024,256]{1,0:T(8,128)(2,1)S(1)}, bf16[1024,256]{1,0:T(8,128)(2,1)}, u32[]{:S(2)}) copy-start(bf16[1024,256]{1,0:T(8,128)(2,1)} %param.15) | copy-start | bytes 1572868
Sparse Core Ops, SparseCore 0:
  9.5 53.9 all-gather.3
  65.6 51.2 all-gather.5
  119.0 57.2 all-gather.7
  186.8 357.7 reduce-scatter.1
where the time goes:
time: 906 us; the launch traced here: 891 us
  waiting for transfers between devices  568 us (63%)
  blocking collectives  107 us (12%)
  local copies, waits for them, and re-layouts  97.6 us (11%)
  matrix products  47.3 us (5%)
  other arithmetic  25.1 us (3%)
  loops' own time  24.3 us (3%)
  between operations  13.6 us (2%)
    reduce_scatter x1, waiting for transfers between devices, body(): lax.psum_scatter(jnp.dot(attended, full_proj, preferred_element_type=jnp....  356 us
    all_to_all x1, blocking collectives, body(): lax.all_to_all(packed, ('ctx', 'tp'), split_axis=0, concat_axis=0, tiled=...  107 us
    all_to_all x1, waiting for transfers between devices, body(): lax.all_to_all(processed, ('ctx', 'tp'), split_axis=0, concat_axis=0, til...  99.5 us
    all_gather x1, waiting for transfers between devices, body(): piece_values = lax.all_gather(own_values, 'ctx', axis=0, tiled=True)  53.4 us
    all_gather x1, waiting for transfers between devices, body(): piece_keys = lax.all_gather(own_keys, 'ctx', axis=0, tiled=True)  49.8 us
    another operation x1, loops' own time, body(): finals = lax.fori_loop(0, block_count, one_block, initial)  23.7 us
    scatter x1, local copies, waits for them, and re-layouts, body(): jnp.zeros((dev_count * capacity, normed.shape[1]), jnp.bfloat16).at[target]  22.6 us
  transfers between devices with their start and end apart: 5, of which 5 were waited for; matrix products, arithmetic and copies ran while one was open for 3% of the time, Pallas kernels for 0%

commit v1 on v0

v1 whole, which is shorter than its diff:
```python
import functools
import math

import jax
import jax.numpy as jnp
import numpy as np
from jax import lax
from jax.experimental import pallas as pl
from jax.experimental.pallas import tpu as pltpu
from jax.sharding import PartitionSpec as P

HEADS = 32
KV_HEADS = 2
HEAD_DIM = 128
FF = 768
TOPK = 4
CAP = 6
BASE2_SCALE = math.log2(math.e) / math.sqrt(HEAD_DIM)
EXPONENT_LIMIT = 100.0
KEY_WIDTH = 1024
SUB_ROWS = 256
PIECE = 512
PIECES = 8
GROUP = 8
GROUP_ROWS = GROUP * CAP
VMEM_BYTES = 56 * 2**20

VMEM_SPEC = pl.BlockSpec(memory_space=pltpu.VMEM)
SMEM_SPEC = pl.BlockSpec(memory_space=pltpu.SMEM)


def piece_swap():
    swap = np.zeros((GROUP, PIECES, CAP, PIECES, GROUP, CAP), np.float32)
    for device in range(GROUP):
        for piece in range(PIECES):
            for slot in range(CAP):
                swap[device, piece, slot, piece, device, slot] = 1
    size = GROUP * PIECES * CAP
    return jnp.asarray(swap.reshape(size, size), jnp.bfloat16)


def dot_f32(left, right):
    return jnp.dot(left, right, preferred_element_type=jnp.float32)


def dot_keys(left, keys):
    return lax.dot_general(
        left, keys, (((1,), (1,)), ((), ())), preferred_element_type=jnp.float32
    )


def attend_kernel(block_ref, q_ref, kv_ref, out_ref, q_wide, top, acc):
    rows, width, sub = q_ref.shape[0], KEY_WIDTH, SUB_ROWS
    heads = q_ref.shape[1] // HEAD_DIM
    tiles = heads * rows // sub
    block = block_ref[0]
    last = (block * rows) // width
    shift = block * rows - last * width
    bound = jnp.full((1, 1), jnp.inf, jnp.float32)
    ones = jnp.ones((width, HEAD_DIM), jnp.bfloat16)

    def load(index):
        at = pl.ds(pl.multiple_of(index * width, width), width)
        keys, values = kv_ref[at, :HEAD_DIM], kv_ref[at, HEAD_DIM:]
        return jnp.concatenate([keys, keys], 1), jnp.concatenate([values, ones], 1)

    norms = []
    for head in range(heads):
        scaled = q_ref[:, head * HEAD_DIM : (head + 1) * HEAD_DIM].astype(jnp.float32) * BASE2_SCALE
        high = scaled.astype(jnp.bfloat16)
        q_wide[head * rows : (head + 1) * rows, :HEAD_DIM] = high
        q_wide[head * rows : (head + 1) * rows, HEAD_DIM:] = (
            scaled - high.astype(jnp.float32)
        ).astype(jnp.bfloat16)
        norms.append(jnp.sqrt(jnp.sum(scaled * scaled, axis=1, keepdims=True)))

    keys, values = load(last)
    for tile in range(tiles):
        at = slice(tile * sub, (tile + 1) * sub)
        first = (tile * sub) % rows
        scores = dot_keys(q_wide[at, :], keys)
        row = lax.broadcasted_iota(jnp.int32, (sub, width), 0) + (first + shift)
        col = lax.broadcasted_iota(jnp.int32, (sub, width), 1)
        scores = jnp.where(col <= row, scores, -1e30)
        best = jnp.max(scores, axis=1, keepdims=True)
        weights = jnp.exp2(scores - best).astype(jnp.bfloat16)
        acc[at, :] = dot_f32(weights, values)
        top[at, :] = jnp.broadcast_to(best, (sub, HEAD_DIM))
        norm = norms[(tile * sub) // rows][first : first + sub]
        bound = jnp.minimum(
            bound, jnp.min((EXPONENT_LIMIT + best) / norm, axis=0, keepdims=True)
        )

    def longest(index, so_far):
        keys = kv_ref[pl.ds(pl.multiple_of(index * width, width), width), :HEAD_DIM]
        keys = keys.astype(jnp.float32)
        length = jnp.sum(keys * keys, axis=1, keepdims=True)
        return jnp.maximum(so_far, jnp.max(length, axis=0, keepdims=True))

    key_norm = jnp.sqrt(lax.fori_loop(0, last, longest, jnp.zeros((1, 1), jnp.float32)))
    safe = jnp.max(key_norm - bound) <= 0.0

    @pl.when(safe)
    def _():
        def step(index, carry):
            keys, values = load(index)
            for tile in range(tiles):
                at = slice(tile * sub, (tile + 1) * sub)
                scores = dot_keys(q_wide[at, :], keys)
                best = top[at, :]
                weights = jnp.concatenate(
                    [
                        jnp.exp2(scores[:, c : c + HEAD_DIM] - best).astype(jnp.bfloat16)
                        for c in range(0, width, HEAD_DIM)
                    ],
                    1,
                )
                acc[at, :] += dot_f32(weights, values)
            return carry

        lax.fori_loop(0, last, step, 0)

    @pl.when(jnp.logical_not(safe))
    def _():
        def step(index, carry):
            keys, values = load(index)

            def one_tile(tile, kept):
                at = pl.ds(pl.multiple_of(tile * sub, sub), sub)
                scores = dot_keys(q_wide[at, :], keys)
                old = top[at, :]
                best = jnp.maximum(old, jnp.max(scores, axis=1, keepdims=True))
                factor = jnp.exp2(old - best)
                weights = jnp.exp2(scores - best[:, :1]).astype(jnp.bfloat16)
                acc[at, :] = acc[at, :] * factor[:, :1] + dot_f32(weights, values)
                top[at, :] = best
                return kept

            return lax.fori_loop(0, tiles, one_tile, carry)

        lax.fori_loop(0, last, step, 0)

    for head in range(heads):
        at = slice(head * rows, (head + 1) * rows)
        out_ref[:, head * HEAD_DIM : (head + 1) * HEAD_DIM] = (
            acc[at, :HEAD_DIM] / acc[at, HEAD_DIM:]
        ).astype(jnp.bfloat16)


def attend(block, queries, keys_values):
    rows, columns = queries.shape
    all_rows = rows * columns // HEAD_DIM
    return pl.pallas_call(
        attend_kernel,
        out_shape=jax.ShapeDtypeStruct(queries.shape, jnp.bfloat16),
        in_specs=[SMEM_SPEC, VMEM_SPEC, VMEM_SPEC],
        out_specs=VMEM_SPEC,
        scratch_shapes=[
            pltpu.VMEM((all_rows, 2 * HEAD_DIM), jnp.bfloat16),
            pltpu.VMEM((all_rows, HEAD_DIM), jnp.float32),
            pltpu.VMEM((all_rows, 2 * HEAD_DIM), jnp.float32),
        ],
        compiler_params=pltpu.CompilerParams(vmem_limit_bytes=VMEM_BYTES),
        name="attend",
    )(block, queries, keys_values)


def dispatch_kernel(target_ref, attn_ref, residual_ref, gain_ref, swap_ref, hidden_ref, out_ref, rows_of):
    step = pl.program_id(0)

    @pl.when(step == 0)
    def _():
        hidden = (
            residual_ref[...].astype(jnp.float32) + attn_ref[...].astype(jnp.float32)
        ).astype(jnp.bfloat16)
        hidden_ref[...] = hidden
        wide = hidden.astype(jnp.float32)
        variance = jnp.mean(wide * wide, axis=-1, keepdims=True)
        normed = (wide * lax.rsqrt(variance + 1e-06) * gain_ref[...]).astype(jnp.bfloat16)
        slots, tokens = rows_of.shape[1], normed.shape[0]
        slot = lax.broadcasted_iota(jnp.int32, (slots, tokens), 0)
        chosen = jnp.zeros((slots, tokens), jnp.float32)
        for route in range(TOPK):
            chosen += jnp.where(slot == target_ref[route : route + 1, :], 1.0, 0.0)
        chosen = chosen.astype(jnp.bfloat16)
        for piece in range(PIECES):
            rows_of[piece] = dot_f32(
                chosen, normed[:, piece * PIECE : (piece + 1) * PIECE]
            ).astype(jnp.bfloat16)

    at = pl.ds(pl.multiple_of(step * GROUP_ROWS, GROUP_ROWS), GROUP_ROWS)
    stacked = jnp.concatenate([rows_of[piece, at, :] for piece in range(PIECES)], 0)
    out_ref[...] = dot_f32(swap_ref[...], stacked).astype(jnp.bfloat16)


def dispatch(target, attn_out, residual, gain, swap, dev_count):
    tokens, model = residual.shape
    slots = dev_count * CAP
    group_block = GROUP_ROWS * PIECES

    def whole(shape):
        return pl.BlockSpec(shape, lambda step: (0, 0))

    return pl.pallas_call(
        dispatch_kernel,
        grid=(dev_count // GROUP,),
        out_shape=(
            jax.ShapeDtypeStruct((tokens, model), jnp.bfloat16),
            jax.ShapeDtypeStruct((slots * PIECES, PIECE), jnp.bfloat16),
        ),
        in_specs=[
            whole((TOPK, tokens)),
            whole((tokens, model)),
            whole((tokens, model)),
            whole((1, model)),
            whole((group_block, group_block)),
        ],
        out_specs=(
            whole((tokens, model)),
            pl.BlockSpec((group_block, PIECE), lambda step: (step, 0)),
        ),
        scratch_shapes=[pltpu.VMEM((PIECES, slots, PIECE), jnp.bfloat16)],
        compiler_params=pltpu.CompilerParams(vmem_limit_bytes=VMEM_BYTES),
        name="norm_and_dispatch",
    )(target, attn_out, residual, gain, swap)


def expert_kernel(arrived_ref, swap_ref, in_ref, down_ref, out_ref, rows_of, gate_up, active):
    step = pl.program_id(0)
    groups = rows_of.shape[1] // GROUP_ROWS
    group_block = GROUP_ROWS * PIECES

    @pl.when(step == 0)
    def _():
        def unpack(group, carry):
            at = pl.ds(pl.multiple_of(group * group_block, group_block), group_block)
            stacked = dot_f32(swap_ref[...], arrived_ref[at, :]).astype(jnp.bfloat16)
            to = pl.ds(pl.multiple_of(group * GROUP_ROWS, GROUP_ROWS), GROUP_ROWS)
            for piece in range(PIECES):
                rows_of[piece, to, :] = stacked[piece * GROUP_ROWS : (piece + 1) * GROUP_ROWS]
            return carry

        lax.fori_loop(0, groups, unpack, 0, unroll=2)
        gate_up[...] = jnp.zeros_like(gate_up)

    @pl.when(step < PIECES)
    def _():
        gate_up[...] += dot_f32(rows_of[step], in_ref[...])

    @pl.when(step == PIECES - 1)
    def _():
        active[...] = (jax.nn.silu(gate_up[:, :FF]) * gate_up[:, FF:]).astype(jnp.bfloat16)

    @pl.when(step >= PIECES)
    def _():
        rows_of[step - PIECES] = dot_f32(active[...], down_ref[...]).astype(jnp.bfloat16)

    @pl.when(step == 2 * PIECES - 1)
    def _():
        def pack(group, carry):
            at = pl.ds(pl.multiple_of(group * GROUP_ROWS, GROUP_ROWS), GROUP_ROWS)
            stacked = jnp.concatenate([rows_of[piece, at, :] for piece in range(PIECES)], 0)
            to = pl.ds(pl.multiple_of(group * group_block, group_block), group_block)
            out_ref[to, :] = dot_f32(swap_ref[...], stacked).astype(jnp.bfloat16)
            return carry

        lax.fori_loop(0, groups, pack, 0, unroll=2)


def run_expert(arrived, swap, w_in, w_out):
    slots = arrived.shape[0] // PIECES
    group_block = GROUP_ROWS * PIECES
    return pl.pallas_call(
        expert_kernel,
        grid=(2 * PIECES,),
        out_shape=jax.ShapeDtypeStruct(arrived.shape, jnp.bfloat16),
        in_specs=[
            pl.BlockSpec(arrived.shape, lambda step: (0, 0)),
            pl.BlockSpec((group_block, group_block), lambda step: (0, 0)),
            pl.BlockSpec((PIECE, 2 * FF), lambda step: (jnp.minimum(step, PIECES - 1), 0)),
            pl.BlockSpec((FF, PIECE), lambda step: (0, jnp.maximum(step - PIECES, 0))),
        ],
        out_specs=pl.BlockSpec(arrived.shape, lambda step: (0, 0)),
        scratch_shapes=[
            pltpu.VMEM((PIECES, slots, PIECE), jnp.bfloat16),
            pltpu.VMEM((slots, 2 * FF), jnp.float32),
            pltpu.VMEM((slots, FF), jnp.bfloat16),
        ],
        compiler_params=pltpu.CompilerParams(vmem_limit_bytes=VMEM_BYTES),
        name="expert",
    )(arrived, swap, w_in, w_out)


def combine_kernel(target_ref, route_ref, hidden_ref, swap_ref, back_ref, out_ref, rows_of):
    step = pl.program_id(0)
    stacked = dot_f32(swap_ref[...], back_ref[...]).astype(jnp.bfloat16)
    to = pl.ds(pl.multiple_of(step * GROUP_ROWS, GROUP_ROWS), GROUP_ROWS)
    for piece in range(PIECES):
        rows_of[piece, to, :] = stacked[piece * GROUP_ROWS : (piece + 1) * GROUP_ROWS]

    @pl.when(step == pl.num_programs(0) - 1)
    def _():
        slots, tokens = rows_of.shape[1], hidden_ref.shape[0]
        route = route_ref[...]
        mixing = route / jnp.sum(route, axis=-1, keepdims=True)
        slot = lax.broadcasted_iota(jnp.int32, (tokens, slots), 1)
        spread = jnp.zeros((tokens, slots), jnp.float32)
        for number in range(TOPK):
            spread += jnp.where(
                slot == target_ref[:, number : number + 1], mixing[:, number : number + 1], 0.0
            )
        high = spread.astype(jnp.bfloat16)
        low = (spread - high.astype(jnp.float32)).astype(jnp.bfloat16)
        both = jnp.concatenate([high, low], 0)
        for piece in range(PIECES):
            columns = slice(piece * PIECE, (piece + 1) * PIECE)
            mixed = dot_f32(both, rows_of[piece])
            out_ref[:, columns] = (
                hidden_ref[:, columns].astype(jnp.float32) + mixed[:tokens] + mixed[tokens:]
            ).astype(jnp.bfloat16)


def combine(target, route_weights, hidden, swap, back):
    tokens, model = hidden.shape
    slots = back.shape[0] // PIECES
    group_block = GROUP_ROWS * PIECES

    def whole(shape):
        return pl.BlockSpec(shape, lambda step: (0, 0))

    return pl.pallas_call(
        combine_kernel,
        grid=(slots // GROUP_ROWS,),
        out_shape=jax.ShapeDtypeStruct((tokens, model), jnp.bfloat16),
        in_specs=[
            whole((tokens, TOPK)),
            whole((tokens, TOPK)),
            whole((tokens, model)),
            whole((group_block, group_block)),
            pl.BlockSpec((group_block, PIECE), lambda step: (step, 0)),
        ],
        out_specs=whole((tokens, model)),
        scratch_shapes=[pltpu.VMEM((PIECES, slots, PIECE), jnp.bfloat16)],
        compiler_params=pltpu.CompilerParams(vmem_limit_bytes=VMEM_BYTES),
        name="combine",
    )(target, route_weights, hidden, swap, back)


def body(
    queries, keys, values, out_proj, residual, norm_gain, expert_ids, route_weights, w_in, w_out
):
    ctx_count = lax.axis_size("ctx")
    dev_count = ctx_count * lax.axis_size("tp")
    ctx_index = lax.axis_index("ctx")
    heads_here = queries.shape[1] // HEAD_DIM
    kv_index = lax.axis_index("tp") * heads_here // (HEADS // KV_HEADS)
    half = queries.shape[0] // 2

    flat_ids = expert_ids.reshape(-1)
    one_hot = (flat_ids[:, None] == jnp.arange(dev_count, dtype=jnp.int32)[None, :]).astype(
        jnp.int32
    )
    earlier = jnp.cumsum(one_hot, axis=0) - one_hot
    target = (flat_ids * CAP + jnp.sum(earlier * one_hot, axis=1)).reshape(expert_ids.shape)
    swap = piece_swap()

    opposite = [(i, ctx_count - 1 - i) for i in range(ctx_count)]
    swapped = lax.ppermute(queries[half:], "ctx", opposite)
    own_kv = jnp.concatenate(
        [
            lax.dynamic_slice_in_dim(keys, kv_index * HEAD_DIM, HEAD_DIM, 1),
            lax.dynamic_slice_in_dim(values, kv_index * HEAD_DIM, HEAD_DIM, 1),
        ],
        1,
    )
    all_kv = lax.all_gather(own_kv, "ctx", axis=0, tiled=True)
    full_proj = lax.all_gather(out_proj, "ctx", axis=1, tiled=True)
    far_block = (2 * ctx_count - 1 - 2 * ctx_index).astype(jnp.int32).reshape(1)
    near_block = (2 * ctx_index).astype(jnp.int32).reshape(1)
    far = attend(far_block, swapped, all_kv)
    returned = lax.ppermute(far, "ctx", opposite)
    near = attend(near_block, queries[:half], all_kv)
    attended = jnp.concatenate([near, returned], 0)
    attn_out = lax.psum_scatter(
        dot_f32(attended, full_proj).astype(jnp.bfloat16), "tp", scatter_dimension=0, tiled=True
    )

    hidden, packed = dispatch(
        target.T, attn_out, residual, norm_gain.reshape(1, -1), swap, dev_count
    )

    def exchange(rows):
        shaped = rows.reshape(dev_count, CAP * PIECES, PIECE)
        return lax.all_to_all(
            shaped, ("ctx", "tp"), split_axis=0, concat_axis=0, tiled=True
        ).reshape(rows.shape)

    processed = run_expert(exchange(packed), swap, w_in[0], w_out[0])
    return combine(target, route_weights, hidden, swap, exchange(processed))


def solution(mesh):
    return jax.shard_map(
        body,
        mesh=mesh,
        in_specs=(
            P("ctx", "tp"),
            P("ctx", None),
            P("ctx", None),
            P("tp", "ctx"),
            P(("ctx", "tp"), None),
            P(),
            P(("ctx", "tp"), None),
            P(("ctx", "tp"), None),
            P(("ctx", "tp"), None, None),
            P(("ctx", "tp"), None, None),
        ),
        out_specs=P(("ctx", "tp"), None),
        check_vma=False,
    )
```

time: 906 us -> 660 us (0.73); the launches traced: 891 us -> 656 us
  waiting for transfers between devices: 568 us -> 320 us
  Pallas kernels: 0 us -> 208 us
  local copies, waits for them, and re-layouts: 97.6 us -> 5.87 us
  matrix products: 47.3 us -> 10.1 us
  loops' own time: 24.3 us -> 0 us
  other arithmetic: 25.1 us -> 1.39 us
  blocking collectives: 107 us -> 83.5 us
    pallas_call x0 -> x5, Pallas kernels: none -> 208 us  [the longest x2 144 us: attend(): pl.pallas_call(attend_kernel, out_shape=jax.ShapeDtypeStruct(queries.shap...]
    reduce_scatter x1, waiting for transfers between devices: 356 us -> 168 us  [body(): lax.psum_scatter(dot_f32(attended, full_proj).astype(jnp.bfloat16), 'tp',...]
    all_gather x2 -> x1, waiting for transfers between devices: 103 us -> 50.4 us  [body(): all_kv = lax.all_gather(own_kv, 'ctx', axis=0, tiled=True)]
    reshape x4 -> x0, local copies, waits for them, and re-layouts: 40.7 us -> none  [the longest x1 10.3 us: body(): flat_rows = arrived.reshape(-1, arrived.shape[-1])]
    dot_general x7 -> x1, matrix products: 47.3 us -> 10.1 us  [dot_f32(): return jnp.dot(left, right, preferred_element_type=jnp.float32)]
    ppermute x0 -> x2, waiting for transfers between devices: none -> 26.5 us  [the longest x1 17.6 us: body(): swapped = lax.ppermute(queries[half:], 'ctx', opposite)]
    all_to_all x1, waiting for transfers between devices: 99.5 us -> 75 us  [exchange(): lax.all_to_all(shaped, ('ctx', 'tp'), split_axis=0, concat_axis=0, tiled=...]
    another operation x33 -> x0, loops' own time: 24.3 us -> none  [the longest x1 23.7 us: body(): finals = lax.fori_loop(0, block_count, one_block, initial)]
  transfers between devices with their start and end apart: 5 -> 6, of which waited for: 5 -> 5; matrix products, arithmetic and copies ran while one was open for 3% -> 1% of each run, Pallas kernels for 0% -> 22%
where the time goes in v1:
time: 660 us; the launch traced here: 656 us
  waiting for transfers between devices  320 us (48%)
  Pallas kernels  208 us (32%)
  blocking collectives  83.5 us (13%)
  starting transfers between devices  13.9 us (2%)
  between operations  13.2 us (2%)
  matrix products  10.1 us (2%)
    reduce_scatter x1, waiting for transfers between devices, body(): lax.psum_scatter(dot_f32(attended, full_proj).astype(jnp.bfloat16), 'tp',...  168 us
    pallas_call x2, Pallas kernels, attend(): pl.pallas_call(attend_kernel, out_shape=jax.ShapeDtypeStruct(queries.shap...  144 us
    all_to_all x1, blocking collectives, exchange(): lax.all_to_all(shaped, ('ctx', 'tp'), split_axis=0, concat_axis=0, tiled=...  83.5 us
    all_to_all x1, waiting for transfers between devices, exchange(): lax.all_to_all(shaped, ('ctx', 'tp'), split_axis=0, concat_axis=0, tiled=...  75 us
    all_gather x1, waiting for transfers between devices, body(): all_kv = lax.all_gather(own_kv, 'ctx', axis=0, tiled=True)  50.4 us
    pallas_call x1, Pallas kernels, run_expert(): pl.pallas_call(expert_kernel, grid=(2 * PIECES,), out_shape=jax.ShapeDtyp...  35.3 us
    ppermute x1, waiting for transfers between devices, body(): swapped = lax.ppermute(queries[half:], 'ctx', opposite)  17.6 us
    pallas_call x1, Pallas kernels, combine(): pl.pallas_call(combine_kernel, grid=(slots // GROUP_ROWS,), out_shape=jax...  15.2 us
  transfers between devices with their start and end apart: 6, of which 5 were waited for; matrix products, arithmetic and copies ran while one was open for 1% of the time, Pallas kernels for 22%

profile of v1, /device:TPU:6, one launch (start us, length us, event | category | flops | bytes accessed | tf_op | source)
XLA Modules:
  0.0 655.8 jit_solution(15463596616560619870)
XLA Ops:
  6.5 0.0 all-gather.3.cloned.1.call-start
  6.5 1.1 constant_dynamic-slice_fusion
  7.6 0.9 pad_maximum_fusion
  8.5 0.0 all-gather.3.cloned.1.call-update
  8.5 0.0 all-gather.5.cloned.1.call-start
  8.6 0.7 all-gather.5.cloned.1.call-update
  9.3 0.0 reduce-scatter.2.cloned.1.call-start
  9.3 2.1 fusion.9
  11.4 6.5 collective-permute-start
  17.9 17.6 %collective-permute-done.q_ref = bf16[512,512]{1,0:T(8,128)(2,1)S(1)} collective-permute-done((bf16[512,512]{1,0:T(8,128)(2,1)S(1)}, bf16[512,512]{1,0:T(8,128)(2,1)S(1)}, u32[]{:S(2)}, u32[]{:S(2)}) %collective-permute-start) | collective-permute-done | bytes 524320 | tf_op jit(solution)/shard_map/ppermute | solution.py:368
  35.5 0.0 copy-start.1
  35.5 50.4 %all-gather.3.cloned.1.call-done.kv_ref = bf16[16384,256]{1,0:T(8,128)(2,1)} async-done(((bf16[1024,256]{1,0:T(8,128)(2,1)}), bf16[16384,256]{1,0:T(8,128)(2,1)}) %all-gather.3.cloned.1.call-update) | async-done | bytes 8388624 | tf_op jit(solution)/shard_map/all_gather | solution.py:376
  85.9 0.0 copy-done.1
  85.9 135.5 %attend.3 = bf16[512,512]{1,0:T(8,128)(2,1)} custom-call(s32[1]{0:T(128)} %bitcast.5.block_ref, bf16[512,512]{1,0:T(8,128)(2,1)} %copy-done.1, bf16[16384,256]{1,0:T(8,128)(2,1)} %all-gather.3.cloned.1.call-done.kv_ref), custom_call_target="tpu_custom_call" | custom-call | tf_op jit(solution)/shard_map/attend/pallas_call | solution.py:153
  221.4 0.0 collective-permute-start.1
  221.4 8.3 %attend.2 = bf16[512,512]{1,0:T(8,128)(2,1)} custom-call(s32[1]{0:T(128)} %bitcast.4.block_ref, bf16[512,512]{1,0:T(8,128)(2,1)} %get-tuple-element.9.q_ref, bf16[16384,256]{1,0:T(8,128)(2,1)} %all-gather.3.cloned.1.call-done.kv_ref), custom_call_target="tpu_custom_call" | custom-call | tf_op jit(solution)/shard_map/attend/pallas_call | solution.py:153
  229.7 0.0 all-gather.5.cloned.1.call-done
  229.7 8.9 %collective-permute-done.1 = bf16[512,512]{1,0:T(8,128)(2,1)S(1)} collective-permute-done((bf16[512,512]{1,0:T(8,128)(2,1)}, bf16[512,512]{1,0:T(8,128)(2,1)S(1)}, u32[]{:S(2)}, u32[]{:S(2)}) %collective-permute-start.1) | collective-permute-done | bytes 524320 | tf_op jit(solution)/shard_map/ppermute | solution.py:381
  238.6 10.1 %convolution_convert_fusion = bf16[1024,4096]{1,0:T(8,128)(2,1)} fusion(bf16[512,4096]{1,0:T(8,128)(2,1)} %all-gather.5.cloned.1.call-done, bf16[512,512]{1,0:T(8,128)(2,1)S(1)} %collective-permute-done.1, bf16[512,512]{1,0:T(8,128)(2,1)} %attend.2), kind=kOutput, calls=%fused_computation | convolution fusion | flops 4301258752 | bytes 13631488 | tf_op jit(solution)/shard_map/dot_general | solution.py:43
  248.7 0.0 copy-start.2
  248.7 0.0 reduce-scatter.2.cloned.1.call-update
  248.7 0.7 copy-done.2
  249.4 0.1 copy.24
  249.5 0.1 eq.29
  249.6 0.1 eq.25
  249.7 0.1 copy.26
  249.8 0.2 fusion.5
  250.1 0.2 fusion.4
  250.4 0.1 reduce_sum.12
  250.5 0.1 copy.28
  250.6 0.0 copy-start
  250.6 0.7 copy.29.target_ref
  251.3 167.6 %reduce-scatter.2.cloned.1.call-done.attn_ref = bf16[128,4096]{1,0:T(8,128)(2,1)} async-done(((bf16[1024,4096]{1,0:T(8,128)(2,1)}), bf16[128,4096]{1,0:T(8,128)(2,1)}) %reduce-scatter.2.cloned.1.call-update) | async-done | bytes 1048592 | tf_op jit(solution)/shard_map/reduce_scatter | solution.py:384
  418.9 13.3 %norm_and_dispatch.1 = (bf16[128,4096]{1,0:T(8,128)(2,1)}, bf16[6144,512]{1,0:T(8,128)(2,1)}) custom-call(s32[4,128]{1,0:T(4,128)} %copy.29.target_ref, bf16[128,4096]{1,0:T(8,128)(2,1)} %reduce-scatter.2.cloned.1.call-done.attn_ref, bf16[128,4096]{1,0:T(8,128)(2,1)} %residual_ref.1, f32[1,4096]{1,0:T(1,128)} %bitcast.32, ...), custom_call_target="tpu_custom_call" | custom-call | tf_op jit(solution)/shard_map/norm_and_dispatch/pallas_call | solution.py:204
  432.2 83.5 %all_to_all.10 = bf16[128,48,512]{2,1,0:T(8,128)(2,1)} all-to-all(bf16[128,48,512]{2,1,0:T(8,128)(2,1)} %bitcast.27), channel_id=1, replica_groups=mesh['ctx'=16,'tp'=8] {'ctx','tp'}, dimensions={0} | all-to-all | bytes 12582912 | tf_op jit(solution)/shard_map/all_to_all | solution.py:394
  515.7 0.0 copy-done
  515.7 35.3 %expert.1 = bf16[6144,512]{1,0:T(8,128)(2,1)} custom-call(bf16[6144,512]{1,0:T(8,128)(2,1)} %bitcast.25, bf16[384,384]{1,0:T(8,128)(2,1)} %constant.43.clone.swap_ref, bf16[4096,1536]{1,0:T(8,128)(2,1)} %bitcast.26, bf16[768,4096]{1,0:T(8,128)(2,1)} %bitcast.28), custom_call_target="tpu_custom_call" | custom-call | tf_op jit(solution)/shard_map/expert/pallas_call | solution.py:273
  551.1 0.0 copy-start.3
  551.1 7.3 %all-to-all-start.1 = ((bf16[128,48,512]{2,1,0:T(8,128)(2,1)}), bf16[128,48,512]{2,1,0:T(8,128)(2,1)}, u32[]{:S(2)}, u32[]{:S(2)}) async-start(bf16[128,48,512]{2,1,0:T(8,128)(2,1)} %bitcast.24), calls=%async_computation.2 | async-start | bytes 12582912 | tf_op jit(solution)/shard_map/all_to_all | solution.py:394
  558.4 0.0 copy-done.3
  558.4 0.7 copy.30.route_ref
  559.1 75.0 %all-to-all-done.1 = bf16[128,48,512]{2,1,0:T(8,128)(2,1)} async-done(((bf16[128,48,512]{2,1,0:T(8,128)(2,1)}), bf16[128,48,512]{2,1,0:T(8,128)(2,1)}, u32[]{:S(2)}, u32[]{:S(2)}) %all-to-all-start.1) | async-done | bytes 6291488 | tf_op jit(solution)/shard_map/all_to_all | solution.py:394
  634.1 15.2 %combine.1 = bf16[128,4096]{1,0:T(8,128)(2,1)} custom-call(s32[128,4]{1,0:T(8,128)} %copy-done, f32[128,4]{1,0:T(8,128)} %copy.30.route_ref, bf16[128,4096]{1,0:T(8,128)(2,1)} %get-tuple-element.7.hidden_ref, bf16[384,384]{1,0:T(8,128)(2,1)} %constant.43.clone.swap_ref, bf16[6144,512]{1,0:T(8,128)(2,1)} %bitcast.12.back_ref), custom_call_target="tpu_custom_call" | custom-call | tf_op jit(solution)/shard_map/combine/pallas_call | solution.py:331
  (8 shorter events, 0.1 us)
Async XLA Ops:
  6.5 79.4 %all-gather.3.cloned.1.call-start = ((), (), s32[]{:S(2)}) async-start(), calls=%async_computation.3 | async-start | bytes 8912896 | tf_op jit(solution)/shard_map/all_gather | solution.py:376
  8.5 221.2 %all-gather.5.cloned.1.call-start = ((), (), s32[]{:S(2)}) async-start(), calls=%async_computation.4 | async-start | bytes 4456448 | tf_op jit(solution)/shard_map/all_gather | solution.py:377
  9.3 409.6 %reduce-scatter.2.cloned.1.call-start = ((), (), s32[]{:S(2)}) async-start(), calls=%async_computation.5 | async-start | bytes 9437184 | tf_op jit(solution)/shard_map/reduce_scatter | solution.py:384
  11.4 24.1 %collective-permute-start = (bf16[512,512]{1,0:T(8,128)(2,1)S(1)}, bf16[512,512]{1,0:T(8,128)(2,1)S(1)}, u32[]{:S(2)}, u32[]{:S(2)}) collective-permute-start(bf16[512,512]{1,0:T(8,128)(2,1)S(1)} %get-tuple-element.10), channel_id=1, source_target_pairs={{0,120},{8,112},{16,104},{24,96},{32,88},{40,80},{48,72},{56,64},{... | collective-permute-start | bytes 1572872 | tf_op jit(solution)/shard_map/ppermute | solution.py:368
  35.5 50.4 %copy-start.1 = (bf16[512,512]{1,0:T(8,128)(2,1)}, bf16[512,512]{1,0:T(8,128)(2,1)S(1)}, u32[]{:S(2)}) copy-start(bf16[512,512]{1,0:T(8,128)(2,1)S(1)} %collective-permute-done.q_ref) | copy-start | bytes 1572868
  221.4 17.2 %collective-permute-start.1 = (bf16[512,512]{1,0:T(8,128)(2,1)}, bf16[512,512]{1,0:T(8,128)(2,1)S(1)}, u32[]{:S(2)}, u32[]{:S(2)}) collective-permute-start(bf16[512,512]{1,0:T(8,128)(2,1)} %attend.3), channel_id=1, source_target_pairs={{0,120},{8,112},{16,104},{24,96},{32,88},{40,80},{48,72},{56,64},{... | collective-permute-start | bytes 1572872 | tf_op jit(solution)/shard_map/ppermute | solution.py:381
  248.7 0.7 copy-start.2
  250.6 265.1 %copy-start = (s32[128,4]{1,0:T(8,128)}, s32[128,4]{1,0:T(8,128)S(1)}, u32[]{:S(2)}) copy-start(s32[128,4]{1,0:T(8,128)S(1)} %add.11.target_ref) | copy-start | bytes 6148
  551.1 7.3 %copy-start.3 = (f32[128,4]{0,1:T(4,128)S(1)}, f32[128,4]{0,1:T(4,128)}, u32[]{:S(2)}) copy-start(f32[128,4]{0,1:T(4,128)} %param.18) | copy-start | bytes 6148
  551.1 83.1 %all-to-all-start.1 = ((bf16[128,48,512]{2,1,0:T(8,128)(2,1)}), bf16[128,48,512]{2,1,0:T(8,128)(2,1)}, u32[]{:S(2)}, u32[]{:S(2)}) async-start(bf16[128,48,512]{2,1,0:T(8,128)(2,1)} %bitcast.24), calls=%async_computation.2 | async-start | bytes 12582912 | tf_op jit(solution)/shard_map/all_to_all | solution.py:394
Sparse Core Ops, SparseCore 0:
  9.5 76.3 all-gather.2
  88.0 57.4 all-gather.4
  248.8 170.0 reduce-scatter.1

commit v2 on v1

--- a/solution.py
+++ b/solution.py
@@ -23,20 +23,50 @@
 PIECES = 8
 GROUP = 8
 GROUP_ROWS = GROUP * CAP
+STEP_GROUPS = 4
+STEP_PIECES = 2
 VMEM_BYTES = 56 * 2**20
+ATTEND_VMEM = 24 * 2**20
+PAIR_HEADS = 2
 
 VMEM_SPEC = pl.BlockSpec(memory_space=pltpu.VMEM)
 SMEM_SPEC = pl.BlockSpec(memory_space=pltpu.SMEM)
 
 
 def piece_swap():
-    swap = np.zeros((GROUP, PIECES, CAP, PIECES, GROUP, CAP), np.float32)
-    for device in range(GROUP):
+    devices = GROUP // 2
+    swap = np.zeros((PIECES, devices, CAP, devices, PIECES, CAP), np.float32)
+    for device in range(devices):
         for piece in range(PIECES):
             for slot in range(CAP):
-                swap[device, piece, slot, piece, device, slot] = 1
-    size = GROUP * PIECES * CAP
-    return jnp.asarray(swap.reshape(size, size), jnp.bfloat16)
+                swap[piece, device, slot, device, piece, slot] = 1
+    size = devices * PIECES * CAP
+    swap = swap.reshape(size, size)
+    return jnp.asarray(np.stack([swap, swap.T]), jnp.bfloat16)
+
+
+def unpack_group(swap_ref, message_ref, first, rows_of, to):
+    size = swap_ref.shape[1]
+    part = size // PIECES
+    halves = [
+        dot_f32(swap_ref[0], message_ref[pl.ds(pl.multiple_of(first + half * size, size), size), :])
+        for half in range(2)
+    ]
+    for piece in range(PIECES):
+        rows_of[piece, to, :] = jnp.concatenate(
+            [half[piece * part : (piece + 1) * part] for half in halves], 0
+        ).astype(jnp.bfloat16)
+
+
+def pack_group(swap_ref, rows_of, at, message_ref, first):
+    size = swap_ref.shape[1]
+    part = size // PIECES
+    pieces = [rows_of[piece, at, :].astype(jnp.float32) for piece in range(PIECES)]
+    for half in range(2):
+        stacked = jnp.concatenate([rows[half * part : (half + 1) * part] for rows in pieces], 0)
+        message_ref[pl.ds(pl.multiple_of(first + half * size, size), size), :] = dot_f32(
+            swap_ref[1], stacked.astype(jnp.bfloat16)
+        ).astype(jnp.bfloat16)
 
 
 def dot_f32(left, right):
@@ -49,13 +79,11 @@
     )
 
 
-def attend_kernel(block_ref, q_ref, kv_ref, out_ref, q_wide, top, acc):
+def attend_part(block, shift, q_ref, kv_ref, out_ref, q_wide, top, acc):
     rows, width, sub = q_ref.shape[0], KEY_WIDTH, SUB_ROWS
     heads = q_ref.shape[1] // HEAD_DIM
     tiles = heads * rows // sub
-    block = block_ref[0]
     last = (block * rows) // width
-    shift = block * rows - last * width
     bound = jnp.full((1, 1), jnp.inf, jnp.float32)
     ones = jnp.ones((width, HEAD_DIM), jnp.bfloat16)
 
@@ -78,13 +106,14 @@
     for tile in range(tiles):
         at = slice(tile * sub, (tile + 1) * sub)
         first = (tile * sub) % rows
-        scores = dot_keys(q_wide[at, :], keys)
-        row = lax.broadcasted_iota(jnp.int32, (sub, width), 0) + (first + shift)
-        col = lax.broadcasted_iota(jnp.int32, (sub, width), 1)
+        seen = shift + first + sub
+        scores = dot_keys(q_wide[at, :], keys[:seen])
+        row = lax.broadcasted_iota(jnp.int32, (sub, seen), 0) + (first + shift)
+        col = lax.broadcasted_iota(jnp.int32, (sub, seen), 1)
         scores = jnp.where(col <= row, scores, -1e30)
         best = jnp.max(scores, axis=1, keepdims=True)
         weights = jnp.exp2(scores - best).astype(jnp.bfloat16)
-        acc[at, :] = dot_f32(weights, values)
+        acc[at, :] = dot_f32(weights, values[:seen])
         top[at, :] = jnp.broadcast_to(best, (sub, HEAD_DIM))
         norm = norms[(tile * sub) // rows][first : first + sub]
         bound = jnp.minimum(
@@ -147,22 +176,29 @@
         ).astype(jnp.bfloat16)
 
 
-def attend(block, queries, keys_values):
-    rows, columns = queries.shape
+def attend_kernel(block_ref, far_ref, near_ref, kv_ref, far_out, near_out, q_wide, top, acc):
+    rows = near_ref.shape[0]
+    attend_part(block_ref[0], rows, far_ref, kv_ref, far_out, q_wide, top, acc)
+    attend_part(block_ref[1], 0, near_ref, kv_ref, near_out, q_wide, top, acc)
+
+
+def attend(blocks, far, near, keys_values):
+    rows, columns = near.shape
     all_rows = rows * columns // HEAD_DIM
+    result = jax.ShapeDtypeStruct((rows, columns), jnp.bfloat16)
     return pl.pallas_call(
         attend_kernel,
-        out_shape=jax.ShapeDtypeStruct(queries.shape, jnp.bfloat16),
-        in_specs=[SMEM_SPEC, VMEM_SPEC, VMEM_SPEC],
-        out_specs=VMEM_SPEC,
+        out_shape=(result, result),
+        in_specs=[SMEM_SPEC, VMEM_SPEC, VMEM_SPEC, VMEM_SPEC],
+        out_specs=(VMEM_SPEC, VMEM_SPEC),
         scratch_shapes=[
             pltpu.VMEM((all_rows, 2 * HEAD_DIM), jnp.bfloat16),
             pltpu.VMEM((all_rows, HEAD_DIM), jnp.float32),
             pltpu.VMEM((all_rows, 2 * HEAD_DIM), jnp.float32),
         ],
-        compiler_params=pltpu.CompilerParams(vmem_limit_bytes=VMEM_BYTES),
+        compiler_params=pltpu.CompilerParams(vmem_limit_bytes=ATTEND_VMEM),
         name="attend",
-    )(block, queries, keys_values)
+    )(blocks, far, near, keys_values)
 
 
 def dispatch_kernel(target_ref, attn_ref, residual_ref, gain_ref, swap_ref, hidden_ref, out_ref, rows_of):
@@ -188,9 +224,11 @@
                 chosen, normed[:, piece * PIECE : (piece + 1) * PIECE]
             ).astype(jnp.bfloat16)
 
-    at = pl.ds(pl.multiple_of(step * GROUP_ROWS, GROUP_ROWS), GROUP_ROWS)
-    stacked = jnp.concatenate([rows_of[piece, at, :] for piece in range(PIECES)], 0)
-    out_ref[...] = dot_f32(swap_ref[...], stacked).astype(jnp.bfloat16)
+    group_block = GROUP_ROWS * PIECES
+    for part in range(STEP_GROUPS):
+        at = (step * STEP_GROUPS + part) * GROUP_ROWS
+        at = pl.ds(pl.multiple_of(at, GROUP_ROWS), GROUP_ROWS)
+        pack_group(swap_ref, rows_of, at, out_ref, part * group_block)
 
 
 def dispatch(target, attn_out, residual, gain, swap, dev_count):
@@ -203,7 +241,7 @@
 
     return pl.pallas_call(
         dispatch_kernel,
-        grid=(dev_count // GROUP,),
+        grid=(dev_count // (GROUP * STEP_GROUPS),),
         out_shape=(
             jax.ShapeDtypeStruct((tokens, model), jnp.bfloat16),
             jax.ShapeDtypeStruct((slots * PIECES, PIECE), jnp.bfloat16),
@@ -213,11 +251,11 @@
             whole((tokens, model)),
             whole((tokens, model)),
             whole((1, model)),
-            whole((group_block, group_block)),
+            pl.BlockSpec(swap.shape, lambda step: (0, 0, 0)),
         ],
         out_specs=(
             whole((tokens, model)),
-            pl.BlockSpec((group_block, PIECE), lambda step: (step, 0)),
+            pl.BlockSpec((STEP_GROUPS * group_block, PIECE), lambda step: (step, 0)),
         ),
         scratch_shapes=[pltpu.VMEM((PIECES, slots, PIECE), jnp.bfloat16)],
         compiler_params=pltpu.CompilerParams(vmem_limit_bytes=VMEM_BYTES),
@@ -227,60 +265,70 @@
 
 def expert_kernel(arrived_ref, swap_ref, in_ref, down_ref, out_ref, rows_of, gate_up, active):
     step = pl.program_id(0)
+    half = pl.num_programs(0) // 2
     groups = rows_of.shape[1] // GROUP_ROWS
     group_block = GROUP_ROWS * PIECES
 
     @pl.when(step == 0)
     def _():
         def unpack(group, carry):
-            at = pl.ds(pl.multiple_of(group * group_block, group_block), group_block)
-            stacked = dot_f32(swap_ref[...], arrived_ref[at, :]).astype(jnp.bfloat16)
             to = pl.ds(pl.multiple_of(group * GROUP_ROWS, GROUP_ROWS), GROUP_ROWS)
-            for piece in range(PIECES):
-                rows_of[piece, to, :] = stacked[piece * GROUP_ROWS : (piece + 1) * GROUP_ROWS]
+            unpack_group(swap_ref, arrived_ref, group * group_block, rows_of, to)
             return carry
 
-        lax.fori_loop(0, groups, unpack, 0, unroll=2)
-        gate_up[...] = jnp.zeros_like(gate_up)
-
-    @pl.when(step < PIECES)
-    def _():
-        gate_up[...] += dot_f32(rows_of[step], in_ref[...])
-
-    @pl.when(step == PIECES - 1)
+        lax.fori_loop(0, groups, unpack, 0, unroll=4)
+
+    def product():
+        first = step * STEP_PIECES
+        rows = jnp.concatenate([rows_of[first + part] for part in range(STEP_PIECES)], 1)
+        return dot_f32(rows, in_ref[...])
+
+    @pl.when(step == 0)
+    def _():
+        gate_up[...] = product()
+
+    @pl.when((step > 0) & (step < half))
+    def _():
+        gate_up[...] += product()
+
+    @pl.when(step == half - 1)
     def _():
         active[...] = (jax.nn.silu(gate_up[:, :FF]) * gate_up[:, FF:]).astype(jnp.bfloat16)
 
-    @pl.when(step >= PIECES)
-    def _():
-        rows_of[step - PIECES] = dot_f32(active[...], down_ref[...]).astype(jnp.bfloat16)
-
-    @pl.when(step == 2 * PIECES - 1)
+    @pl.when(step >= half)
+    def _():
+        first = (step - half) * STEP_PIECES
+        for part in range(STEP_PIECES):
+            rows_of[first + part] = dot_f32(
+                active[...], down_ref[:, part * PIECE : (part + 1) * PIECE]
+            ).astype(jnp.bfloat16)
+
+    @pl.when(step == 2 * half - 1)
     def _():
         def pack(group, carry):
             at = pl.ds(pl.multiple_of(group * GROUP_ROWS, GROUP_ROWS), GROUP_ROWS)
-            stacked = jnp.concatenate([rows_of[piece, at, :] for piece in range(PIECES)], 0)
-            to = pl.ds(pl.multiple_of(group * group_block, group_block), group_block)
-            out_ref[to, :] = dot_f32(swap_ref[...], stacked).astype(jnp.bfloat16)
+            pack_group(swap_ref, rows_of, at, out_ref, group * group_block)
             return carry
 
-        lax.fori_loop(0, groups, pack, 0, unroll=2)
+        lax.fori_loop(0, groups, pack, 0, unroll=4)
 
 
 def run_expert(arrived, swap, w_in, w_out):
     slots = arrived.shape[0] // PIECES
     group_block = GROUP_ROWS * PIECES
+    half = PIECES // STEP_PIECES
+    width = STEP_PIECES * PIECE
     return pl.pallas_call(
         expert_kernel,
-        grid=(2 * PIECES,),
+        grid=(2 * half,),
         out_shape=jax.ShapeDtypeStruct(arrived.shape, jnp.bfloat16),
         in_specs=[
-            pl.BlockSpec(arrived.shape, lambda step: (0, 0)),
-            pl.BlockSpec((group_block, group_block), lambda step: (0, 0)),
-            pl.BlockSpec((PIECE, 2 * FF), lambda step: (jnp.minimum(step, PIECES - 1), 0)),
-            pl.BlockSpec((FF, PIECE), lambda step: (0, jnp.maximum(step - PIECES, 0))),
-        ],
-        out_specs=pl.BlockSpec(arrived.shape, lambda step: (0, 0)),
+            pl.BlockSpec(arrived.shape, lambda step: (0, 0), pipeline_mode=pl.Buffered(1)),
+            pl.BlockSpec(swap.shape, lambda step: (0, 0, 0)),
+            pl.BlockSpec((width, 2 * FF), lambda step: (jnp.minimum(step, half - 1), 0)),
+            pl.BlockSpec((FF, width), lambda step: (0, jnp.maximum(step - half, 0))),
+        ],
+        out_specs=pl.BlockSpec(arrived.shape, lambda step: (0, 0), pipeline_mode=pl.Buffered(1)),
         scratch_shapes=[
             pltpu.VMEM((PIECES, slots, PIECE), jnp.bfloat16),
             pltpu.VMEM((slots, 2 * FF), jnp.float32),
@@ -293,10 +341,11 @@
 
 def combine_kernel(target_ref, route_ref, hidden_ref, swap_ref, back_ref, out_ref, rows_of):
     step = pl.program_id(0)
-    stacked = dot_f32(swap_ref[...], back_ref[...]).astype(jnp.bfloat16)
-    to = pl.ds(pl.multiple_of(step * GROUP_ROWS, GROUP_ROWS), GROUP_ROWS)
-    for piece in range(PIECES):
-        rows_of[piece, to, :] = stacked[piece * GROUP_ROWS : (piece + 1) * GROUP_ROWS]
+    group_block = GROUP_ROWS * PIECES
+    for part in range(STEP_GROUPS):
+        to = (step * STEP_GROUPS + part) * GROUP_ROWS
+        to = pl.ds(pl.multiple_of(to, GROUP_ROWS), GROUP_ROWS)
+        unpack_group(swap_ref, back_ref, part * group_block, rows_of, to)
 
     @pl.when(step == pl.num_programs(0) - 1)
     def _():
@@ -330,14 +379,14 @@
 
     return pl.pallas_call(
         combine_kernel,
-        grid=(slots // GROUP_ROWS,),
+        grid=(slots // (GROUP_ROWS * STEP_GROUPS),),
         out_shape=jax.ShapeDtypeStruct((tokens, model), jnp.bfloat16),
         in_specs=[
             whole((tokens, TOPK)),
             whole((tokens, TOPK)),
             whole((tokens, model)),
-            whole((group_block, group_block)),
-            pl.BlockSpec((group_block, PIECE), lambda step: (step, 0)),
+            pl.BlockSpec(swap.shape, lambda step: (0, 0, 0)),
+            pl.BlockSpec((STEP_GROUPS * group_block, PIECE), lambda step: (step, 0)),
         ],
         out_specs=whole((tokens, model)),
         scratch_shapes=[pltpu.VMEM((PIECES, slots, PIECE), jnp.bfloat16)],
@@ -375,12 +424,16 @@
     )
     all_kv = lax.all_gather(own_kv, "ctx", axis=0, tiled=True)
     full_proj = lax.all_gather(out_proj, "ctx", axis=1, tiled=True)
-    far_block = (2 * ctx_count - 1 - 2 * ctx_index).astype(jnp.int32).reshape(1)
-    near_block = (2 * ctx_index).astype(jnp.int32).reshape(1)
-    far = attend(far_block, swapped, all_kv)
-    returned = lax.ppermute(far, "ctx", opposite)
-    near = attend(near_block, queries[:half], all_kv)
-    attended = jnp.concatenate([near, returned], 0)
+    blocks = jnp.stack([2 * ctx_count - 1 - 2 * ctx_index, 2 * ctx_index]).astype(jnp.int32)
+    nears, returned = [], []
+    for first in range(0, heads_here, PAIR_HEADS):
+        pair = slice(first * HEAD_DIM, (first + PAIR_HEADS) * HEAD_DIM)
+        far, near = attend(blocks, swapped[:, pair], queries[:half, pair], all_kv)
+        nears.append(near)
+        returned.append(lax.ppermute(far, "ctx", opposite))
+    attended = jnp.concatenate(
+        [jnp.concatenate(nears, 1), jnp.concatenate(returned, 1)], 0
+    )
     attn_out = lax.psum_scatter(
         dot_f32(attended, full_proj).astype(jnp.bfloat16), "tp", scatter_dimension=0, tiled=True
     )

time: 660 us -> 523 us (0.79)
  waiting for transfers between devices: 320 us -> 199 us
  Pallas kernels: 208 us -> 183 us
    reduce_scatter x1, waiting for transfers between devices: 168 us -> 46.2 us  [body(): lax.psum_scatter(dot_f32(attended, full_proj).astype(jnp.bfloat16), 'tp',...]
    pallas_call x5, Pallas kernels: 208 us -> 183 us  [the longest x2 139 us: attend(): pl.pallas_call(attend_kernel, out_shape=(result, result), in_specs=[SMEM_...]
  transfers between devices with their start and end apart: 6 -> 7, of which waited for: 5 -> 5; matrix products, arithmetic and copies ran while one was open for 1% -> 1% of each run, Pallas kernels for 22% -> 27%
where the time goes in v2:
time: 523 us; the launch traced here: 519 us
  waiting for transfers between devices  199 us (38%)
  Pallas kernels  183 us (35%)
  blocking collectives  83.5 us (16%)
  starting transfers between devices  19.4 us (4%)
  between operations  13.2 us (3%)
  matrix products  11.6 us (2%)
  local copies, waits for them, and re-layouts  8.45 us (2%)
    pallas_call x2, Pallas kernels, attend(): pl.pallas_call(attend_kernel, out_shape=(result, result), in_specs=[SMEM_...  139 us
    all_to_all x1, blocking collectives, exchange(): lax.all_to_all(shaped, ('ctx', 'tp'), split_axis=0, concat_axis=0, tiled=...  83.5 us
    all_to_all x1, waiting for transfers between devices, exchange(): lax.all_to_all(shaped, ('ctx', 'tp'), split_axis=0, concat_axis=0, tiled=...  75 us
    all_gather x1, waiting for transfers between devices, body(): all_kv = lax.all_gather(own_kv, 'ctx', axis=0, tiled=True)  51.1 us
    reduce_scatter x1, waiting for transfers between devices, body(): lax.psum_scatter(dot_f32(attended, full_proj).astype(jnp.bfloat16), 'tp',...  46.2 us
    pallas_call x1, Pallas kernels, run_expert(): pl.pallas_call(expert_kernel, grid=(2 * half,), out_shape=jax.ShapeDtypeS...  28.1 us
    ppermute x1, waiting for transfers between devices, body(): swapped = lax.ppermute(queries[half:], 'ctx', opposite)  16.9 us
    dot_general x1, matrix products, dot_f32(): return jnp.dot(left, right, preferred_element_type=jnp.float32)  11.6 us
  transfers between devices with their start and end apart: 7, of which 5 were waited for; matrix products, arithmetic and copies ran while one was open for 1% of the time, Pallas kernels for 27%

profile of v2, /device:TPU:6, one launch (start us, length us, event | category | flops | bytes accessed | tf_op | source)
XLA Modules:
  0.0 519.4 jit_solution(11789548102409337323)
XLA Ops:
  6.5 0.0 copy-start.2
  6.5 0.0 all-gather.3.cloned.1.call-start
  6.5 1.2 constant_dynamic-slice_fusion
  7.7 0.9 pad_maximum_fusion
  8.5 0.0 all-gather.3.cloned.1.call-update
  8.6 0.0 all-gather.5.cloned.1.call-start
  8.6 0.7 all-gather.5.cloned.1.call-update
  9.3 0.0 reduce-scatter.2.cloned.1.call-start
  9.4 1.1 slice.23
  10.5 6.6 %collective-permute-start = (bf16[512,512]{1,0:T(8,128)(2,1)S(1)}, bf16[512,512]{1,0:T(8,128)(2,1)S(1)}, u32[]{:S(2)}, u32[]{:S(2)}) collective-permute-start(bf16[512,512]{1,0:T(8,128)(2,1)S(1)} %slice.23), channel_id=1, source_target_pairs={{0,120},{8,112},{16,104},{24,96},{32,88},{40,80},{48,72},{56,64},{... | collective-permute-start | bytes 1572872 | tf_op jit(solution)/shard_map/ppermute | solution.py:417
  17.0 0.1 pad_add_fusion.block_ref
  17.1 0.0 copy-done.2
  17.1 16.9 %collective-permute-done = bf16[512,512]{1,0:T(8,128)(2,1)S(1)} collective-permute-done((bf16[512,512]{1,0:T(8,128)(2,1)S(1)}, bf16[512,512]{1,0:T(8,128)(2,1)S(1)}, u32[]{:S(2)}, u32[]{:S(2)}) %collective-permute-start) | collective-permute-done | bytes 524320 | tf_op jit(solution)/shard_map/ppermute | solution.py:417
  34.1 51.1 %all-gather.3.cloned.1.call-done.kv_ref = bf16[16384,256]{1,0:T(8,128)(2,1)} async-done(((bf16[1024,256]{1,0:T(8,128)(2,1)}), bf16[16384,256]{1,0:T(8,128)(2,1)}) %all-gather.3.cloned.1.call-update) | async-done | bytes 8388624 | tf_op jit(solution)/shard_map/all_gather | solution.py:425
  85.2 0.0 copy-start
  85.2 3.4 copy-done
  88.6 0.0 copy-start.1
  88.6 69.3 %attend.2 = (bf16[512,256]{1,0:T(8,128)(2,1)S(1)}, bf16[512,256]{1,0:T(8,128)(2,1)S(1)}) custom-call(s32[2]{0:T(128)S(1)} %pad_add_fusion.block_ref, bf16[512,256]{1,0:T(8,128)(2,1)S(1)} %get-tuple-element.19.far_ref, bf16[512,256]{1,0:T(8,128)(2,1)S(1)} %get-tuple-element.17.near_ref, bf16[16384,256]{1,0:T(8,128)(2,1)S(1)} %copy-done), custom_call_target="tpu_custom_call" | custom-call | tf_op jit(solution)/shard_map/attend/pallas_call | solution.py:189
  157.8 3.0 collective-permute-start.1
  160.9 0.0 copy-done.1
  160.9 69.5 %attend.3 = (bf16[512,256]{1,0:T(8,128)(2,1)S(1)}, bf16[512,256]{1,0:T(8,128)(2,1)S(1)}) custom-call(s32[2]{0:T(128)S(1)} %pad_add_fusion.block_ref, bf16[512,256]{1,0:T(8,128)(2,1)S(1)} %get-tuple-element.20.far_ref, bf16[512,256]{1,0:T(8,128)(2,1)S(1)} %get-tuple-element.18.near_ref, bf16[16384,256]{1,0:T(8,128)(2,1)S(1)} %copy-done.1), custom_call_target="tpu_custom_call" | custom-call | tf_op jit(solution)/shard_map/attend/pallas_call | solution.py:189
  230.3 2.4 collective-permute-start.2
  232.7 0.0 all-gather.5.cloned.1.call-done
  232.7 0.0 collective-permute-done.1
  232.7 8.7 %collective-permute-done.2 = bf16[512,256]{1,0:T(8,128)(2,1)S(1)} collective-permute-done((bf16[512,256]{1,0:T(8,128)(2,1)S(1)}, bf16[512,256]{1,0:T(8,128)(2,1)S(1)}, u32[]{:S(2)}, u32[]{:S(2)}) %collective-permute-start.2) | collective-permute-done | bytes 262176 | tf_op jit(solution)/shard_map/ppermute | solution.py:433
  241.5 11.6 %convolution_convert_fusion = bf16[1024,4096]{1,0:T(8,128)(2,1)} fusion(bf16[512,4096]{1,0:T(8,128)(2,1)} %all-gather.5.cloned.1.call-done, bf16[512,256]{1,0:T(8,128)(2,1)S(1)} %collective-permute-done.2, bf16[512,256]{1,0:T(8,128)(2,1)S(1)} %collective-permute-done.1, bf16[512,256]{1,0:T(8,128)(2,1)S(1)} %get-tuple-element.12, ...), kind=kOutput, calls=%fused_computation | convolution fusion | flops 4303355904 | bytes 13631488 | tf_op jit(solution)/shard_map/dot_general | solution.py:73
  253.1 0.0 reduce-scatter.2.cloned.1.call-update
  253.1 0.7 copy-done.4
  253.7 0.1 copy.24
  253.8 0.1 eq.29
  254.0 0.1 eq.25
  254.1 0.1 copy.26
  254.2 0.2 fusion.9
  254.5 0.2 fusion.8
  254.7 0.1 reduce_sum.12
  254.9 0.1 copy.28
  255.0 0.0 copy-start.3
  255.0 0.7 copy.29.target_ref
  255.7 46.2 %reduce-scatter.2.cloned.1.call-done.attn_ref = bf16[128,4096]{1,0:T(8,128)(2,1)} async-done(((bf16[1024,4096]{1,0:T(8,128)(2,1)}), bf16[128,4096]{1,0:T(8,128)(2,1)}) %reduce-scatter.2.cloned.1.call-update) | async-done | bytes 1048592 | tf_op jit(solution)/shard_map/reduce_scatter | solution.py:437
  301.9 8.2 %norm_and_dispatch.1 = (bf16[128,4096]{1,0:T(8,128)(2,1)}, bf16[6144,512]{1,0:T(8,128)(2,1)}) custom-call(s32[4,128]{1,0:T(4,128)} %copy.29.target_ref, bf16[128,4096]{1,0:T(8,128)(2,1)} %reduce-scatter.2.cloned.1.call-done.attn_ref, bf16[128,4096]{1,0:T(8,128)(2,1)} %residual_ref.1, f32[1,4096]{1,0:T(1,128)} %bitcast.32, ...), custom_call_target="tpu_custom_call" | custom-call | tf_op jit(solution)/shard_map/norm_and_dispatch/pallas_call | solution.py:242
  310.0 83.5 %all_to_all.10 = bf16[128,48,512]{2,1,0:T(8,128)(2,1)} all-to-all(bf16[128,48,512]{2,1,0:T(8,128)(2,1)} %bitcast.27), channel_id=1, replica_groups=mesh['ctx'=16,'tp'=8] {'ctx','tp'}, dimensions={0} | all-to-all | bytes 12582912 | tf_op jit(solution)/shard_map/all_to_all | solution.py:447
  393.5 0.0 copy-done.3
  393.5 28.1 %expert.1 = bf16[6144,512]{1,0:T(8,128)(2,1)} custom-call(bf16[6144,512]{1,0:T(8,128)(2,1)} %bitcast.25, bf16[2,192,192]{2,1,0:T(8,128)(2,1)} %constant.43.clone.swap_ref, bf16[4096,1536]{1,0:T(8,128)(2,1)} %bitcast.26, bf16[768,4096]{1,0:T(8,128)(2,1)} %bitcast.28), custom_call_target="tpu_custom_call" | custom-call | tf_op jit(solution)/shard_map/expert/pallas_call | solution.py:321
  421.6 7.3 %all-to-all-start.1 = ((bf16[128,48,512]{2,1,0:T(8,128)(2,1)}), bf16[128,48,512]{2,1,0:T(8,128)(2,1)}, u32[]{:S(2)}, u32[]{:S(2)}) async-start(bf16[128,48,512]{2,1,0:T(8,128)(2,1)} %bitcast.24), calls=%async_computation.2 | async-start | bytes 12582912 | tf_op jit(solution)/shard_map/all_to_all | solution.py:447
  429.0 0.0 copy-done.5
  429.0 0.8 copy.30.route_ref
  429.7 75.0 %all-to-all-done.1 = bf16[128,48,512]{2,1,0:T(8,128)(2,1)} async-done(((bf16[128,48,512]{2,1,0:T(8,128)(2,1)}), bf16[128,48,512]{2,1,0:T(8,128)(2,1)}, u32[]{:S(2)}, u32[]{:S(2)}) %all-to-all-start.1) | async-done | bytes 6291488 | tf_op jit(solution)/shard_map/all_to_all | solution.py:447
  504.7 8.1 %combine.1 = bf16[128,4096]{1,0:T(8,128)(2,1)} custom-call(s32[128,4]{1,0:T(8,128)} %copy-done.3, f32[128,4]{1,0:T(8,128)} %copy.30.route_ref, bf16[128,4096]{1,0:T(8,128)(2,1)} %get-tuple-element.15.hidden_ref, bf16[2,192,192]{2,1,0:T(8,128)(2,1)} %constant.43.clone.swap_ref, bf16[6144,512]{1,0:T(8,128)(2,1)} %bitcast.12.back_ref), custom_call_target="tpu_custom_call" | custom-call | tf_op jit(solution)/shard_map/combine/pallas_call | solution.py:380
  (12 shorter events, 0.2 us)
Async XLA Ops:
  6.5 10.6 %copy-start.2 = (bf16[1024,512]{1,0:T(8,128)(2,1)S(1)}, bf16[1024,512]{1,0:T(8,128)(2,1)}, u32[]{:S(2)}) copy-start(bf16[1024,512]{1,0:T(8,128)(2,1)} %param.11) | copy-start | bytes 3145732
  6.5 78.6 %all-gather.3.cloned.1.call-start = ((), (), s32[]{:S(2)}) async-start(), calls=%async_computation.3 | async-start | bytes 8912896 | tf_op jit(solution)/shard_map/all_gather | solution.py:425
  8.6 224.2 %all-gather.5.cloned.1.call-start = ((), (), s32[]{:S(2)}) async-start(), calls=%async_computation.4 | async-start | bytes 4456448 | tf_op jit(solution)/shard_map/all_gather | solution.py:426
  9.3 292.5 %reduce-scatter.2.cloned.1.call-start = ((), (), s32[]{:S(2)}) async-start(), calls=%async_computation.5 | async-start | bytes 9437184 | tf_op jit(solution)/shard_map/reduce_scatter | solution.py:437
  10.5 23.6 %collective-permute-start = (bf16[512,512]{1,0:T(8,128)(2,1)S(1)}, bf16[512,512]{1,0:T(8,128)(2,1)S(1)}, u32[]{:S(2)}, u32[]{:S(2)}) collective-permute-start(bf16[512,512]{1,0:T(8,128)(2,1)S(1)} %slice.23), channel_id=1, source_target_pairs={{0,120},{8,112},{16,104},{24,96},{32,88},{40,80},{48,72},{56,64},{... | collective-permute-start | bytes 1572872 | tf_op jit(solution)/shard_map/ppermute | solution.py:417
  85.2 3.4 copy-start
  88.6 72.3 %copy-start.1 = (bf16[16384,256]{1,0:T(8,128)(2,1)S(1)}, bf16[16384,256]{1,0:T(8,128)(2,1)}, u32[]{:S(2)}) copy-start(bf16[16384,256]{1,0:T(8,128)(2,1)} %all-gather.3.cloned.1.call-done.kv_ref) | copy-start | bytes 25165828
  157.8 74.9 %collective-permute-start.1 = (bf16[512,256]{1,0:T(8,128)(2,1)S(1)}, bf16[512,256]{1,0:T(8,128)(2,1)S(1)}, u32[]{:S(2)}, u32[]{:S(2)}) collective-permute-start(bf16[512,256]{1,0:T(8,128)(2,1)S(1)} %get-tuple-element.13), channel_id=1, source_target_pairs={{0,120},{8,112},{16,104},{24,96},{32,88},{40,80},{48,72},{56,64},{... | collective-permute-start | bytes 786440 | tf_op jit(solution)/shard_map/ppermute | solution.py:433
  230.3 11.2 %collective-permute-start.2 = (bf16[512,256]{1,0:T(8,128)(2,1)S(1)}, bf16[512,256]{1,0:T(8,128)(2,1)S(1)}, u32[]{:S(2)}, u32[]{:S(2)}) collective-permute-start(bf16[512,256]{1,0:T(8,128)(2,1)S(1)} %get-tuple-element.14), channel_id=1, source_target_pairs={{0,120},{8,112},{16,104},{24,96},{32,88},{40,80},{48,72},{56,64},{... | collective-permute-start | bytes 786440 | tf_op jit(solution)/shard_map/ppermute | solution.py:433
  253.1 0.7 copy-start.4
  255.0 138.5 %copy-start.3 = (s32[128,4]{1,0:T(8,128)}, s32[128,4]{1,0:T(8,128)S(1)}, u32[]{:S(2)}) copy-start(s32[128,4]{1,0:T(8,128)S(1)} %add.11.target_ref) | copy-start | bytes 6148
  421.6 7.3 %copy-start.5 = (f32[128,4]{0,1:T(4,128)S(1)}, f32[128,4]{0,1:T(4,128)}, u32[]{:S(2)}) copy-start(f32[128,4]{0,1:T(4,128)} %param.18) | copy-start | bytes 6148
  421.6 83.1 %all-to-all-start.1 = ((bf16[128,48,512]{2,1,0:T(8,128)(2,1)}), bf16[128,48,512]{2,1,0:T(8,128)(2,1)}, u32[]{:S(2)}, u32[]{:S(2)}) async-start(bf16[128,48,512]{2,1,0:T(8,128)(2,1)} %bitcast.24), calls=%async_computation.2 | async-start | bytes 12582912 | tf_op jit(solution)/shard_map/all_to_all | solution.py:447
Sparse Core Ops, SparseCore 0:
  9.5 75.6 all-gather.2
  87.3 57.3 all-gather.4
  253.2 48.6 reduce-scatter.1

commit v3 on v2

--- a/solution.py
+++ b/solution.py
@@ -18,7 +18,8 @@
 BASE2_SCALE = math.log2(math.e) / math.sqrt(HEAD_DIM)
 EXPONENT_LIMIT = 100.0
 KEY_WIDTH = 1024
-SUB_ROWS = 256
+SUB_ROWS = 512
+WIDE_ROWS = 2048
 PIECE = 512
 PIECES = 8
 GROUP = 8
@@ -26,8 +27,8 @@
 STEP_GROUPS = 4
 STEP_PIECES = 2
 VMEM_BYTES = 56 * 2**20
-ATTEND_VMEM = 24 * 2**20
-PAIR_HEADS = 2
+EXPERT_VMEM = 46 * 2**20
+ATTEND_VMEM = 44 * 2**20
 
 VMEM_SPEC = pl.BlockSpec(memory_space=pltpu.VMEM)
 SMEM_SPEC = pl.BlockSpec(memory_space=pltpu.SMEM)
@@ -79,18 +80,23 @@
     )
 
 
-def attend_part(block, shift, q_ref, kv_ref, out_ref, q_wide, top, acc):
+def attend_part(block, shift, parity, q_ref, mine_ref, other_ref, out_ref, q_wide, top, acc):
     rows, width, sub = q_ref.shape[0], KEY_WIDTH, SUB_ROWS
     heads = q_ref.shape[1] // HEAD_DIM
     tiles = heads * rows // sub
     last = (block * rows) // width
     bound = jnp.full((1, 1), jnp.inf, jnp.float32)
-    ones = jnp.ones((width, HEAD_DIM), jnp.bfloat16)
-
-    def load(index):
-        at = pl.ds(pl.multiple_of(index * width, width), width)
-        keys, values = kv_ref[at, :HEAD_DIM], kv_ref[at, HEAD_DIM:]
-        return jnp.concatenate([keys, keys], 1), jnp.concatenate([values, ones], 1)
+    ones = jnp.ones((acc.shape[0] - HEAD_DIM, width), jnp.bfloat16)
+
+    def load(index, ordered=False):
+        at = pl.ds(pl.multiple_of(index * (width // 2), width // 2), width // 2)
+        first, second = mine_ref[at, :], other_ref[at, :]
+        if ordered:
+            swapped = parity > 0
+            first, second = jnp.where(swapped, second, first), jnp.where(swapped, first, second)
+        both = jnp.concatenate([first, second], 0)
+        keys, values = both[:, :HEAD_DIM], both[:, HEAD_DIM:]
+        return jnp.concatenate([keys, keys], 1), jnp.concatenate([values.T, ones], 0)
 
     norms = []
     for head in range(heads):
@@ -100,105 +106,126 @@
         q_wide[head * rows : (head + 1) * rows, HEAD_DIM:] = (
             scaled - high.astype(jnp.float32)
         ).astype(jnp.bfloat16)
-        norms.append(jnp.sqrt(jnp.sum(scaled * scaled, axis=1, keepdims=True)))
-
-    keys, values = load(last)
+        norms.append(jnp.max(jnp.sum(scaled * scaled, axis=1, keepdims=True), axis=0, keepdims=True))
+    longest_query = jnp.sqrt(functools.reduce(jnp.maximum, norms))
+
+    keys, values = load(last, ordered=True)
+    least = jnp.full((1, sub), jnp.inf, jnp.float32)
     for tile in range(tiles):
         at = slice(tile * sub, (tile + 1) * sub)
         first = (tile * sub) % rows
         seen = shift + first + sub
-        scores = dot_keys(q_wide[at, :], keys[:seen])
-        row = lax.broadcasted_iota(jnp.int32, (sub, seen), 0) + (first + shift)
-        col = lax.broadcasted_iota(jnp.int32, (sub, seen), 1)
-        scores = jnp.where(col <= row, scores, -1e30)
-        best = jnp.max(scores, axis=1, keepdims=True)
+        scores = dot_keys(keys[:seen], q_wide[at, :])
+        key = lax.broadcasted_iota(jnp.int32, (seen, sub), 0)
+        row = lax.broadcasted_iota(jnp.int32, (seen, sub), 1) + (first + shift)
+        scores = jnp.where(key <= row, scores, -1e30)
+        best = jnp.max(scores, axis=0, keepdims=True)
         weights = jnp.exp2(scores - best).astype(jnp.bfloat16)
-        acc[at, :] = dot_f32(weights, values[:seen])
-        top[at, :] = jnp.broadcast_to(best, (sub, HEAD_DIM))
-        norm = norms[(tile * sub) // rows][first : first + sub]
-        bound = jnp.minimum(
-            bound, jnp.min((EXPONENT_LIMIT + best) / norm, axis=0, keepdims=True)
-        )
+        acc[:, at] = dot_f32(values[:, :seen], weights)
+        top[:, at] = jnp.broadcast_to(best, (top.shape[0], sub))
+        least = jnp.minimum(least, best)
+    bound = (EXPONENT_LIMIT + jnp.min(least, axis=1, keepdims=True)) / longest_query
 
     def longest(index, so_far):
-        keys = kv_ref[pl.ds(pl.multiple_of(index * width, width), width), :HEAD_DIM]
-        keys = keys.astype(jnp.float32)
-        length = jnp.sum(keys * keys, axis=1, keepdims=True)
-        return jnp.maximum(so_far, jnp.max(length, axis=0, keepdims=True))
+        at = pl.ds(pl.multiple_of(index * (width // 2), width // 2), width // 2)
+        for held in (mine_ref, other_ref):
+            keys = held[at, :HEAD_DIM].astype(jnp.float32)
+            length = jnp.sum(keys * keys, axis=1, keepdims=True)
+            so_far = jnp.maximum(so_far, jnp.max(length, axis=0, keepdims=True))
+        return so_far
 
     key_norm = jnp.sqrt(lax.fori_loop(0, last, longest, jnp.zeros((1, 1), jnp.float32)))
     safe = jnp.max(key_norm - bound) <= 0.0
 
     @pl.when(safe)
+    def _():
+        def step(index, carry):
+            keys, values = load(index)
+            for first in range(0, heads * rows, WIDE_ROWS):
+                at = slice(first, first + WIDE_ROWS)
+                scores = dot_keys(keys, q_wide[at, :])
+                weights = jnp.exp2(scores - top[:1, at]).astype(jnp.bfloat16)
+                acc[:, at] += dot_f32(values, weights)
+            return carry
+
+        lax.fori_loop(0, last, step, 0)
+
+    @pl.when(jnp.logical_not(safe))
     def _():
         def step(index, carry):
             keys, values = load(index)
             for tile in range(tiles):
                 at = slice(tile * sub, (tile + 1) * sub)
-                scores = dot_keys(q_wide[at, :], keys)
-                best = top[at, :]
-                weights = jnp.concatenate(
-                    [
-                        jnp.exp2(scores[:, c : c + HEAD_DIM] - best).astype(jnp.bfloat16)
-                        for c in range(0, width, HEAD_DIM)
-                    ],
-                    1,
-                )
-                acc[at, :] += dot_f32(weights, values)
+                scores = dot_keys(keys, q_wide[at, :])
+                old = top[:1, at]
+                best = jnp.maximum(old, jnp.max(scores, axis=0, keepdims=True))
+                weights = jnp.exp2(scores - best).astype(jnp.bfloat16)
+                acc[:, at] = acc[:, at] * jnp.exp2(old - best) + dot_f32(values, weights)
+                top[:, at] = jnp.broadcast_to(best, (top.shape[0], sub))
             return carry
-
-        lax.fori_loop(0, last, step, 0)
-
-    @pl.when(jnp.logical_not(safe))
-    def _():
-        def step(index, carry):
-            keys, values = load(index)
-
-            def one_tile(tile, kept):
-                at = pl.ds(pl.multiple_of(tile * sub, sub), sub)
-                scores = dot_keys(q_wide[at, :], keys)
-                old = top[at, :]
-                best = jnp.maximum(old, jnp.max(scores, axis=1, keepdims=True))
-                factor = jnp.exp2(old - best)
-                weights = jnp.exp2(scores - best[:, :1]).astype(jnp.bfloat16)
-                acc[at, :] = acc[at, :] * factor[:, :1] + dot_f32(weights, values)
-                top[at, :] = best
-                return kept
-
-            return lax.fori_loop(0, tiles, one_tile, carry)
 
         lax.fori_loop(0, last, step, 0)
 
     for head in range(heads):
         at = slice(head * rows, (head + 1) * rows)
-        out_ref[:, head * HEAD_DIM : (head + 1) * HEAD_DIM] = (
-            acc[at, :HEAD_DIM] / acc[at, HEAD_DIM:]
-        ).astype(jnp.bfloat16)
-
-
-def attend_kernel(block_ref, far_ref, near_ref, kv_ref, far_out, near_out, q_wide, top, acc):
+        mean = acc[:HEAD_DIM, at] / acc[HEAD_DIM : HEAD_DIM + 1, at]
+        out_ref[:, head * HEAD_DIM : (head + 1) * HEAD_DIM] = mean.T.astype(jnp.bfloat16)
+
+
+def attend_kernel(place_ref, far_ref, near_ref, mine_ref, other_ref, far_out, near_out, *scratch):
     rows = near_ref.shape[0]
-    attend_part(block_ref[0], rows, far_ref, kv_ref, far_out, q_wide, top, acc)
-    attend_part(block_ref[1], 0, near_ref, kv_ref, near_out, q_wide, top, acc)
-
-
-def attend(blocks, far, near, keys_values):
+    parity = place_ref[2]
+    attend_part(place_ref[0], rows, parity, far_ref, mine_ref, other_ref, far_out, *scratch)
+    attend_part(place_ref[1], 0, parity, near_ref, mine_ref, other_ref, near_out, *scratch)
+
+
+def attend(place, far, near, mine, other):
     rows, columns = near.shape
     all_rows = rows * columns // HEAD_DIM
     result = jax.ShapeDtypeStruct((rows, columns), jnp.bfloat16)
     return pl.pallas_call(
         attend_kernel,
         out_shape=(result, result),
-        in_specs=[SMEM_SPEC, VMEM_SPEC, VMEM_SPEC, VMEM_SPEC],
+        in_specs=[SMEM_SPEC] + [VMEM_SPEC] * 4,
         out_specs=(VMEM_SPEC, VMEM_SPEC),
         scratch_shapes=[
             pltpu.VMEM((all_rows, 2 * HEAD_DIM), jnp.bfloat16),
-            pltpu.VMEM((all_rows, HEAD_DIM), jnp.float32),
-            pltpu.VMEM((all_rows, 2 * HEAD_DIM), jnp.float32),
+            pltpu.VMEM((8, all_rows), jnp.float32),
+            pltpu.VMEM((HEAD_DIM + 16, all_rows), jnp.float32),
         ],
         compiler_params=pltpu.CompilerParams(vmem_limit_bytes=ATTEND_VMEM),
         name="attend",
-    )(blocks, far, near, keys_values)
+    )(place, far, near, mine, other)
+
+
+def project_kernel(attended_ref, proj_ref, *rest):
+    rest[-1][...] = dot_f32(attended_ref[...], proj_ref[...]).astype(jnp.bfloat16)
+
+
+def project(attended, proj, half, so_far=None):
+    rows, depth = attended.shape
+    model = proj.shape[1]
+    width = 2 * PIECE
+    operands = (attended, proj) if so_far is None else (attended, proj, so_far)
+    return pl.pallas_call(
+        project_kernel,
+        grid=(model // width,),
+        out_shape=jax.ShapeDtypeStruct((2 * rows, model), jnp.bfloat16),
+        in_specs=[
+            pl.BlockSpec((rows, depth), lambda step: (0, 0)),
+            pl.BlockSpec((depth, width), lambda step: (0, step)),
+            pl.BlockSpec(memory_space=pl.ANY),
+        ][: len(operands)],
+        out_specs=pl.BlockSpec((rows, width), lambda step: (half, step)),
+        input_output_aliases={} if so_far is None else {2: 0},
+        cost_estimate=pl.CostEstimate(
+            flops=2 * rows * depth * model,
+            bytes_accessed=2 * (rows * depth + depth * model + rows * model),
+            transcendentals=0,
+        ),
+        compiler_params=pltpu.CompilerParams(vmem_limit_bytes=VMEM_BYTES // 2),
+        name="project",
+    )(*operands)
 
 
 def dispatch_kernel(target_ref, attn_ref, residual_ref, gain_ref, swap_ref, hidden_ref, out_ref, rows_of):
@@ -263,78 +290,78 @@
     )(target, attn_out, residual, gain, swap)
 
 
-def expert_kernel(arrived_ref, swap_ref, in_ref, down_ref, out_ref, rows_of, gate_up, active):
-    step = pl.program_id(0)
-    half = pl.num_programs(0) // 2
+def expert_kernel(
+    arrived_ref, swap_ref, in_hbm, down_hbm, out_ref, in_ref, down_ref, landed, rows_of, gate_up, active
+):
     groups = rows_of.shape[1] // GROUP_ROWS
     group_block = GROUP_ROWS * PIECES
-
-    @pl.when(step == 0)
-    def _():
-        def unpack(group, carry):
-            to = pl.ds(pl.multiple_of(group * GROUP_ROWS, GROUP_ROWS), GROUP_ROWS)
-            unpack_group(swap_ref, arrived_ref, group * group_block, rows_of, to)
-            return carry
-
-        lax.fori_loop(0, groups, unpack, 0, unroll=4)
-
-    def product():
-        first = step * STEP_PIECES
-        rows = jnp.concatenate([rows_of[first + part] for part in range(STEP_PIECES)], 1)
-        return dot_f32(rows, in_ref[...])
-
-    @pl.when(step == 0)
-    def _():
-        gate_up[...] = product()
-
-    @pl.when((step > 0) & (step < half))
-    def _():
-        gate_up[...] += product()
-
-    @pl.when(step == half - 1)
-    def _():
-        active[...] = (jax.nn.silu(gate_up[:, :FF]) * gate_up[:, FF:]).astype(jnp.bfloat16)
-
-    @pl.when(step >= half)
-    def _():
-        first = (step - half) * STEP_PIECES
-        for part in range(STEP_PIECES):
-            rows_of[first + part] = dot_f32(
-                active[...], down_ref[:, part * PIECE : (part + 1) * PIECE]
+    steps = PIECES // STEP_PIECES
+    width = STEP_PIECES * PIECE
+
+    def columns(step):
+        return slice(step * width, (step + 1) * width)
+
+    weights_in = [
+        pltpu.make_async_copy(in_hbm.at[columns(step), :], in_ref.at[columns(step), :], landed.at[0, step])
+        for step in range(steps)
+    ]
+    weights_down = [
+        pltpu.make_async_copy(
+            down_hbm.at[:, columns(step)], down_ref.at[:, columns(step)], landed.at[1, step]
+        )
+        for step in range(steps)
+    ]
+    for copy in weights_in + weights_down:
+        copy.start()
+
+    def unpack(group, carry):
+        to = pl.ds(pl.multiple_of(group * GROUP_ROWS, GROUP_ROWS), GROUP_ROWS)
+        unpack_group(swap_ref, arrived_ref, group * group_block, rows_of, to)
+        return carry
+
+    lax.fori_loop(0, groups, unpack, 0, unroll=4)
+    for step in range(steps):
+        weights_in[step].wait()
+        pieces = range(step * STEP_PIECES, (step + 1) * STEP_PIECES)
+        rows = jnp.concatenate([rows_of[piece] for piece in pieces], 1)
+        part = dot_f32(rows, in_ref[columns(step), :])
+        if step == 0:
+            gate_up[...] = part
+        else:
+            gate_up[...] += part
+    active[...] = (jax.nn.silu(gate_up[:, :FF]) * gate_up[:, FF:]).astype(jnp.bfloat16)
+    for step in range(steps):
+        weights_down[step].wait()
+        for piece in range(step * STEP_PIECES, (step + 1) * STEP_PIECES):
+            rows_of[piece] = dot_f32(
+                active[...], down_ref[:, piece * PIECE : (piece + 1) * PIECE]
             ).astype(jnp.bfloat16)
 
-    @pl.when(step == 2 * half - 1)
-    def _():
-        def pack(group, carry):
-            at = pl.ds(pl.multiple_of(group * GROUP_ROWS, GROUP_ROWS), GROUP_ROWS)
-            pack_group(swap_ref, rows_of, at, out_ref, group * group_block)
-            return carry
-
-        lax.fori_loop(0, groups, pack, 0, unroll=4)
+    def pack(group, carry):
+        at = pl.ds(pl.multiple_of(group * GROUP_ROWS, GROUP_ROWS), GROUP_ROWS)
+        pack_group(swap_ref, rows_of, at, out_ref, group * group_block)
+        return carry
+
+    lax.fori_loop(0, groups, pack, 0, unroll=4)
 
 
 def run_expert(arrived, swap, w_in, w_out):
     slots = arrived.shape[0] // PIECES
-    group_block = GROUP_ROWS * PIECES
-    half = PIECES // STEP_PIECES
-    width = STEP_PIECES * PIECE
+    any_spec = pl.BlockSpec(memory_space=pl.ANY)
     return pl.pallas_call(
         expert_kernel,
-        grid=(2 * half,),
         out_shape=jax.ShapeDtypeStruct(arrived.shape, jnp.bfloat16),
-        in_specs=[
-            pl.BlockSpec(arrived.shape, lambda step: (0, 0), pipeline_mode=pl.Buffered(1)),
-            pl.BlockSpec(swap.shape, lambda step: (0, 0, 0)),
-            pl.BlockSpec((width, 2 * FF), lambda step: (jnp.minimum(step, half - 1), 0)),
-            pl.BlockSpec((FF, width), lambda step: (0, jnp.maximum(step - half, 0))),
-        ],
-        out_specs=pl.BlockSpec(arrived.shape, lambda step: (0, 0), pipeline_mode=pl.Buffered(1)),
+        in_specs=[VMEM_SPEC, VMEM_SPEC, any_spec, any_spec],
+        out_specs=VMEM_SPEC,
         scratch_shapes=[
+            pltpu.VMEM(w_in.shape, jnp.bfloat16),
+            pltpu.VMEM(w_out.shape, jnp.bfloat16),
+            pltpu.SemaphoreType.DMA((2, PIECES // STEP_PIECES)),
             pltpu.VMEM((PIECES, slots, PIECE), jnp.bfloat16),
             pltpu.VMEM((slots, 2 * FF), jnp.float32),
             pltpu.VMEM((slots, FF), jnp.bfloat16),
         ],
-        compiler_params=pltpu.CompilerParams(vmem_limit_bytes=VMEM_BYTES),
+        compiler_params=pltpu.CompilerParams(vmem_limit_bytes=EXPERT_VMEM),
         name="expert",
     )(arrived, swap, w_in, w_out)
 
@@ -415,28 +442,26 @@
 
     opposite = [(i, ctx_count - 1 - i) for i in range(ctx_count)]
     swapped = lax.ppermute(queries[half:], "ctx", opposite)
+    parity = lax.axis_index("tp") % 2
+    column = kv_index * HEAD_DIM
     own_kv = jnp.concatenate(
         [
-            lax.dynamic_slice_in_dim(keys, kv_index * HEAD_DIM, HEAD_DIM, 1),
-            lax.dynamic_slice_in_dim(values, kv_index * HEAD_DIM, HEAD_DIM, 1),
+            lax.dynamic_slice(full, (parity * half, column), (half, HEAD_DIM))
+            for full in (keys, values)
         ],
         1,
     )
-    all_kv = lax.all_gather(own_kv, "ctx", axis=0, tiled=True)
+    mine = lax.all_gather(own_kv, "ctx", axis=0, tiled=True)
+    swapped, mine = lax.optimization_barrier((swapped, mine))
+    other = lax.ppermute(mine, "tp", [(i, i ^ 1) for i in range(lax.axis_size("tp"))])
     full_proj = lax.all_gather(out_proj, "ctx", axis=1, tiled=True)
-    blocks = jnp.stack([2 * ctx_count - 1 - 2 * ctx_index, 2 * ctx_index]).astype(jnp.int32)
-    nears, returned = [], []
-    for first in range(0, heads_here, PAIR_HEADS):
-        pair = slice(first * HEAD_DIM, (first + PAIR_HEADS) * HEAD_DIM)
-        far, near = attend(blocks, swapped[:, pair], queries[:half, pair], all_kv)
-        nears.append(near)
-        returned.append(lax.ppermute(far, "ctx", opposite))
-    attended = jnp.concatenate(
-        [jnp.concatenate(nears, 1), jnp.concatenate(returned, 1)], 0
-    )
-    attn_out = lax.psum_scatter(
-        dot_f32(attended, full_proj).astype(jnp.bfloat16), "tp", scatter_dimension=0, tiled=True
-    )
+    place = jnp.stack(
+        [2 * ctx_count - 1 - 2 * ctx_index, 2 * ctx_index, parity]
+    ).astype(jnp.int32)
+    far, near = attend(place, swapped, queries[:half], mine, other)
+    returned = lax.ppermute(far, "ctx", opposite)
+    projected = project(returned, full_proj, 1, project(near, full_proj, 0))
+    attn_out = lax.psum_scatter(projected, "tp", scatter_dimension=0, tiled=True)
 
     hidden, packed = dispatch(
         target.T, attn_out, residual, norm_gain.reshape(1, -1), swap, dev_count

time: 523 us -> 437 us (0.84)
  Pallas kernels: 183 us -> 116 us
  waiting for transfers between devices: 199 us -> 187 us
  matrix products: 11.6 us -> 0 us
  local copies, waits for them, and re-layouts: 8.45 us -> 16.1 us
    pallas_call x2 -> x1, Pallas kernels: 139 us -> 69.2 us  [attend(): pl.pallas_call(attend_kernel, out_shape=(result, result), in_specs=[SMEM_...]
    all_gather x1, waiting for transfers between devices: 51.1 us -> 34.5 us  [body(): mine = lax.all_gather(own_kv, 'ctx', axis=0, tiled=True)]
    dot_general x1 -> x0, matrix products: 11.6 us -> none  [dot_f32(): return jnp.dot(left, right, preferred_element_type=jnp.float32)]
    ppermute x2, waiting for transfers between devices: 8.74 us -> 16.2 us  [the longest x1 8.78 us: body(): returned = lax.ppermute(far, 'ctx', opposite)]
    unnamed x15 -> x19, local copies, waits for them, and re-layouts: 4.92 us -> 11.7 us
    pallas_call x1 -> x3, Pallas kernels: 28.1 us -> 30.3 us  [the longest x1 23.5 us: run_expert(): pl.pallas_call(expert_kernel, out_shape=jax.ShapeDtypeStruct(arrived.shap...]
  transfers between devices with their start and end apart: 7 -> 7, of which waited for: 5 -> 6; matrix products, arithmetic and copies ran while one was open for 1% -> 1% of each run, Pallas kernels for 27% -> 17%
where the time goes in v3:
time: 437 us; the launch traced here: 434 us
  waiting for transfers between devices  187 us (43%)
  Pallas kernels  116 us (27%)
  blocking collectives  83.5 us (19%)
  starting transfers between devices  17 us (4%)
  local copies, waits for them, and re-layouts  16.1 us (4%)
  between operations  13.2 us (3%)
    all_to_all x1, blocking collectives, exchange(): lax.all_to_all(shaped, ('ctx', 'tp'), split_axis=0, concat_axis=0, tiled=...  83.5 us
    all_to_all x1, waiting for transfers between devices, exchange(): lax.all_to_all(shaped, ('ctx', 'tp'), split_axis=0, concat_axis=0, tiled=...  75 us
    pallas_call x1, Pallas kernels, attend(): pl.pallas_call(attend_kernel, out_shape=(result, result), in_specs=[SMEM_...  69.2 us
    reduce_scatter x1, waiting for transfers between devices, body(): lax.psum_scatter(projected, 'tp', scatter_dimension=0, tiled=True)  46.7 us
    all_gather x1, waiting for transfers between devices, body(): mine = lax.all_gather(own_kv, 'ctx', axis=0, tiled=True)  34.5 us
    pallas_call x1, Pallas kernels, run_expert(): pl.pallas_call(expert_kernel, out_shape=jax.ShapeDtypeStruct(arrived.shap...  23.5 us
    ppermute x1, waiting for transfers between devices, body(): swapped = lax.ppermute(queries[half:], 'ctx', opposite)  14 us
    unnamed x19, local copies, waits for them, and re-layouts  11.7 us
  transfers between devices with their start and end apart: 7, of which 6 were waited for; matrix products, arithmetic and copies ran while one was open for 1% of the time, Pallas kernels for 17%

profile of v3, /device:TPU:6, one launch (start us, length us, event | category | flops | bytes accessed | tf_op | source)
XLA Modules:
  0.0 434.0 jit_solution(1387353351132798974)
XLA Ops:
  6.5 0.0 all-gather.3.cloned.1.call-start
  6.5 0.9 dynamic_slice.6
  7.5 0.9 dynamic_slice.7
  8.4 0.7 pad_maximum_fusion
  9.1 0.0 all-gather.3.cloned.1.call-update
  9.1 0.0 all-gather.5.cloned.1.call-start
  9.2 0.7 all-gather.5.cloned.1.call-update
  9.9 0.0 reduce-scatter.2.cloned.1.call-start
  9.9 1.3 fusion.5
  11.2 6.6 %collective-permute-start = (bf16[512,512]{1,0:T(8,128)(2,1)S(1)}, bf16[512,512]{1,0:T(8,128)(2,1)S(1)}, u32[]{:S(2)}, u32[]{:S(2)}) collective-permute-start(bf16[512,512]{1,0:T(8,128)(2,1)S(1)} %get-tuple-element.18), channel_id=1, source_target_pairs={{0,120},{8,112},{16,104},{24,96},{32,88},{40,80},{48,72},{56,64},{... | collective-permute-start | bytes 1572872 | tf_op jit(solution)/shard_map/ppermute | solution.py:444
  17.8 14.0 %collective-permute-done.far_ref = bf16[512,512]{1,0:T(8,128)(2,1)S(1)} collective-permute-done((bf16[512,512]{1,0:T(8,128)(2,1)S(1)}, bf16[512,512]{1,0:T(8,128)(2,1)S(1)}, u32[]{:S(2)}, u32[]{:S(2)}) %collective-permute-start) | collective-permute-done | bytes 524320 | tf_op jit(solution)/shard_map/ppermute | solution.py:444
  31.7 34.5 %all-gather.3.cloned.1.call-done.mine_ref = bf16[8192,256]{1,0:T(8,128)(2,1)} async-done(((bf16[512,256]{1,0:T(8,128)(2,1)}), bf16[8192,256]{1,0:T(8,128)(2,1)}) %all-gather.3.cloned.1.call-update) | async-done | bytes 4194320 | tf_op jit(solution)/shard_map/all_gather | solution.py:454
  66.2 0.0 collective-permute-start.1
  66.2 0.1 pad_add_fusion.place_ref
  66.3 7.4 %collective-permute-done.1.other_ref = bf16[8192,256]{1,0:T(8,128)(2,1)} collective-permute-done((bf16[8192,256]{1,0:T(8,128)(2,1)}, bf16[8192,256]{1,0:T(8,128)(2,1)}, u32[]{:S(2)}, u32[]{:S(2)}) %collective-permute-start.1) | collective-permute-done | bytes 4194336 | tf_op jit(solution)/shard_map/ppermute | solution.py:456
  73.7 2.2 copy-done.3
  75.9 69.2 %attend.1 = (bf16[512,512]{1,0:T(8,128)(2,1)S(1)}, bf16[512,512]{1,0:T(8,128)(2,1)S(1)}) custom-call(s32[3]{0:T(128)S(1)} %pad_add_fusion.place_ref, bf16[512,512]{1,0:T(8,128)(2,1)S(1)} %collective-permute-done.far_ref, bf16[512,512]{1,0:T(8,128)(2,1)S(1)} %get-tuple-element.17.near_ref, bf16[8192,256]{1,0:T(8,128)(2,1)S(1)} %copy-done.3, ...), custom_call_target="tpu_custom_call" | custom-call | tf_op jit(solution)/shard_map/attend/pallas_call | solution.py:186
  145.1 3.0 collective-permute-start.2
  148.1 2.2 copy-done.2
  150.3 3.4 project.2.rest_0_
  153.7 8.8 %collective-permute-done.2.attended_ref = bf16[512,512]{1,0:T(8,128)(2,1)S(1)} collective-permute-done((bf16[512,512]{1,0:T(8,128)(2,1)S(1)}, bf16[512,512]{1,0:T(8,128)(2,1)S(1)}, u32[]{:S(2)}, u32[]{:S(2)}) %collective-permute-start.2) | collective-permute-done | bytes 524320 | tf_op jit(solution)/shard_map/ppermute | solution.py:462
  162.5 3.4 project.3
  165.9 0.0 copy-start
  165.9 3.2 copy-done
  169.1 0.0 reduce-scatter.2.cloned.1.call-update
  169.1 0.7 copy-done.6
  169.8 0.1 copy.25
  169.9 0.1 eq.31
  170.0 0.1 eq.27
  170.1 0.1 copy.27
  170.2 0.2 fusion.2
  170.6 0.2 fusion.1
  170.8 0.1 reduce_sum.12
  170.9 0.1 copy.29
  171.0 0.0 copy-start.5
  171.1 0.7 copy.30.target_ref
  171.7 46.7 %reduce-scatter.2.cloned.1.call-done.attn_ref = bf16[128,4096]{1,0:T(8,128)(2,1)} async-done(((bf16[1024,4096]{1,0:T(8,128)(2,1)}), bf16[128,4096]{1,0:T(8,128)(2,1)}) %reduce-scatter.2.cloned.1.call-update) | async-done | bytes 1048592 | tf_op jit(solution)/shard_map/reduce_scatter | solution.py:464
  218.4 8.1 %norm_and_dispatch.1 = (bf16[128,4096]{1,0:T(8,128)(2,1)}, bf16[6144,512]{1,0:T(8,128)(2,1)}) custom-call(s32[4,128]{1,0:T(4,128)} %copy.30.target_ref, bf16[128,4096]{1,0:T(8,128)(2,1)} %reduce-scatter.2.cloned.1.call-done.attn_ref, bf16[128,4096]{1,0:T(8,128)(2,1)} %residual_ref.1, f32[1,4096]{1,0:T(1,128)} %bitcast.32, ...), custom_call_target="tpu_custom_call" | custom-call | tf_op jit(solution)/shard_map/norm_and_dispatch/pallas_call | solution.py:269
  226.5 83.5 %all_to_all.10 = bf16[128,48,512]{2,1,0:T(8,128)(2,1)} all-to-all(bf16[128,48,512]{2,1,0:T(8,128)(2,1)} %bitcast.27), channel_id=1, replica_groups=mesh['ctx'=16,'tp'=8] {'ctx','tp'}, dimensions={0} | all-to-all | bytes 12582912 | tf_op jit(solution)/shard_map/all_to_all | solution.py:472
  310.0 0.0 copy-done.5
  310.0 0.0 copy-done.4
  310.0 23.5 %expert.1 = bf16[6144,512]{1,0:T(8,128)(2,1)S(1)} custom-call(bf16[6144,512]{1,0:T(8,128)(2,1)} %bitcast.25, bf16[2,192,192]{2,1,0:T(8,128)(2,1)S(1)} %copy-done.4, bf16[4096,1536]{1,0:T(8,128)(2,1)} %bitcast.26, bf16[768,4096]{1,0:T(8,128)(2,1)} %bitcast.28), custom_call_target="tpu_custom_call" | custom-call | tf_op jit(solution)/shard_map/expert/pallas_call | solution.py:351
  333.6 0.0 copy-start.1
  333.6 2.6 copy-done.1
  336.2 7.3 %all-to-all-start.1 = ((bf16[128,48,512]{2,1,0:T(8,128)(2,1)}), bf16[128,48,512]{2,1,0:T(8,128)(2,1)}, u32[]{:S(2)}, u32[]{:S(2)}) async-start(bf16[128,48,512]{2,1,0:T(8,128)(2,1)} %bitcast.24), calls=%async_computation.2 | async-start | bytes 12582912 | tf_op jit(solution)/shard_map/all_to_all | solution.py:472
  343.6 0.7 copy.31.route_ref
  344.3 75.0 %all-to-all-done.1 = bf16[128,48,512]{2,1,0:T(8,128)(2,1)} async-done(((bf16[128,48,512]{2,1,0:T(8,128)(2,1)}), bf16[128,48,512]{2,1,0:T(8,128)(2,1)}, u32[]{:S(2)}, u32[]{:S(2)}) %all-to-all-start.1) | async-done | bytes 6291488 | tf_op jit(solution)/shard_map/all_to_all | solution.py:472
  419.3 8.2 %combine.1 = bf16[128,4096]{1,0:T(8,128)(2,1)} custom-call(s32[128,4]{1,0:T(8,128)} %copy-done.5, f32[128,4]{1,0:T(8,128)} %copy.31.route_ref, bf16[128,4096]{1,0:T(8,128)(2,1)} %get-tuple-element.15.hidden_ref, bf16[2,192,192]{2,1,0:T(8,128)(2,1)} %constant.56.clone.swap_ref, bf16[6144,512]{1,0:T(8,128)(2,1)} %bitcast.13.back_ref), custom_call_target="tpu_custom_call" | custom-call | tf_op jit(solution)/shard_map/combine/pallas_call | solution.py:407
  (15 shorter events, 0.1 us)
Async XLA Ops:
  6.5 59.7 %all-gather.3.cloned.1.call-start = ((), (), s32[]{:S(2)}) async-start(), calls=%async_computation.3 | async-start | bytes 4456448 | tf_op jit(solution)/shard_map/all_gather | solution.py:454
  9.1 139.0 %all-gather.5.cloned.1.call-start = ((), (), s32[]{:S(2)}) async-start(), calls=%async_computation.4 | async-start | bytes 4456448 | tf_op jit(solution)/shard_map/all_gather | solution.py:457
  9.9 208.6 %reduce-scatter.2.cloned.1.call-start = ((), (), s32[]{:S(2)}) async-start(), calls=%async_computation.5 | async-start | bytes 9437184 | tf_op jit(solution)/shard_map/reduce_scatter | solution.py:464
  11.2 20.5 %collective-permute-start = (bf16[512,512]{1,0:T(8,128)(2,1)S(1)}, bf16[512,512]{1,0:T(8,128)(2,1)S(1)}, u32[]{:S(2)}, u32[]{:S(2)}) collective-permute-start(bf16[512,512]{1,0:T(8,128)(2,1)S(1)} %get-tuple-element.18), channel_id=1, source_target_pairs={{0,120},{8,112},{16,104},{24,96},{32,88},{40,80},{48,72},{56,64},{... | collective-permute-start | bytes 1572872 | tf_op jit(solution)/shard_map/ppermute | solution.py:444
  66.2 7.5 %collective-permute-start.1 = (bf16[8192,256]{1,0:T(8,128)(2,1)}, bf16[8192,256]{1,0:T(8,128)(2,1)}, u32[]{:S(2)}, u32[]{:S(2)}) collective-permute-start(bf16[8192,256]{1,0:T(8,128)(2,1)} %all-gather.3.cloned.1.call-done.mine_ref), channel_id=1, source_target_pairs={{0,1},{1,0},{2,3},{3,2},{4,5},{5,4},{6,7},{7,6},{8,9},{9,8},{10,11... | collective-permute-start | bytes 12582920 | tf_op jit(solution)/shard_map/ppermute | solution.py:456
  73.7 2.2 copy-start.3
  145.1 17.4 %collective-permute-start.2 = (bf16[512,512]{1,0:T(8,128)(2,1)S(1)}, bf16[512,512]{1,0:T(8,128)(2,1)S(1)}, u32[]{:S(2)}, u32[]{:S(2)}) collective-permute-start(bf16[512,512]{1,0:T(8,128)(2,1)S(1)} %get-tuple-element.13), channel_id=1, source_target_pairs={{0,120},{8,112},{16,104},{24,96},{32,88},{40,80},{48,72},{56,64},{... | collective-permute-start | bytes 1572872 | tf_op jit(solution)/shard_map/ppermute | solution.py:462
  148.1 2.2 copy-start.2
  165.9 3.2 copy-start
  169.1 0.7 copy-start.6
  171.0 139.0 %copy-start.5 = (s32[128,4]{1,0:T(8,128)}, s32[128,4]{1,0:T(8,128)S(1)}, u32[]{:S(2)}) copy-start(s32[128,4]{1,0:T(8,128)S(1)} %add.19.target_ref) | copy-start | bytes 6148
  226.5 83.5 %copy-start.4 = (bf16[2,192,192]{2,1,0:T(8,128)(2,1)S(1)}, bf16[2,192,192]{2,1,0:T(8,128)(2,1)}, u32[]{:S(2)}) copy-start(bf16[2,192,192]{2,1,0:T(8,128)(2,1)} %constant.56.clone.swap_ref) | copy-start | bytes 442372
  333.6 2.6 copy-start.1
  336.2 7.3 %copy-start.7 = (f32[128,4]{0,1:T(4,128)S(1)}, f32[128,4]{0,1:T(4,128)}, u32[]{:S(2)}) copy-start(f32[128,4]{0,1:T(4,128)} %param.18) | copy-start | bytes 6148
  336.2 83.1 %all-to-all-start.1 = ((bf16[128,48,512]{2,1,0:T(8,128)(2,1)}), bf16[128,48,512]{2,1,0:T(8,128)(2,1)}, u32[]{:S(2)}, u32[]{:S(2)}) async-start(bf16[128,48,512]{2,1,0:T(8,128)(2,1)} %bitcast.24), calls=%async_computation.2 | async-start | bytes 12582912 | tf_op jit(solution)/shard_map/all_to_all | solution.py:472
Sparse Core Ops, SparseCore 0:
  9.5 56.6 all-gather.2
  68.3 57.4 all-gather.4
  169.3 49.1 reduce-scatter.1

commit v4 on v3

--- a/solution.py
+++ b/solution.py
@@ -26,9 +26,10 @@
 GROUP_ROWS = GROUP * CAP
 STEP_GROUPS = 4
 STEP_PIECES = 2
+PROJECT_WIDTH = 2048
 VMEM_BYTES = 56 * 2**20
 EXPERT_VMEM = 46 * 2**20
-ATTEND_VMEM = 44 * 2**20
+ATTEND_VMEM = 36 * 2**20
 
 VMEM_SPEC = pl.BlockSpec(memory_space=pltpu.VMEM)
 SMEM_SPEC = pl.BlockSpec(memory_space=pltpu.SMEM)
@@ -78,6 +79,26 @@
     return lax.dot_general(
         left, keys, (((1,), (1,)), ((), ())), preferred_element_type=jnp.float32
     )
+
+
+def own_half_kernel(place_ref, keys_ref, values_ref, out_ref):
+    out_ref[:, :HEAD_DIM] = keys_ref[...]
+    out_ref[:, HEAD_DIM:] = values_ref[...]
+
+
+def own_half(place, keys, values, half):
+    taken = pl.BlockSpec((half, HEAD_DIM), lambda step, place_ref: (place_ref[2], place_ref[3]))
+    return pl.pallas_call(
+        own_half_kernel,
+        grid_spec=pltpu.PrefetchScalarGridSpec(
+            num_scalar_prefetch=1,
+            grid=(1,),
+            in_specs=[taken, taken],
+            out_specs=pl.BlockSpec((half, 2 * HEAD_DIM), lambda step, place_ref: (0, 0)),
+        ),
+        out_shape=jax.ShapeDtypeStruct((half, 2 * HEAD_DIM), jnp.bfloat16),
+        name="own_half",
+    )(place, keys, values)
 
 
 def attend_part(block, shift, parity, q_ref, mine_ref, other_ref, out_ref, q_wide, top, acc):
@@ -199,31 +220,34 @@
 
 
 def project_kernel(attended_ref, proj_ref, *rest):
-    rest[-1][...] = dot_f32(attended_ref[...], proj_ref[...]).astype(jnp.bfloat16)
+    out_ref = rest[-1]
+    proj = jnp.concatenate([proj_ref[part] for part in range(proj_ref.shape[0])], 1)
+    out_ref[...] = dot_f32(attended_ref[...], proj).astype(jnp.bfloat16)
 
 
 def project(attended, proj, half, so_far=None):
     rows, depth = attended.shape
-    model = proj.shape[1]
-    width = 2 * PIECE
+    parts, _, width = proj.shape
+    model = parts * width
+    taken = PROJECT_WIDTH // width
     operands = (attended, proj) if so_far is None else (attended, proj, so_far)
     return pl.pallas_call(
         project_kernel,
-        grid=(model // width,),
+        grid=(parts // taken,),
         out_shape=jax.ShapeDtypeStruct((2 * rows, model), jnp.bfloat16),
         in_specs=[
             pl.BlockSpec((rows, depth), lambda step: (0, 0)),
-            pl.BlockSpec((depth, width), lambda step: (0, step)),
+            pl.BlockSpec((taken, depth, width), lambda step: (step, 0, 0)),
             pl.BlockSpec(memory_space=pl.ANY),
         ][: len(operands)],
-        out_specs=pl.BlockSpec((rows, width), lambda step: (half, step)),
+        out_specs=pl.BlockSpec((rows, taken * width), lambda step: (half, step)),
         input_output_aliases={} if so_far is None else {2: 0},
         cost_estimate=pl.CostEstimate(
             flops=2 * rows * depth * model,
             bytes_accessed=2 * (rows * depth + depth * model + rows * model),
             transcendentals=0,
         ),
-        compiler_params=pltpu.CompilerParams(vmem_limit_bytes=VMEM_BYTES // 2),
+        compiler_params=pltpu.CompilerParams(vmem_limit_bytes=VMEM_BYTES),
         name="project",
     )(*operands)
 
@@ -443,21 +467,13 @@
     opposite = [(i, ctx_count - 1 - i) for i in range(ctx_count)]
     swapped = lax.ppermute(queries[half:], "ctx", opposite)
     parity = lax.axis_index("tp") % 2
-    column = kv_index * HEAD_DIM
-    own_kv = jnp.concatenate(
-        [
-            lax.dynamic_slice(full, (parity * half, column), (half, HEAD_DIM))
-            for full in (keys, values)
-        ],
-        1,
-    )
-    mine = lax.all_gather(own_kv, "ctx", axis=0, tiled=True)
+    place = jnp.stack(
+        [2 * ctx_count - 1 - 2 * ctx_index, 2 * ctx_index, parity, kv_index]
+    ).astype(jnp.int32)
+    mine = lax.all_gather(own_half(place, keys, values, half), "ctx", axis=0, tiled=True)
     swapped, mine = lax.optimization_barrier((swapped, mine))
     other = lax.ppermute(mine, "tp", [(i, i ^ 1) for i in range(lax.axis_size("tp"))])
-    full_proj = lax.all_gather(out_proj, "ctx", axis=1, tiled=True)
-    place = jnp.stack(
-        [2 * ctx_count - 1 - 2 * ctx_index, 2 * ctx_index, parity]
-    ).astype(jnp.int32)
+    full_proj = lax.all_gather(out_proj, "ctx", axis=0, tiled=False)
     far, near = attend(place, swapped, queries[:half], mine, other)
     returned = lax.ppermute(far, "ctx", opposite)
     projected = project(returned, full_proj, 1, project(near, full_proj, 0))

time: 437 us -> 437 us (level)
  local copies, waits for them, and re-layouts: 16.1 us -> 11 us
  Pallas kernels: 116 us -> 121 us
    pallas_call x2 -> x3, Pallas kernels: 6.8 us -> 13.7 us  [the longest x2 11.3 us: project(): pl.pallas_call(project_kernel, grid=(parts // taken,), out_shape=jax.Shap...]
    unnamed x19 -> x21, local copies, waits for them, and re-layouts: 11.7 us -> 8.5 us
where the time goes in v4:
time: 437 us; the launch traced here: 433 us
  waiting for transfers between devices  187 us (43%)
  Pallas kernels  121 us (28%)
  blocking collectives  83.5 us (19%)
  starting transfers between devices  17 us (4%)
  between operations  13.2 us (3%)
  local copies, waits for them, and re-layouts  11 us (3%)
    all_to_all x1, blocking collectives, exchange(): lax.all_to_all(shaped, ('ctx', 'tp'), split_axis=0, concat_axis=0, tiled=...  83.5 us
    all_to_all x1, waiting for transfers between devices, exchange(): lax.all_to_all(shaped, ('ctx', 'tp'), split_axis=0, concat_axis=0, tiled=...  75 us
    pallas_call x1, Pallas kernels, attend(): pl.pallas_call(attend_kernel, out_shape=(result, result), in_specs=[SMEM_...  67.2 us
    reduce_scatter x1, waiting for transfers between devices, body(): lax.psum_scatter(projected, 'tp', scatter_dimension=0, tiled=True)  46.8 us
    all_gather x1, waiting for transfers between devices, body(): lax.all_gather(own_half(place, keys, values, half), 'ctx', axis=0, tiled=...  34.3 us
    pallas_call x1, Pallas kernels, run_expert(): pl.pallas_call(expert_kernel, out_shape=jax.ShapeDtypeStruct(arrived.shap...  23.5 us
    ppermute x1, waiting for transfers between devices, body(): swapped = lax.ppermute(queries[half:], 'ctx', opposite)  14.2 us
    pallas_call x2, Pallas kernels, project(): pl.pallas_call(project_kernel, grid=(parts // taken,), out_shape=jax.Shap...  11.3 us
  transfers between devices with their start and end apart: 7, of which 6 were waited for; matrix products, arithmetic and copies ran while one was open for 1% of the time, Pallas kernels for 17%

profile of v4, /device:TPU:6, one launch (start us, length us, event | category | flops | bytes accessed | tf_op | source)
XLA Modules:
  0.0 433.4 jit_solution(3470341765551604866)
XLA Ops:
  6.5 0.0 all-gather.4.cloned.1.call-start
  6.5 0.6 pad_add_fusion.place_ref
  7.1 2.4 own_half.1
  9.5 0.0 all-gather.4.cloned.1.call-update
  9.5 0.0 all-gather.6.cloned.1.call-start
  9.6 0.7 all-gather.6.cloned.1.call-update
  10.3 0.0 reduce-scatter.2.cloned.1.call-start
  10.3 1.3 fusion.5
  11.6 6.6 %collective-permute-start = (bf16[512,512]{1,0:T(8,128)(2,1)S(1)}, bf16[512,512]{1,0:T(8,128)(2,1)S(1)}, u32[]{:S(2)}, u32[]{:S(2)}) collective-permute-start(bf16[512,512]{1,0:T(8,128)(2,1)S(1)} %get-tuple-element.18), channel_id=1, source_target_pairs={{0,120},{8,112},{16,104},{24,96},{32,88},{40,80},{48,72},{56,64},{... | collective-permute-start | bytes 1572872 | tf_op jit(solution)/shard_map/ppermute | solution.py:468
  18.1 14.2 %collective-permute-done.far_ref = bf16[512,512]{1,0:T(8,128)(2,1)S(1)} collective-permute-done((bf16[512,512]{1,0:T(8,128)(2,1)S(1)}, bf16[512,512]{1,0:T(8,128)(2,1)S(1)}, u32[]{:S(2)}, u32[]{:S(2)}) %collective-permute-start) | collective-permute-done | bytes 524320 | tf_op jit(solution)/shard_map/ppermute | solution.py:468
  32.3 34.3 %all-gather.4.cloned.1.call-done.mine_ref = bf16[8192,256]{1,0:T(8,128)(2,1)} async-done(((bf16[512,256]{1,0:T(8,128)(2,1)}), bf16[8192,256]{1,0:T(8,128)(2,1)}) %all-gather.4.cloned.1.call-update) | async-done | bytes 4194320 | tf_op jit(solution)/shard_map/all_gather | solution.py:473
  66.6 0.0 collective-permute-start.1
  66.6 7.4 %collective-permute-done.1.other_ref = bf16[8192,256]{1,0:T(8,128)(2,1)S(1)} collective-permute-done((bf16[8192,256]{1,0:T(8,128)(2,1)}, bf16[8192,256]{1,0:T(8,128)(2,1)S(1)}, u32[]{:S(2)}, u32[]{:S(2)}) %collective-permute-start.1) | collective-permute-done | bytes 4194336 | tf_op jit(solution)/shard_map/ppermute | solution.py:475
  73.9 2.2 copy-done.1
  76.1 0.6 copy-done.4
  76.7 67.2 %attend.1 = (bf16[512,512]{1,0:T(8,128)(2,1)S(1)}, bf16[512,512]{1,0:T(8,128)(2,1)S(1)}) custom-call(s32[4]{0:T(128)S(1)} %copy-done.4, bf16[512,512]{1,0:T(8,128)(2,1)S(1)} %collective-permute-done.far_ref, bf16[512,512]{1,0:T(8,128)(2,1)S(1)} %get-tuple-element.17.near_ref, bf16[8192,256]{1,0:T(8,128)(2,1)S(1)} %copy-done.1, ...), custom_call_target="tpu_custom_call" | custom-call | tf_op jit(solution)/shard_map/attend/pallas_call | solution.py:207
  143.9 0.0 copy-start.3
  143.9 0.8 copy-done.3
  144.7 3.0 collective-permute-start.2
  147.7 5.6 %project.2.rest_0_ = bf16[1024,4096]{1,0:T(8,128)(2,1)} custom-call(bf16[512,512]{1,0:T(8,128)(2,1)} %copy-done.3, bf16[16,512,256]{2,1,0:T(8,128)(2,1)} %bitcast.28), custom_call_target="tpu_custom_call" | custom-call | flops 2147483648 | bytes 8912896 | tf_op jit(solution)/shard_map/project/pallas_call | solution.py:234
  153.3 8.7 %collective-permute-done.2.attended_ref = bf16[512,512]{1,0:T(8,128)(2,1)S(1)} collective-permute-done((bf16[512,512]{1,0:T(8,128)(2,1)S(1)}, bf16[512,512]{1,0:T(8,128)(2,1)S(1)}, u32[]{:S(2)}, u32[]{:S(2)}) %collective-permute-start.2) | collective-permute-done | bytes 524320 | tf_op jit(solution)/shard_map/ppermute | solution.py:478
  162.0 0.8 copy-done.6
  162.8 5.7 %project.3 = bf16[1024,4096]{1,0:T(8,128)(2,1)} custom-call(bf16[512,512]{1,0:T(8,128)(2,1)} %copy-done.6, bf16[16,512,256]{2,1,0:T(8,128)(2,1)} %bitcast.29, bf16[1024,4096]{1,0:T(8,128)(2,1)} %project.2.rest_0_), custom_call_target="tpu_custom_call", output_to_operand_aliasing={{}: (2, {})} | custom-call | flops 2147483648 | bytes 8912896 | tf_op jit(solution)/shard_map/project/pallas_call | solution.py:234
  168.5 0.0 reduce-scatter.2.cloned.1.call-update
  168.5 0.7 copy-done.7
  169.1 0.1 copy.25
  169.3 0.1 eq.31
  169.4 0.1 eq.27
  169.5 0.1 copy.27
  169.6 0.2 fusion.2
  169.9 0.2 fusion.1
  170.1 0.1 reduce_sum.12
  170.3 0.1 copy.29
  170.4 0.0 copy-start.5
  170.4 0.7 copy.30.target_ref
  171.1 46.8 %reduce-scatter.2.cloned.1.call-done.attn_ref = bf16[128,4096]{1,0:T(8,128)(2,1)} async-done(((bf16[1024,4096]{1,0:T(8,128)(2,1)}), bf16[128,4096]{1,0:T(8,128)(2,1)}) %reduce-scatter.2.cloned.1.call-update) | async-done | bytes 1048592 | tf_op jit(solution)/shard_map/reduce_scatter | solution.py:480
  217.9 8.1 %norm_and_dispatch.1 = (bf16[128,4096]{1,0:T(8,128)(2,1)}, bf16[6144,512]{1,0:T(8,128)(2,1)}) custom-call(s32[4,128]{1,0:T(4,128)} %copy.30.target_ref, bf16[128,4096]{1,0:T(8,128)(2,1)} %reduce-scatter.2.cloned.1.call-done.attn_ref, bf16[128,4096]{1,0:T(8,128)(2,1)} %residual_ref.1, f32[1,4096]{1,0:T(1,128)} %bitcast.36, ...), custom_call_target="tpu_custom_call" | custom-call | tf_op jit(solution)/shard_map/norm_and_dispatch/pallas_call | solution.py:293
  226.0 83.5 %all_to_all.10 = bf16[128,48,512]{2,1,0:T(8,128)(2,1)} all-to-all(bf16[128,48,512]{2,1,0:T(8,128)(2,1)} %bitcast.31), channel_id=1, replica_groups=mesh['ctx'=16,'tp'=8] {'ctx','tp'}, dimensions={0} | all-to-all | bytes 12582912 | tf_op jit(solution)/shard_map/all_to_all | solution.py:488
  309.5 0.0 copy-done.5
  309.5 0.0 copy-done.2
  309.5 23.5 %expert.1 = bf16[6144,512]{1,0:T(8,128)(2,1)S(1)} custom-call(bf16[6144,512]{1,0:T(8,128)(2,1)} %bitcast.27, bf16[2,192,192]{2,1,0:T(8,128)(2,1)S(1)} %copy-done.2, bf16[4096,1536]{1,0:T(8,128)(2,1)} %bitcast.30, bf16[768,4096]{1,0:T(8,128)(2,1)} %bitcast.32), custom_call_target="tpu_custom_call" | custom-call | tf_op jit(solution)/shard_map/expert/pallas_call | solution.py:375
  333.0 0.0 copy-start
  333.0 2.6 copy-done
  335.7 7.3 %all-to-all-start.1 = ((bf16[128,48,512]{2,1,0:T(8,128)(2,1)}), bf16[128,48,512]{2,1,0:T(8,128)(2,1)}, u32[]{:S(2)}, u32[]{:S(2)}) async-start(bf16[128,48,512]{2,1,0:T(8,128)(2,1)} %bitcast.26), calls=%async_computation.2 | async-start | bytes 12582912 | tf_op jit(solution)/shard_map/all_to_all | solution.py:488
  343.0 0.0 copy-done.8
  343.0 0.7 copy.31.route_ref
  343.7 75.0 %all-to-all-done.1 = bf16[128,48,512]{2,1,0:T(8,128)(2,1)} async-done(((bf16[128,48,512]{2,1,0:T(8,128)(2,1)}), bf16[128,48,512]{2,1,0:T(8,128)(2,1)}, u32[]{:S(2)}, u32[]{:S(2)}) %all-to-all-start.1) | async-done | bytes 6291488 | tf_op jit(solution)/shard_map/all_to_all | solution.py:488
  418.7 8.1 %combine.1 = bf16[128,4096]{1,0:T(8,128)(2,1)} custom-call(s32[128,4]{1,0:T(8,128)} %copy-done.5, f32[128,4]{1,0:T(8,128)} %copy.31.route_ref, bf16[128,4096]{1,0:T(8,128)(2,1)} %get-tuple-element.15.hidden_ref, bf16[2,192,192]{2,1,0:T(8,128)(2,1)} %constant.48.clone.swap_ref, bf16[6144,512]{1,0:T(8,128)(2,1)} %bitcast.15.back_ref), custom_call_target="tpu_custom_call" | custom-call | tf_op jit(solution)/shard_map/combine/pallas_call | solution.py:431
  (15 shorter events, 0.1 us)
Async XLA Ops:
  6.5 60.0 %all-gather.4.cloned.1.call-start = ((), (), s32[]{:S(2)}) async-start(), calls=%async_computation.3 | async-start | bytes 4456448 | tf_op jit(solution)/shard_map/all_gather | solution.py:473
  9.5 138.2 %all-gather.6.cloned.1.call-start = ((), (), s32[]{:S(2)}) async-start(), calls=%async_computation.5 | async-start | bytes 4456448 | tf_op jit(solution)/shard_map/all_gather | solution.py:476
  10.3 207.6 %reduce-scatter.2.cloned.1.call-start = ((), (), s32[]{:S(2)}) async-start(), calls=%async_computation.4 | async-start | bytes 9437184 | tf_op jit(solution)/shard_map/reduce_scatter | solution.py:480
  11.6 20.7 %collective-permute-start = (bf16[512,512]{1,0:T(8,128)(2,1)S(1)}, bf16[512,512]{1,0:T(8,128)(2,1)S(1)}, u32[]{:S(2)}, u32[]{:S(2)}) collective-permute-start(bf16[512,512]{1,0:T(8,128)(2,1)S(1)} %get-tuple-element.18), channel_id=1, source_target_pairs={{0,120},{8,112},{16,104},{24,96},{32,88},{40,80},{48,72},{56,64},{... | collective-permute-start | bytes 1572872 | tf_op jit(solution)/shard_map/ppermute | solution.py:468
  66.6 7.4 %collective-permute-start.1 = (bf16[8192,256]{1,0:T(8,128)(2,1)}, bf16[8192,256]{1,0:T(8,128)(2,1)S(1)}, u32[]{:S(2)}, u32[]{:S(2)}) collective-permute-start(bf16[8192,256]{1,0:T(8,128)(2,1)} %all-gather.4.cloned.1.call-done.mine_ref), channel_id=1, source_target_pairs={{0,1},{1,0},{2,3},{3,2},{4,5},{5,4},{6,7},{7,6},{8,9},{9,8},{10,11... | collective-permute-start | bytes 12582920 | tf_op jit(solution)/shard_map/ppermute | solution.py:475
  73.9 2.2 copy-start.1
  76.1 0.6 copy-start.4
  143.9 0.8 copy-start.3
  144.7 17.3 %collective-permute-start.2 = (bf16[512,512]{1,0:T(8,128)(2,1)S(1)}, bf16[512,512]{1,0:T(8,128)(2,1)S(1)}, u32[]{:S(2)}, u32[]{:S(2)}) collective-permute-start(bf16[512,512]{1,0:T(8,128)(2,1)S(1)} %get-tuple-element.13), channel_id=1, source_target_pairs={{0,120},{8,112},{16,104},{24,96},{32,88},{40,80},{48,72},{56,64},{... | collective-permute-start | bytes 1572872 | tf_op jit(solution)/shard_map/ppermute | solution.py:478
  162.0 0.8 copy-start.6
  168.5 0.7 copy-start.7
  170.4 139.1 %copy-start.5 = (s32[128,4]{1,0:T(8,128)}, s32[128,4]{1,0:T(8,128)S(1)}, u32[]{:S(2)}) copy-start(s32[128,4]{1,0:T(8,128)S(1)} %add.11.target_ref) | copy-start | bytes 6148
  226.0 83.5 %copy-start.2 = (bf16[2,192,192]{2,1,0:T(8,128)(2,1)S(1)}, bf16[2,192,192]{2,1,0:T(8,128)(2,1)}, u32[]{:S(2)}) copy-start(bf16[2,192,192]{2,1,0:T(8,128)(2,1)} %constant.48.clone.swap_ref) | copy-start | bytes 442372
  333.0 2.6 copy-start
  335.7 7.3 %copy-start.8 = (f32[128,4]{0,1:T(4,128)S(1)}, f32[128,4]{0,1:T(4,128)}, u32[]{:S(2)}) copy-start(f32[128,4]{0,1:T(4,128)} %param.18) | copy-start | bytes 6148
  335.7 83.1 %all-to-all-start.1 = ((bf16[128,48,512]{2,1,0:T(8,128)(2,1)}), bf16[128,48,512]{2,1,0:T(8,128)(2,1)}, u32[]{:S(2)}, u32[]{:S(2)}) async-start(bf16[128,48,512]{2,1,0:T(8,128)(2,1)} %bitcast.26), calls=%async_computation.2 | async-start | bytes 12582912 | tf_op jit(solution)/shard_map/all_to_all | solution.py:488
Sparse Core Ops, SparseCore 0:
  9.6 56.9 all-gather.3
  68.7 51.2 all-gather.5
  168.6 49.2 reduce-scatter.1

commit v5 on v4

--- a/solution.py
+++ b/solution.py
@@ -26,7 +26,7 @@
 GROUP_ROWS = GROUP * CAP
 STEP_GROUPS = 4
 STEP_PIECES = 2
-PROJECT_WIDTH = 2048
+PROJECT_WIDTH = 1024
 VMEM_BYTES = 56 * 2**20
 EXPERT_VMEM = 46 * 2**20
 ATTEND_VMEM = 36 * 2**20
@@ -60,13 +60,14 @@
         ).astype(jnp.bfloat16)
 
 
-def pack_group(swap_ref, rows_of, at, message_ref, first):
+def pack_group(swap_ref, rows_of, at, message_ref, first, second=None):
     size = swap_ref.shape[1]
     part = size // PIECES
     pieces = [rows_of[piece, at, :].astype(jnp.float32) for piece in range(PIECES)]
     for half in range(2):
         stacked = jnp.concatenate([rows[half * part : (half + 1) * part] for rows in pieces], 0)
-        message_ref[pl.ds(pl.multiple_of(first + half * size, size), size), :] = dot_f32(
+        to = first + half * size if second is None or half == 0 else second
+        message_ref[pl.ds(pl.multiple_of(to, size), size), :] = dot_f32(
             swap_ref[1], stacked.astype(jnp.bfloat16)
         ).astype(jnp.bfloat16)
 
@@ -193,8 +194,9 @@
         out_ref[:, head * HEAD_DIM : (head + 1) * HEAD_DIM] = mean.T.astype(jnp.bfloat16)
 
 
-def attend_kernel(place_ref, far_ref, near_ref, mine_ref, other_ref, far_out, near_out, *scratch):
+def attend_kernel(place_ref, far_ref, near_ref, mine_ref, other_ref, out_ref, *scratch):
     rows = near_ref.shape[0]
+    near_out, far_out = out_ref.at[pl.ds(0, rows), :], out_ref.at[pl.ds(rows, rows), :]
     parity = place_ref[2]
     attend_part(place_ref[0], rows, parity, far_ref, mine_ref, other_ref, far_out, *scratch)
     attend_part(place_ref[1], 0, parity, near_ref, mine_ref, other_ref, near_out, *scratch)
@@ -203,12 +205,11 @@
 def attend(place, far, near, mine, other):
     rows, columns = near.shape
     all_rows = rows * columns // HEAD_DIM
-    result = jax.ShapeDtypeStruct((rows, columns), jnp.bfloat16)
     return pl.pallas_call(
         attend_kernel,
-        out_shape=(result, result),
+        out_shape=jax.ShapeDtypeStruct((2 * rows, columns), jnp.bfloat16),
         in_specs=[SMEM_SPEC] + [VMEM_SPEC] * 4,
-        out_specs=(VMEM_SPEC, VMEM_SPEC),
+        out_specs=VMEM_SPEC,
         scratch_shapes=[
             pltpu.VMEM((all_rows, 2 * HEAD_DIM), jnp.bfloat16),
             pltpu.VMEM((8, all_rows), jnp.float32),
@@ -219,37 +220,27 @@
     )(place, far, near, mine, other)
 
 
-def project_kernel(attended_ref, proj_ref, *rest):
-    out_ref = rest[-1]
+def project_kernel(attended_ref, proj_ref, out_ref):
     proj = jnp.concatenate([proj_ref[part] for part in range(proj_ref.shape[0])], 1)
     out_ref[...] = dot_f32(attended_ref[...], proj).astype(jnp.bfloat16)
 
 
-def project(attended, proj, half, so_far=None):
+def project(attended, proj):
     rows, depth = attended.shape
     parts, _, width = proj.shape
-    model = parts * width
     taken = PROJECT_WIDTH // width
-    operands = (attended, proj) if so_far is None else (attended, proj, so_far)
     return pl.pallas_call(
         project_kernel,
         grid=(parts // taken,),
-        out_shape=jax.ShapeDtypeStruct((2 * rows, model), jnp.bfloat16),
+        out_shape=jax.ShapeDtypeStruct((rows, parts * width), jnp.bfloat16),
         in_specs=[
             pl.BlockSpec((rows, depth), lambda step: (0, 0)),
             pl.BlockSpec((taken, depth, width), lambda step: (step, 0, 0)),
-            pl.BlockSpec(memory_space=pl.ANY),
-        ][: len(operands)],
-        out_specs=pl.BlockSpec((rows, taken * width), lambda step: (half, step)),
-        input_output_aliases={} if so_far is None else {2: 0},
-        cost_estimate=pl.CostEstimate(
-            flops=2 * rows * depth * model,
-            bytes_accessed=2 * (rows * depth + depth * model + rows * model),
-            transcendentals=0,
-        ),
+        ],
+        out_specs=pl.BlockSpec((rows, taken * width), lambda step: (0, step)),
         compiler_params=pltpu.CompilerParams(vmem_limit_bytes=VMEM_BYTES),
         name="project",
-    )(*operands)
+    )(attended, proj)
 
 
 def dispatch_kernel(target_ref, attn_ref, residual_ref, gain_ref, swap_ref, hidden_ref, out_ref, rows_of):
@@ -363,7 +354,8 @@
 
     def pack(group, carry):
         at = pl.ds(pl.multiple_of(group * GROUP_ROWS, GROUP_ROWS), GROUP_ROWS)
-        pack_group(swap_ref, rows_of, at, out_ref, group * group_block)
+        second = (groups - 1 - group) * group_block + group_block // 2
+        pack_group(swap_ref, rows_of, at, out_ref, group * group_block, second)
         return carry
 
     lax.fori_loop(0, groups, pack, 0, unroll=4)
@@ -474,13 +466,22 @@
     swapped, mine = lax.optimization_barrier((swapped, mine))
     other = lax.ppermute(mine, "tp", [(i, i ^ 1) for i in range(lax.axis_size("tp"))])
     full_proj = lax.all_gather(out_proj, "ctx", axis=0, tiled=False)
-    far, near = attend(place, swapped, queries[:half], mine, other)
-    returned = lax.ppermute(far, "ctx", opposite)
-    projected = project(returned, full_proj, 1, project(near, full_proj, 0))
+    projected = project(attend(place, swapped, queries[:half], mine, other), full_proj)
     attn_out = lax.psum_scatter(projected, "tp", scatter_dimension=0, tiled=True)
 
+    tp_count = dev_count // ctx_count
+    home = [
+        (c * tp_count + t, (c if 2 * t < tp_count else ctx_count - 1 - c) * tp_count + t)
+        for c in range(ctx_count)
+        for t in range(tp_count)
+    ]
+
+    def trade(array):
+        return lax.ppermute(array, ("ctx", "tp"), home)
+
+    residual, projected = lax.optimization_barrier((residual, projected))
     hidden, packed = dispatch(
-        target.T, attn_out, residual, norm_gain.reshape(1, -1), swap, dev_count
+        trade(target).T, attn_out, trade(residual), norm_gain.reshape(1, -1), swap, dev_count
     )
 
     def exchange(rows):
@@ -489,8 +490,9 @@
             shaped, ("ctx", "tp"), split_axis=0, concat_axis=0, tiled=True
         ).reshape(rows.shape)
 
-    processed = run_expert(exchange(packed), swap, w_in[0], w_out[0])
-    return combine(target, route_weights, hidden, swap, exchange(processed))
+    hidden, arrived = lax.optimization_barrier((hidden, exchange(packed)))
+    processed = run_expert(arrived, swap, w_in[0], w_out[0])
+    return combine(target, route_weights, trade(hidden), swap, exchange(processed))
 
 
 def solution(mesh):

time: 437 us -> 444 us (1.016)
  starting transfers between devices: 17 us -> 30.8 us
    ppermute x1 -> x3, waiting for transfers between devices: 8.67 us -> 111 us  [trade(): return lax.ppermute(array, ('ctx', 'tp'), home)]
    all_to_all x1, waiting for transfers between devices: 75 us -> 0.01 us  [exchange(): lax.all_to_all(shaped, ('ctx', 'tp'), split_axis=0, concat_axis=0, tiled=...]
    reduce_scatter x1, waiting for transfers between devices: 46.8 us -> 16.6 us  [body(): lax.psum_scatter(projected, 'tp', scatter_dimension=0, tiled=True)]
    ppermute x1 -> x3, starting transfers between devices: 3.01 us -> 16.9 us  [trade(): return lax.ppermute(array, ('ctx', 'tp'), home)]
    pallas_call x2 -> x1, Pallas kernels: 11.3 us -> 8.75 us  [project(): pl.pallas_call(project_kernel, grid=(parts // taken,), out_shape=jax.Shap...]
    unnamed x21 -> x27, local copies, waits for them, and re-layouts: 8.5 us -> 9.05 us
  transfers between devices with their start and end apart: 7 -> 9, of which waited for: 6 -> 6; matrix products, arithmetic and copies ran while one was open for 1% -> 1% of each run, Pallas kernels for 17% -> 15%
where the time goes in v5:
time: 444 us; the launch traced here: 443 us
  waiting for transfers between devices  185 us (42%)
  Pallas kernels  118 us (27%)
  blocking collectives  83.5 us (19%)
  starting transfers between devices  30.8 us (7%)
  between operations  13.3 us (3%)
  local copies, waits for them, and re-layouts  11.5 us (3%)
    ppermute x3, waiting for transfers between devices, trade(): return lax.ppermute(array, ('ctx', 'tp'), home)  111 us
    all_to_all x1, blocking collectives, exchange(): lax.all_to_all(shaped, ('ctx', 'tp'), split_axis=0, concat_axis=0, tiled=...  83.5 us
    pallas_call x1, Pallas kernels, attend(): pl.pallas_call(attend_kernel, out_shape=jax.ShapeDtypeStruct((2 * rows, c...  67.2 us
    all_gather x1, waiting for transfers between devices, body(): lax.all_gather(own_half(place, keys, values, half), 'ctx', axis=0, tiled=...  34.3 us
    pallas_call x1, Pallas kernels, run_expert(): pl.pallas_call(expert_kernel, out_shape=jax.ShapeDtypeStruct(arrived.shap...  23.5 us
    ppermute x3, starting transfers between devices, trade(): return lax.ppermute(array, ('ctx', 'tp'), home)  16.9 us
    reduce_scatter x1, waiting for transfers between devices, body(): lax.psum_scatter(projected, 'tp', scatter_dimension=0, tiled=True)  16.6 us
    ppermute x1, waiting for transfers between devices, body(): swapped = lax.ppermute(queries[half:], 'ctx', opposite)  14.2 us
  transfers between devices with their start and end apart: 9, of which 6 were waited for; matrix products, arithmetic and copies ran while one was open for 1% of the time, Pallas kernels for 15%

profile of v5, /device:TPU:6, one launch (start us, length us, event | category | flops | bytes accessed | tf_op | source)
XLA Modules:
  0.0 443.0 jit_solution(38645530248495018)
XLA Ops:
  6.5 0.6 pad_add_fusion.place_ref
  7.1 2.4 own_half.1
  9.5 0.0 all-gather.4.cloned.1.call-update
  9.5 0.0 all-gather.6.cloned.1.call-start
  9.6 0.7 all-gather.6.cloned.1.call-update
  10.3 0.0 reduce-scatter.2.cloned.1.call-start
  10.3 1.3 fusion.5
  11.6 6.6 %collective-permute-start.1 = (bf16[512,512]{1,0:T(8,128)(2,1)S(1)}, bf16[512,512]{1,0:T(8,128)(2,1)S(1)}, u32[]{:S(2)}, u32[]{:S(2)}) collective-permute-start(bf16[512,512]{1,0:T(8,128)(2,1)S(1)} %get-tuple-element.20), channel_id=1, source_target_pairs={{0,120},{8,112},{16,104},{24,96},{32,88},{40,80},{48,72},{56,64},{... | collective-permute-start | bytes 1572872 | tf_op jit(solution)/shard_map/ppermute | solution.py:460
  18.2 14.2 %collective-permute-done.1.far_ref = bf16[512,512]{1,0:T(8,128)(2,1)S(1)} collective-permute-done((bf16[512,512]{1,0:T(8,128)(2,1)S(1)}, bf16[512,512]{1,0:T(8,128)(2,1)S(1)}, u32[]{:S(2)}, u32[]{:S(2)}) %collective-permute-start.1) | collective-permute-done | bytes 524320 | tf_op jit(solution)/shard_map/ppermute | solution.py:460
  32.4 34.3 %all-gather.4.cloned.1.call-done.mine_ref = bf16[8192,256]{1,0:T(8,128)(2,1)} async-done(((bf16[512,256]{1,0:T(8,128)(2,1)}), bf16[8192,256]{1,0:T(8,128)(2,1)}) %all-gather.4.cloned.1.call-update) | async-done | bytes 4194320 | tf_op jit(solution)/shard_map/all_gather | solution.py:465
  66.6 0.0 collective-permute-start.2
  66.6 7.4 %collective-permute-done.2.other_ref = bf16[8192,256]{1,0:T(8,128)(2,1)S(1)} collective-permute-done((bf16[8192,256]{1,0:T(8,128)(2,1)}, bf16[8192,256]{1,0:T(8,128)(2,1)S(1)}, u32[]{:S(2)}, u32[]{:S(2)}) %collective-permute-start.2) | collective-permute-done | bytes 4194336 | tf_op jit(solution)/shard_map/ppermute | solution.py:467
  74.0 2.2 copy-done.1
  76.2 0.6 copy-done.4
  76.8 67.2 %attend.1.attended_ref = bf16[1024,512]{1,0:T(8,128)(2,1)S(1)} custom-call(s32[4]{0:T(128)S(1)} %copy-done.4, bf16[512,512]{1,0:T(8,128)(2,1)S(1)} %collective-permute-done.1.far_ref, bf16[512,512]{1,0:T(8,128)(2,1)S(1)} %get-tuple-element.19.near_ref, bf16[8192,256]{1,0:T(8,128)(2,1)S(1)} %copy-done.1, bf16[8192,256]{1,0:T(8,128)(2,1)S(1)} %collective-permute-done.2.other_ref), custom_call_target="tpu_custom_call" | custom-call | tf_op jit(solution)/shard_map/attend/pallas_call | solution.py:208
  144.0 0.0 copy-start.2
  144.0 1.0 copy-done.2
  144.9 8.8 %project.1 = bf16[1024,4096]{1,0:T(8,128)(2,1)} custom-call(bf16[1024,512]{1,0:T(8,128)(2,1)} %copy-done.2, bf16[16,512,256]{2,1,0:T(8,128)(2,1)} %bitcast.31), custom_call_target="tpu_custom_call" | custom-call | tf_op jit(solution)/shard_map/project/pallas_call | solution.py:232
  153.7 0.0 reduce-scatter.2.cloned.1.call-update
  153.7 0.7 copy-done.8
  154.4 0.1 copy.24
  154.5 0.1 eq.31
  154.6 0.1 eq.27
  154.7 0.1 copy.26
  154.8 0.1 copy-done.10
  154.9 4.9 %collective-permute-start.3 = (bf16[128,4096]{1,0:T(8,128)(2,1)S(1)}, bf16[128,4096]{1,0:T(8,128)(2,1)S(1)}, u32[]{:S(2)}, u32[]{:S(2)}) collective-permute-start(bf16[128,4096]{1,0:T(8,128)(2,1)S(1)} %copy-done.10), channel_id=1, source_target_pairs={{0,0},{1,1},{2,2},{3,3},{4,124},{5,125},{6,126},{7,127},{8,8},{9,9... | collective-permute-start | bytes 3145736 | tf_op jit(solution)/shard_map/ppermute | solution.py:480
  159.8 0.2 fusion.2
  160.2 0.2 fusion.1
  160.4 0.1 reduce_sum.12
  160.5 0.1 copy.28
  160.7 4.2 collective-permute-start
  164.9 21.8 %collective-permute-done = s32[128,4]{1,0:T(8,128)S(1)} collective-permute-done((s32[128,4]{1,0:T(8,128)S(1)}, s32[128,4]{1,0:T(8,128)S(1)}, u32[]{:S(2)}, u32[]{:S(2)}) %collective-permute-start) | collective-permute-done | bytes 2080 | tf_op jit(solution)/shard_map/ppermute | solution.py:480
  186.7 0.6 copy.29.target_ref
  187.4 0.0 collective-permute-done.3.residual_ref
  187.4 16.6 %reduce-scatter.2.cloned.1.call-done.attn_ref = bf16[128,4096]{1,0:T(8,128)(2,1)} async-done(((bf16[1024,4096]{1,0:T(8,128)(2,1)}), bf16[128,4096]{1,0:T(8,128)(2,1)}) %reduce-scatter.2.cloned.1.call-update) | async-done | bytes 1048592 | tf_op jit(solution)/shard_map/reduce_scatter | solution.py:470
  204.0 8.1 %norm_and_dispatch.1 = (bf16[128,4096]{1,0:T(8,128)(2,1)}, bf16[6144,512]{1,0:T(8,128)(2,1)}) custom-call(s32[4,128]{1,0:T(4,128)} %copy.29.target_ref, bf16[128,4096]{1,0:T(8,128)(2,1)} %reduce-scatter.2.cloned.1.call-done.attn_ref, bf16[128,4096]{1,0:T(8,128)(2,1)} %copy-done.6, f32[1,4096]{1,0:T(1,128)} %bitcast.35, ...), custom_call_target="tpu_custom_call" | custom-call | tf_op jit(solution)/shard_map/norm_and_dispatch/pallas_call | solution.py:284
  212.1 83.5 %all_to_all.10 = bf16[128,48,512]{2,1,0:T(8,128)(2,1)} all-to-all(bf16[128,48,512]{2,1,0:T(8,128)(2,1)} %bitcast.29), channel_id=1, replica_groups=mesh['ctx'=16,'tp'=8] {'ctx','tp'}, dimensions={0} | all-to-all | bytes 12582912 | tf_op jit(solution)/shard_map/all_to_all | solution.py:489
  295.6 0.0 copy-done.3
  295.6 23.5 %expert.1 = bf16[6144,512]{1,0:T(8,128)(2,1)S(1)} custom-call(bf16[6144,512]{1,0:T(8,128)(2,1)} %bitcast.27, bf16[2,192,192]{2,1,0:T(8,128)(2,1)S(1)} %copy-done.3, bf16[4096,1536]{1,0:T(8,128)(2,1)} %bitcast.28, bf16[768,4096]{1,0:T(8,128)(2,1)} %bitcast.30), custom_call_target="tpu_custom_call" | custom-call | tf_op jit(solution)/shard_map/expert/pallas_call | solution.py:367
  319.2 2.6 copy-done
  321.8 7.3 %all-to-all-start.1 = ((bf16[128,48,512]{2,1,0:T(8,128)(2,1)}), bf16[128,48,512]{2,1,0:T(8,128)(2,1)}, u32[]{:S(2)}, u32[]{:S(2)}) async-start(bf16[128,48,512]{2,1,0:T(8,128)(2,1)} %bitcast.26), calls=%async_computation.2 | async-start | bytes 12582912 | tf_op jit(solution)/shard_map/all_to_all | solution.py:489
  329.1 0.0 copy-done.11
  329.1 7.7 %collective-permute-start.4 = (bf16[128,4096]{1,0:T(8,128)(2,1)S(1)}, bf16[128,4096]{1,0:T(8,128)(2,1)S(1)}, u32[]{:S(2)}, u32[]{:S(2)}) collective-permute-start(bf16[128,4096]{1,0:T(8,128)(2,1)S(1)} %copy-done.11), channel_id=1, source_target_pairs={{0,0},{1,1},{2,2},{3,3},{4,124},{5,125},{6,126},{7,127},{8,8},{9,9... | collective-permute-start | bytes 3145736 | tf_op jit(solution)/shard_map/ppermute | solution.py:480
  336.9 0.7 copy.30.route_ref
  337.6 89.7 %collective-permute-done.4.hidden_ref = bf16[128,4096]{1,0:T(8,128)(2,1)S(1)} collective-permute-done((bf16[128,4096]{1,0:T(8,128)(2,1)S(1)}, bf16[128,4096]{1,0:T(8,128)(2,1)S(1)}, u32[]{:S(2)}, u32[]{:S(2)}) %collective-permute-start.4) | collective-permute-done | bytes 1048608 | tf_op jit(solution)/shard_map/ppermute | solution.py:480
  427.3 0.0 all-to-all-done.1
  427.3 1.0 copy-done.5
  428.3 8.1 %combine.1 = bf16[128,4096]{1,0:T(8,128)(2,1)} custom-call(s32[128,4]{1,0:T(8,128)} %copy-done.7, f32[128,4]{1,0:T(8,128)} %copy.30.route_ref, bf16[128,4096]{1,0:T(8,128)(2,1)} %copy-done.5, bf16[2,192,192]{2,1,0:T(8,128)(2,1)} %constant.48.clone.swap_ref, bf16[6144,512]{1,0:T(8,128)(2,1)} %bitcast.15.back_ref), custom_call_target="tpu_custom_call" | custom-call | tf_op jit(solution)/shard_map/combine/pallas_call | solution.py:423
  (24 shorter events, 0.1 us)
Async XLA Ops:
  6.5 60.1 %all-gather.4.cloned.1.call-start = ((), (), s32[]{:S(2)}) async-start(), calls=%async_computation.3 | async-start | bytes 4456448 | tf_op jit(solution)/shard_map/all_gather | solution.py:465
  9.5 135.4 %all-gather.6.cloned.1.call-start = ((), (), s32[]{:S(2)}) async-start(), calls=%async_computation.5 | async-start | bytes 4456448 | tf_op jit(solution)/shard_map/all_gather | solution.py:468
  10.3 193.7 %reduce-scatter.2.cloned.1.call-start = ((), (), s32[]{:S(2)}) async-start(), calls=%async_computation.4 | async-start | bytes 9437184 | tf_op jit(solution)/shard_map/reduce_scatter | solution.py:470
  11.6 20.7 %collective-permute-start.1 = (bf16[512,512]{1,0:T(8,128)(2,1)S(1)}, bf16[512,512]{1,0:T(8,128)(2,1)S(1)}, u32[]{:S(2)}, u32[]{:S(2)}) collective-permute-start(bf16[512,512]{1,0:T(8,128)(2,1)S(1)} %get-tuple-element.20), channel_id=1, source_target_pairs={{0,120},{8,112},{16,104},{24,96},{32,88},{40,80},{48,72},{56,64},{... | collective-permute-start | bytes 1572872 | tf_op jit(solution)/shard_map/ppermute | solution.py:460
  66.6 7.4 %collective-permute-start.2 = (bf16[8192,256]{1,0:T(8,128)(2,1)}, bf16[8192,256]{1,0:T(8,128)(2,1)S(1)}, u32[]{:S(2)}, u32[]{:S(2)}) collective-permute-start(bf16[8192,256]{1,0:T(8,128)(2,1)} %all-gather.4.cloned.1.call-done.mine_ref), channel_id=1, source_target_pairs={{0,1},{1,0},{2,3},{3,2},{4,5},{5,4},{6,7},{7,6},{8,9},{9,8},{10,11... | collective-permute-start | bytes 12582920 | tf_op jit(solution)/shard_map/ppermute | solution.py:467
  74.0 2.2 copy-start.1
  76.2 0.6 copy-start.4
  144.0 1.0 copy-start.2
  153.7 0.7 copy-start.8
  153.7 1.2 copy-start.10
  154.9 32.5 %collective-permute-start.3 = (bf16[128,4096]{1,0:T(8,128)(2,1)S(1)}, bf16[128,4096]{1,0:T(8,128)(2,1)S(1)}, u32[]{:S(2)}, u32[]{:S(2)}) collective-permute-start(bf16[128,4096]{1,0:T(8,128)(2,1)S(1)} %copy-done.10), channel_id=1, source_target_pairs={{0,0},{1,1},{2,2},{3,3},{4,124},{5,125},{6,126},{7,127},{8,8},{9,9... | collective-permute-start | bytes 3145736 | tf_op jit(solution)/shard_map/ppermute | solution.py:480
  160.7 135.0 %copy-start.7 = (s32[128,4]{1,0:T(8,128)}, s32[128,4]{1,0:T(8,128)S(1)}, u32[]{:S(2)}) copy-start(s32[128,4]{1,0:T(8,128)S(1)} %add.11.target_ref) | copy-start | bytes 6148
  160.7 26.1 %collective-permute-start = (s32[128,4]{1,0:T(8,128)S(1)}, s32[128,4]{1,0:T(8,128)S(1)}, u32[]{:S(2)}, u32[]{:S(2)}) collective-permute-start(s32[128,4]{1,0:T(8,128)S(1)} %add.11.target_ref), channel_id=1, source_target_pairs={{0,0},{1,1},{2,2},{3,3},{4,124},{5,125},{6,126},{7,127},{8,8},{9,9... | collective-permute-start | bytes 6152 | tf_op jit(solution)/shard_map/ppermute | solution.py:480
  187.4 16.6 %copy-start.6 = (bf16[128,4096]{1,0:T(8,128)(2,1)}, bf16[128,4096]{1,0:T(8,128)(2,1)S(1)}, u32[]{:S(2)}) copy-start(bf16[128,4096]{1,0:T(8,128)(2,1)S(1)} %collective-permute-done.3.residual_ref) | copy-start | bytes 3145732
  212.1 83.5 %copy-start.3 = (bf16[2,192,192]{2,1,0:T(8,128)(2,1)S(1)}, bf16[2,192,192]{2,1,0:T(8,128)(2,1)}, u32[]{:S(2)}) copy-start(bf16[2,192,192]{2,1,0:T(8,128)(2,1)} %constant.48.clone.swap_ref) | copy-start | bytes 442372
  319.2 2.6 copy-start
  321.8 7.3 %copy-start.11 = (bf16[128,4096]{1,0:T(8,128)(2,1)S(1)}, bf16[128,4096]{1,0:T(8,128)(2,1)}, u32[]{:S(2)}) copy-start(bf16[128,4096]{1,0:T(8,128)(2,1)} %get-tuple-element.17) | copy-start | bytes 3145732
  321.8 15.1 %copy-start.9 = (f32[128,4]{0,1:T(4,128)S(1)}, f32[128,4]{0,1:T(4,128)}, u32[]{:S(2)}) copy-start(f32[128,4]{0,1:T(4,128)} %param.18) | copy-start | bytes 6148
  321.8 105.5 %all-to-all-start.1 = ((bf16[128,48,512]{2,1,0:T(8,128)(2,1)}), bf16[128,48,512]{2,1,0:T(8,128)(2,1)}, u32[]{:S(2)}, u32[]{:S(2)}) async-start(bf16[128,48,512]{2,1,0:T(8,128)(2,1)} %bitcast.26), calls=%async_computation.2 | async-start | bytes 12582912 | tf_op jit(solution)/shard_map/all_to_all | solution.py:489
  329.1 98.1 %collective-permute-start.4 = (bf16[128,4096]{1,0:T(8,128)(2,1)S(1)}, bf16[128,4096]{1,0:T(8,128)(2,1)S(1)}, u32[]{:S(2)}, u32[]{:S(2)}) collective-permute-start(bf16[128,4096]{1,0:T(8,128)(2,1)S(1)} %copy-done.11), channel_id=1, source_target_pairs={{0,0},{1,1},{2,2},{3,3},{4,124},{5,125},{6,126},{7,127},{8,8},{9,9... | collective-permute-start | bytes 3145736 | tf_op jit(solution)/shard_map/ppermute | solution.py:480
  427.3 1.0 copy-start.5
Sparse Core Ops, SparseCore 0:
  9.7 56.9 all-gather.3
  68.8 51.3 all-gather.5
  153.8 50.1 reduce-scatter.1

commit v6 on v5

--- a/solution.py
+++ b/solution.py
@@ -24,6 +24,7 @@
 PIECES = 8
 GROUP = 8
 GROUP_ROWS = GROUP * CAP
+DISPATCH_GROUPS = 8
 STEP_GROUPS = 4
 STEP_PIECES = 2
 PROJECT_WIDTH = 1024
@@ -37,21 +38,29 @@
 
 def piece_swap():
     devices = GROUP // 2
-    swap = np.zeros((PIECES, devices, CAP, devices, PIECES, CAP), np.float32)
+    length = PIECES * CAP
+    swap = np.zeros((3, devices * length, devices * length), np.float32)
     for device in range(devices):
         for piece in range(PIECES):
             for slot in range(CAP):
-                swap[piece, device, slot, device, piece, slot] = 1
-    size = devices * PIECES * CAP
-    swap = swap.reshape(size, size)
-    return jnp.asarray(np.stack([swap, swap.T]), jnp.bfloat16)
-
-
-def unpack_group(swap_ref, message_ref, first, rows_of, to):
+                to = (piece * devices + device) * CAP + slot
+                swap[0, to, device * length + piece * CAP + slot] = 1
+                swap[2, to, device * length + tile_row(piece, slot)] = 1
+    swap[1] = swap[0].T
+    return jnp.asarray(swap, jnp.bfloat16)
+
+
+def tile_row(piece, slot):
+    if piece < CAP:
+        return piece * 8 + slot
+    return ((piece - CAP) * (CAP // 2) + slot // 2) * 8 + CAP + slot % 2
+
+
+def unpack_group(swap_ref, which, message_ref, first, rows_of, to):
     size = swap_ref.shape[1]
     part = size // PIECES
     halves = [
-        dot_f32(swap_ref[0], message_ref[pl.ds(pl.multiple_of(first + half * size, size), size), :])
+        dot_f32(swap_ref[which], message_ref[pl.ds(pl.multiple_of(first + half * size, size), size), :])
         for half in range(2)
     ]
     for piece in range(PIECES):
@@ -243,8 +252,10 @@
     )(attended, proj)
 
 
-def dispatch_kernel(target_ref, attn_ref, residual_ref, gain_ref, swap_ref, hidden_ref, out_ref, rows_of):
+def dispatch_kernel(target_ref, attn_ref, residual_ref, gain_ref, hidden_ref, out_ref, normed):
     step = pl.program_id(0)
+    tokens = attn_ref.shape[0]
+    devices = out_ref.shape[0]
 
     @pl.when(step == 0)
     def _():
@@ -254,55 +265,62 @@
         hidden_ref[...] = hidden
         wide = hidden.astype(jnp.float32)
         variance = jnp.mean(wide * wide, axis=-1, keepdims=True)
-        normed = (wide * lax.rsqrt(variance + 1e-06) * gain_ref[...]).astype(jnp.bfloat16)
-        slots, tokens = rows_of.shape[1], normed.shape[0]
-        slot = lax.broadcasted_iota(jnp.int32, (slots, tokens), 0)
-        chosen = jnp.zeros((slots, tokens), jnp.float32)
+        normed[...] = (wide * lax.rsqrt(variance + 1e-06) * gain_ref[...]).astype(jnp.bfloat16)
+
+    number = lax.broadcasted_iota(jnp.int32, (devices * 8, tokens), 0)
+    row = number & 7
+    first = (step * devices + (number >> 3)) * CAP
+
+    def chosen(slot):
+        found = jnp.zeros(slot.shape, jnp.float32)
         for route in range(TOPK):
-            chosen += jnp.where(slot == target_ref[route : route + 1, :], 1.0, 0.0)
-        chosen = chosen.astype(jnp.bfloat16)
-        for piece in range(PIECES):
-            rows_of[piece] = dot_f32(
-                chosen, normed[:, piece * PIECE : (piece + 1) * PIECE]
-            ).astype(jnp.bfloat16)
-
-    group_block = GROUP_ROWS * PIECES
-    for part in range(STEP_GROUPS):
-        at = (step * STEP_GROUPS + part) * GROUP_ROWS
-        at = pl.ds(pl.multiple_of(at, GROUP_ROWS), GROUP_ROWS)
-        pack_group(swap_ref, rows_of, at, out_ref, part * group_block)
-
-
-def dispatch(target, attn_out, residual, gain, swap, dev_count):
+            found += jnp.where(slot == target_ref[route : route + 1, :], 1.0, 0.0)
+        return found.astype(jnp.bfloat16)
+
+    def columns(piece):
+        return normed[:, piece * PIECE : (piece + 1) * PIECE]
+
+    main = chosen(jnp.where(row < CAP, first + row, -1))
+    tails = [
+        chosen(jnp.where(row >= CAP, first + row - CAP + 2 * pair, -1)) for pair in range(CAP // 2)
+    ]
+    for pair in range(CAP // 2):
+        tiles = []
+        for tile in (2 * pair, 2 * pair + 1):
+            taken = jnp.concatenate([main, tails[tile % (CAP // 2)]], 1)
+            source = jnp.concatenate([columns(tile), columns(CAP + tile // (CAP // 2))], 0)
+            tiles.append(dot_f32(taken, source).reshape(devices, 8, PIECE))
+        out_ref[:, pair * 16 : (pair + 1) * 16, :] = jnp.concatenate(tiles, 1).astype(jnp.bfloat16)
+
+
+def dispatch(target, attn_out, residual, gain, dev_count):
     tokens, model = residual.shape
-    slots = dev_count * CAP
-    group_block = GROUP_ROWS * PIECES
+    devices = GROUP * DISPATCH_GROUPS
 
     def whole(shape):
         return pl.BlockSpec(shape, lambda step: (0, 0))
 
     return pl.pallas_call(
         dispatch_kernel,
-        grid=(dev_count // (GROUP * STEP_GROUPS),),
+        grid=(dev_count // devices,),
         out_shape=(
             jax.ShapeDtypeStruct((tokens, model), jnp.bfloat16),
-            jax.ShapeDtypeStruct((slots * PIECES, PIECE), jnp.bfloat16),
+            jax.ShapeDtypeStruct((dev_count, CAP * PIECES, PIECE), jnp.bfloat16),
         ),
         in_specs=[
             whole((TOPK, tokens)),
             whole((tokens, model)),
             whole((tokens, model)),
             whole((1, model)),
-            pl.BlockSpec(swap.shape, lambda step: (0, 0, 0)),
         ],
         out_specs=(
             whole((tokens, model)),
-            pl.BlockSpec((STEP_GROUPS * group_block, PIECE), lambda step: (step, 0)),
+            pl.BlockSpec((devices, CAP * PIECES, PIECE), lambda step: (step, 0, 0)),
         ),
-        scratch_shapes=[pltpu.VMEM((PIECES, slots, PIECE), jnp.bfloat16)],
+        scratch_shapes=[pltpu.VMEM((tokens, model), jnp.bfloat16)],
         compiler_params=pltpu.CompilerParams(vmem_limit_bytes=VMEM_BYTES),
         name="norm_and_dispatch",
-    )(target, attn_out, residual, gain, swap)
+    )(target, attn_out, residual, gain)
 
 
 def expert_kernel(
@@ -331,7 +349,7 @@
 
     def unpack(group, carry):
         to = pl.ds(pl.multiple_of(group * GROUP_ROWS, GROUP_ROWS), GROUP_ROWS)
-        unpack_group(swap_ref, arrived_ref, group * group_block, rows_of, to)
+        unpack_group(swap_ref, 2, arrived_ref, group * group_block, rows_of, to)
         return carry
 
     lax.fori_loop(0, groups, unpack, 0, unroll=4)
@@ -377,6 +395,11 @@
             pltpu.VMEM((slots, 2 * FF), jnp.float32),
             pltpu.VMEM((slots, FF), jnp.bfloat16),
         ],
+        cost_estimate=pl.CostEstimate(
+            flops=2 * slots * (w_in.size + w_out.size),
+            bytes_accessed=2 * (2 * arrived.size + w_in.size + w_out.size),
+            transcendentals=slots * FF,
+        ),
         compiler_params=pltpu.CompilerParams(vmem_limit_bytes=EXPERT_VMEM),
         name="expert",
     )(arrived, swap, w_in, w_out)
@@ -388,7 +411,7 @@
     for part in range(STEP_GROUPS):
         to = (step * STEP_GROUPS + part) * GROUP_ROWS
         to = pl.ds(pl.multiple_of(to, GROUP_ROWS), GROUP_ROWS)
-        unpack_group(swap_ref, back_ref, part * group_block, rows_of, to)
+        unpack_group(swap_ref, 0, back_ref, part * group_block, rows_of, to)
 
     @pl.when(step == pl.num_programs(0) - 1)
     def _():
@@ -481,18 +504,18 @@
 
     residual, projected = lax.optimization_barrier((residual, projected))
     hidden, packed = dispatch(
-        trade(target).T, attn_out, trade(residual), norm_gain.reshape(1, -1), swap, dev_count
+        trade(target).T, attn_out, trade(residual), norm_gain.reshape(1, -1), dev_count
     )
 
-    def exchange(rows):
-        shaped = rows.reshape(dev_count, CAP * PIECES, PIECE)
-        return lax.all_to_all(
-            shaped, ("ctx", "tp"), split_axis=0, concat_axis=0, tiled=True
-        ).reshape(rows.shape)
+    def exchange(messages):
+        shaped = messages.reshape(dev_count, CAP * PIECES, PIECE)
+        arrived = lax.all_to_all(shaped, ("ctx", "tp"), split_axis=0, concat_axis=0, tiled=True)
+        return arrived.reshape(dev_count * CAP * PIECES, PIECE)
 
     hidden, arrived = lax.optimization_barrier((hidden, exchange(packed)))
     processed = run_expert(arrived, swap, w_in[0], w_out[0])
-    return combine(target, route_weights, trade(hidden), swap, exchange(processed))
+    hidden, processed = lax.optimization_barrier((trade(hidden), processed))
+    return combine(target, route_weights, hidden, swap, exchange(processed))
 
 
 def solution(mesh):

time: 444 us -> 426 us (0.959)
  waiting for transfers between devices: 185 us -> 170 us
    ppermute x3, waiting for transfers between devices: 111 us -> 21.9 us  [trade(): return lax.ppermute(array, ('ctx', 'tp'), home)]
    all_to_all x1, waiting for transfers between devices: 0.01 us -> 74.9 us  [exchange(): lax.all_to_all(shaped, ('ctx', 'tp'), split_axis=0, concat_axis=0, tiled=...]
  transfers between devices with their start and end apart: 9 -> 9, of which waited for: 6 -> 7; matrix products, arithmetic and copies ran while one was open for 1% -> 1% of each run, Pallas kernels for 15% -> 21%
where the time goes in v6:
time: 426 us; the launch traced here: 423 us
  waiting for transfers between devices  170 us (40%)
  Pallas kernels  116 us (27%)
  blocking collectives  83.5 us (20%)
  starting transfers between devices  27.3 us (6%)
  between operations  13.3 us (3%)
  local copies, waits for them, and re-layouts  11.5 us (3%)
    all_to_all x1, blocking collectives, exchange(): lax.all_to_all(shaped, ('ctx', 'tp'), split_axis=0, concat_axis=0, tiled=...  83.5 us
    all_to_all x1, waiting for transfers between devices, exchange(): lax.all_to_all(shaped, ('ctx', 'tp'), split_axis=0, concat_axis=0, tiled=...  74.9 us
    pallas_call x1, Pallas kernels, attend(): pl.pallas_call(attend_kernel, out_shape=jax.ShapeDtypeStruct((2 * rows, c...  67.2 us
    all_gather x1, waiting for transfers between devices, body(): lax.all_gather(own_half(place, keys, values, half), 'ctx', axis=0, tiled=...  34.3 us
    pallas_call x1, Pallas kernels, run_expert(): pl.pallas_call(expert_kernel, out_shape=jax.ShapeDtypeStruct(arrived.shap...  23.5 us
    ppermute x3, waiting for transfers between devices, trade(): return lax.ppermute(array, ('ctx', 'tp'), home)  21.9 us
    reduce_scatter x1, waiting for transfers between devices, body(): lax.psum_scatter(projected, 'tp', scatter_dimension=0, tiled=True)  16.6 us
    ppermute x1, waiting for transfers between devices, body(): swapped = lax.ppermute(queries[half:], 'ctx', opposite)  14.2 us
  transfers between devices with their start and end apart: 9, of which 7 were waited for; matrix products, arithmetic and copies ran while one was open for 1% of the time, Pallas kernels for 21%

profile of v6, /device:TPU:6, one launch (start us, length us, event | category | flops | bytes accessed | tf_op | source)
XLA Modules:
  0.0 423.0 jit_solution(11318409152760015018)
XLA Ops:
  6.5 0.0 all-gather.4.cloned.1.call-start
  6.5 0.6 pad_add_fusion.place_ref
  7.1 2.4 own_half.1
  9.5 0.0 all-gather.4.cloned.1.call-update
  9.5 0.0 all-gather.6.cloned.1.call-start
  9.6 0.7 all-gather.6.cloned.1.call-update
  10.3 0.0 reduce-scatter.2.cloned.1.call-start
  10.3 1.3 fusion.5
  11.6 6.6 %collective-permute-start.1 = (bf16[512,512]{1,0:T(8,128)(2,1)S(1)}, bf16[512,512]{1,0:T(8,128)(2,1)S(1)}, u32[]{:S(2)}, u32[]{:S(2)}) collective-permute-start(bf16[512,512]{1,0:T(8,128)(2,1)S(1)} %get-tuple-element.24), channel_id=1, source_target_pairs={{0,120},{8,112},{16,104},{24,96},{32,88},{40,80},{48,72},{56,64},{... | collective-permute-start | bytes 1572872 | tf_op jit(solution)/shard_map/ppermute | solution.py:483
  18.2 14.2 %collective-permute-done.1.far_ref = bf16[512,512]{1,0:T(8,128)(2,1)S(1)} collective-permute-done((bf16[512,512]{1,0:T(8,128)(2,1)S(1)}, bf16[512,512]{1,0:T(8,128)(2,1)S(1)}, u32[]{:S(2)}, u32[]{:S(2)}) %collective-permute-start.1) | collective-permute-done | bytes 524320 | tf_op jit(solution)/shard_map/ppermute | solution.py:483
  32.4 34.3 %all-gather.4.cloned.1.call-done.mine_ref = bf16[8192,256]{1,0:T(8,128)(2,1)} async-done(((bf16[512,256]{1,0:T(8,128)(2,1)}), bf16[8192,256]{1,0:T(8,128)(2,1)}) %all-gather.4.cloned.1.call-update) | async-done | bytes 4194320 | tf_op jit(solution)/shard_map/all_gather | solution.py:488
  66.6 0.0 collective-permute-start.2
  66.6 7.4 %collective-permute-done.2.other_ref = bf16[8192,256]{1,0:T(8,128)(2,1)S(1)} collective-permute-done((bf16[8192,256]{1,0:T(8,128)(2,1)}, bf16[8192,256]{1,0:T(8,128)(2,1)S(1)}, u32[]{:S(2)}, u32[]{:S(2)}) %collective-permute-start.2) | collective-permute-done | bytes 4194336 | tf_op jit(solution)/shard_map/ppermute | solution.py:490
  74.0 2.2 copy-done.1
  76.2 0.6 copy-done.4
  76.8 67.2 %attend.1.attended_ref = bf16[1024,512]{1,0:T(8,128)(2,1)S(1)} custom-call(s32[4]{0:T(128)S(1)} %copy-done.4, bf16[512,512]{1,0:T(8,128)(2,1)S(1)} %collective-permute-done.1.far_ref, bf16[512,512]{1,0:T(8,128)(2,1)S(1)} %get-tuple-element.23.near_ref, bf16[8192,256]{1,0:T(8,128)(2,1)S(1)} %copy-done.1, bf16[8192,256]{1,0:T(8,128)(2,1)S(1)} %collective-permute-done.2.other_ref), custom_call_target="tpu_custom_call" | custom-call | tf_op jit(solution)/shard_map/attend/pallas_call | solution.py:217
  144.0 0.0 copy-start.2
  144.0 1.0 copy-done.2
  144.9 8.8 %project.1 = bf16[1024,4096]{1,0:T(8,128)(2,1)} custom-call(bf16[1024,512]{1,0:T(8,128)(2,1)} %copy-done.2, bf16[16,512,256]{2,1,0:T(8,128)(2,1)} %bitcast.27), custom_call_target="tpu_custom_call" | custom-call | tf_op jit(solution)/shard_map/project/pallas_call | solution.py:241
  153.7 0.0 reduce-scatter.2.cloned.1.call-update
  153.7 0.7 copy-done.8
  154.4 0.1 copy.24
  154.5 0.1 eq.31
  154.6 0.1 eq.27
  154.7 0.1 copy.26
  154.8 0.1 copy-done.10
  154.9 4.9 %collective-permute-start.3 = (bf16[128,4096]{1,0:T(8,128)(2,1)S(1)}, bf16[128,4096]{1,0:T(8,128)(2,1)S(1)}, u32[]{:S(2)}, u32[]{:S(2)}) collective-permute-start(bf16[128,4096]{1,0:T(8,128)(2,1)S(1)} %copy-done.10), channel_id=1, source_target_pairs={{0,0},{1,1},{2,2},{3,3},{4,124},{5,125},{6,126},{7,127},{8,8},{9,9... | collective-permute-start | bytes 3145736 | tf_op jit(solution)/shard_map/ppermute | solution.py:503
  159.8 0.2 fusion.2
  160.2 0.2 fusion.1
  160.4 0.1 reduce_sum.12
  160.5 0.1 copy.28
  160.7 0.0 copy-start.7
  160.7 4.2 %collective-permute-start = (s32[128,4]{1,0:T(8,128)S(1)}, s32[128,4]{1,0:T(8,128)S(1)}, u32[]{:S(2)}, u32[]{:S(2)}) collective-permute-start(s32[128,4]{1,0:T(8,128)S(1)} %add.11.target_ref), channel_id=1, source_target_pairs={{0,0},{1,1},{2,2},{3,3},{4,124},{5,125},{6,126},{7,127},{8,8},{9,9... | collective-permute-start | bytes 6152 | tf_op jit(solution)/shard_map/ppermute | solution.py:503
  164.9 21.8 %collective-permute-done = s32[128,4]{1,0:T(8,128)S(1)} collective-permute-done((s32[128,4]{1,0:T(8,128)S(1)}, s32[128,4]{1,0:T(8,128)S(1)}, u32[]{:S(2)}, u32[]{:S(2)}) %collective-permute-start) | collective-permute-done | bytes 2080 | tf_op jit(solution)/shard_map/ppermute | solution.py:503
  186.7 0.6 copy.29.target_ref
  187.4 0.0 collective-permute-done.3.residual_ref
  187.4 16.6 %reduce-scatter.2.cloned.1.call-done.attn_ref = bf16[128,4096]{1,0:T(8,128)(2,1)} async-done(((bf16[1024,4096]{1,0:T(8,128)(2,1)}), bf16[128,4096]{1,0:T(8,128)(2,1)}) %reduce-scatter.2.cloned.1.call-update) | async-done | bytes 1048592 | tf_op jit(solution)/shard_map/reduce_scatter | solution.py:493
  204.0 6.3 %norm_and_dispatch.1 = (bf16[128,4096]{1,0:T(8,128)(2,1)}, bf16[128,48,512]{2,1,0:T(8,128)(2,1)}) custom-call(s32[4,128]{1,0:T(4,128)} %copy.29.target_ref, bf16[128,4096]{1,0:T(8,128)(2,1)} %reduce-scatter.2.cloned.1.call-done.attn_ref, bf16[128,4096]{1,0:T(8,128)(2,1)} %copy-done.6, f32[1,4096]{1,0:T(1,128)} %bitcast.31), custom_call_target="tpu_custom_call" | custom-call | tf_op jit(solution)/shard_map/norm_and_dispatch/pallas_call | solution.py:303
  210.3 83.5 %all_to_all.10 = bf16[128,48,512]{2,1,0:T(8,128)(2,1)} all-to-all(bf16[128,48,512]{2,1,0:T(8,128)(2,1)} %get-tuple-element.18), channel_id=1, replica_groups=mesh['ctx'=16,'tp'=8] {'ctx','tp'}, dimensions={0} | all-to-all | bytes 12582912 | tf_op jit(solution)/shard_map/all_to_all | solution.py:512
  293.8 4.1 collective-permute-start.4
  297.9 23.5 %expert.1 = bf16[6144,512]{1,0:T(8,128)(2,1)S(1)} custom-call(bf16[6144,512]{1,0:T(8,128)(2,1)} %bitcast.26, bf16[3,192,192]{2,1,0:T(8,128)(2,1)S(1)} %copy-done.3, bf16[4096,1536]{1,0:T(8,128)(2,1)} %bitcast.33, bf16[768,4096]{1,0:T(8,128)(2,1)} %bitcast.34), custom_call_target="tpu_custom_call" | custom-call | flops 14495514624 | bytes 31457280 | tf_op jit(solution)/shard_map/expert/pallas_call | solution.py:385
  321.5 2.6 copy-done
  324.1 0.1 collective-permute-done.4.hidden_ref
  324.2 1.0 copy-done.5
  325.2 7.4 %all-to-all-start.1 = ((bf16[128,48,512]{2,1,0:T(8,128)(2,1)}), bf16[128,48,512]{2,1,0:T(8,128)(2,1)}, u32[]{:S(2)}, u32[]{:S(2)}) async-start(bf16[128,48,512]{2,1,0:T(8,128)(2,1)} %bitcast.25), calls=%async_computation.2 | async-start | bytes 12582912 | tf_op jit(solution)/shard_map/all_to_all | solution.py:512
  332.6 0.7 copy.30.route_ref
  333.3 74.9 %all-to-all-done.1 = bf16[128,48,512]{2,1,0:T(8,128)(2,1)} async-done(((bf16[128,48,512]{2,1,0:T(8,128)(2,1)}), bf16[128,48,512]{2,1,0:T(8,128)(2,1)}, u32[]{:S(2)}, u32[]{:S(2)}) %all-to-all-start.1) | async-done | bytes 6291488 | tf_op jit(solution)/shard_map/all_to_all | solution.py:512
  408.3 8.2 %combine.1 = bf16[128,4096]{1,0:T(8,128)(2,1)} custom-call(s32[128,4]{1,0:T(8,128)} %copy-done.7, f32[128,4]{1,0:T(8,128)} %copy.30.route_ref, bf16[128,4096]{1,0:T(8,128)(2,1)} %copy-done.5, bf16[3,192,192]{2,1,0:T(8,128)(2,1)} %constant.48.clone.swap_ref, bf16[6144,512]{1,0:T(8,128)(2,1)} %bitcast.14.back_ref), custom_call_target="tpu_custom_call" | custom-call | tf_op jit(solution)/shard_map/combine/pallas_call | solution.py:446
  (24 shorter events, 0.1 us)
Async XLA Ops:
  6.5 60.1 %all-gather.4.cloned.1.call-start = ((), (), s32[]{:S(2)}) async-start(), calls=%async_computation.3 | async-start | bytes 4456448 | tf_op jit(solution)/shard_map/all_gather | solution.py:488
  9.5 135.4 %all-gather.6.cloned.1.call-start = ((), (), s32[]{:S(2)}) async-start(), calls=%async_computation.5 | async-start | bytes 4456448 | tf_op jit(solution)/shard_map/all_gather | solution.py:491
  10.3 193.7 %reduce-scatter.2.cloned.1.call-start = ((), (), s32[]{:S(2)}) async-start(), calls=%async_computation.4 | async-start | bytes 9437184 | tf_op jit(solution)/shard_map/reduce_scatter | solution.py:493
  11.6 20.7 %collective-permute-start.1 = (bf16[512,512]{1,0:T(8,128)(2,1)S(1)}, bf16[512,512]{1,0:T(8,128)(2,1)S(1)}, u32[]{:S(2)}, u32[]{:S(2)}) collective-permute-start(bf16[512,512]{1,0:T(8,128)(2,1)S(1)} %get-tuple-element.24), channel_id=1, source_target_pairs={{0,120},{8,112},{16,104},{24,96},{32,88},{40,80},{48,72},{56,64},{... | collective-permute-start | bytes 1572872 | tf_op jit(solution)/shard_map/ppermute | solution.py:483
  66.6 7.4 %collective-permute-start.2 = (bf16[8192,256]{1,0:T(8,128)(2,1)}, bf16[8192,256]{1,0:T(8,128)(2,1)S(1)}, u32[]{:S(2)}, u32[]{:S(2)}) collective-permute-start(bf16[8192,256]{1,0:T(8,128)(2,1)} %all-gather.4.cloned.1.call-done.mine_ref), channel_id=1, source_target_pairs={{0,1},{1,0},{2,3},{3,2},{4,5},{5,4},{6,7},{7,6},{8,9},{9,8},{10,11... | collective-permute-start | bytes 12582920 | tf_op jit(solution)/shard_map/ppermute | solution.py:490
  74.0 2.2 copy-start.1
  76.2 0.6 copy-start.4
  144.0 1.0 copy-start.2
  153.7 0.7 copy-start.8
  153.7 1.2 copy-start.10
  154.9 32.5 %collective-permute-start.3 = (bf16[128,4096]{1,0:T(8,128)(2,1)S(1)}, bf16[128,4096]{1,0:T(8,128)(2,1)S(1)}, u32[]{:S(2)}, u32[]{:S(2)}) collective-permute-start(bf16[128,4096]{1,0:T(8,128)(2,1)S(1)} %copy-done.10), channel_id=1, source_target_pairs={{0,0},{1,1},{2,2},{3,3},{4,124},{5,125},{6,126},{7,127},{8,8},{9,9... | collective-permute-start | bytes 3145736 | tf_op jit(solution)/shard_map/ppermute | solution.py:503
  160.7 133.2 %copy-start.7 = (s32[128,4]{1,0:T(8,128)}, s32[128,4]{1,0:T(8,128)S(1)}, u32[]{:S(2)}) copy-start(s32[128,4]{1,0:T(8,128)S(1)} %add.11.target_ref) | copy-start | bytes 6148
  160.7 26.1 %collective-permute-start = (s32[128,4]{1,0:T(8,128)S(1)}, s32[128,4]{1,0:T(8,128)S(1)}, u32[]{:S(2)}, u32[]{:S(2)}) collective-permute-start(s32[128,4]{1,0:T(8,128)S(1)} %add.11.target_ref), channel_id=1, source_target_pairs={{0,0},{1,1},{2,2},{3,3},{4,124},{5,125},{6,126},{7,127},{8,8},{9,9... | collective-permute-start | bytes 6152 | tf_op jit(solution)/shard_map/ppermute | solution.py:503
  187.4 16.6 %copy-start.6 = (bf16[128,4096]{1,0:T(8,128)(2,1)}, bf16[128,4096]{1,0:T(8,128)(2,1)S(1)}, u32[]{:S(2)}) copy-start(bf16[128,4096]{1,0:T(8,128)(2,1)S(1)} %collective-permute-done.3.residual_ref) | copy-start | bytes 3145732
  210.3 83.5 %copy-start.11 = (bf16[128,4096]{1,0:T(8,128)(2,1)S(1)}, bf16[128,4096]{1,0:T(8,128)(2,1)}, u32[]{:S(2)}) copy-start(bf16[128,4096]{1,0:T(8,128)(2,1)} %get-tuple-element.19) | copy-start | bytes 3145732
  210.3 87.6 %copy-start.3 = (bf16[3,192,192]{2,1,0:T(8,128)(2,1)S(1)}, bf16[3,192,192]{2,1,0:T(8,128)(2,1)}, u32[]{:S(2)}) copy-start(bf16[3,192,192]{2,1,0:T(8,128)(2,1)} %constant.48.clone.swap_ref) | copy-start | bytes 663556
  293.8 30.4 %collective-permute-start.4 = (bf16[128,4096]{1,0:T(8,128)(2,1)S(1)}, bf16[128,4096]{1,0:T(8,128)(2,1)S(1)}, u32[]{:S(2)}, u32[]{:S(2)}) collective-permute-start(bf16[128,4096]{1,0:T(8,128)(2,1)S(1)} %copy-done.11), channel_id=1, source_target_pairs={{0,0},{1,1},{2,2},{3,3},{4,124},{5,125},{6,126},{7,127},{8,8},{9,9... | collective-permute-start | bytes 3145736 | tf_op jit(solution)/shard_map/ppermute | solution.py:503
  321.5 2.6 copy-start
  324.2 1.0 copy-start.5
  324.2 8.4 %copy-start.9 = (f32[128,4]{0,1:T(4,128)S(1)}, f32[128,4]{0,1:T(4,128)}, u32[]{:S(2)}) copy-start(f32[128,4]{0,1:T(4,128)} %param.18) | copy-start | bytes 6148
  325.2 83.0 %all-to-all-start.1 = ((bf16[128,48,512]{2,1,0:T(8,128)(2,1)}), bf16[128,48,512]{2,1,0:T(8,128)(2,1)}, u32[]{:S(2)}, u32[]{:S(2)}) async-start(bf16[128,48,512]{2,1,0:T(8,128)(2,1)} %bitcast.25), calls=%async_computation.2 | async-start | bytes 12582912 | tf_op jit(solution)/shard_map/all_to_all | solution.py:512
Sparse Core Ops, SparseCore 0:
  9.7 56.9 all-gather.3
  68.8 51.3 all-gather.5
  153.8 50.1 reduce-scatter.1

commit v7 on v6

--- a/solution.py
+++ b/solution.py
@@ -27,9 +27,8 @@
 DISPATCH_GROUPS = 8
 STEP_GROUPS = 4
 STEP_PIECES = 2
-PROJECT_WIDTH = 1024
+PROJECT_WIDTH = 2048
 VMEM_BYTES = 56 * 2**20
-EXPERT_VMEM = 46 * 2**20
 ATTEND_VMEM = 36 * 2**20
 
 VMEM_SPEC = pl.BlockSpec(memory_space=pltpu.VMEM)
@@ -69,13 +68,13 @@
         ).astype(jnp.bfloat16)
 
 
-def pack_group(swap_ref, rows_of, at, message_ref, first, second=None):
+def pack_group(swap_ref, rows_of, at, message_ref, first):
     size = swap_ref.shape[1]
     part = size // PIECES
     pieces = [rows_of[piece, at, :].astype(jnp.float32) for piece in range(PIECES)]
     for half in range(2):
         stacked = jnp.concatenate([rows[half * part : (half + 1) * part] for rows in pieces], 0)
-        to = first + half * size if second is None or half == 0 else second
+        to = first + half * size
         message_ref[pl.ds(pl.multiple_of(to, size), size), :] = dot_f32(
             swap_ref[1], stacked.astype(jnp.bfloat16)
         ).astype(jnp.bfloat16)
@@ -324,59 +323,90 @@
 
 
 def expert_kernel(
-    arrived_ref, swap_ref, in_hbm, down_hbm, out_ref, in_ref, down_ref, landed, rows_of, gate_up, active
+    arrived_hbm, swap_ref, in_hbm, down_hbm, out_hbm, in_ref, down_ref, landed, messages, moved, left, rows_of, gate_up, active
 ):
+    group_block = GROUP_ROWS * PIECES
     groups = rows_of.shape[1] // GROUP_ROWS
-    group_block = GROUP_ROWS * PIECES
     steps = PIECES // STEP_PIECES
     width = STEP_PIECES * PIECE
-
-    def columns(step):
-        return slice(step * width, (step + 1) * width)
-
-    weights_in = [
-        pltpu.make_async_copy(in_hbm.at[columns(step), :], in_ref.at[columns(step), :], landed.at[0, step])
-        for step in range(steps)
-    ]
-    weights_down = [
-        pltpu.make_async_copy(
-            down_hbm.at[:, columns(step)], down_ref.at[:, columns(step)], landed.at[1, step]
-        )
-        for step in range(steps)
-    ]
-    for copy in weights_in + weights_down:
-        copy.start()
-
-    def unpack(group, carry):
-        to = pl.ds(pl.multiple_of(group * GROUP_ROWS, GROUP_ROWS), GROUP_ROWS)
-        unpack_group(swap_ref, 2, arrived_ref, group * group_block, rows_of, to)
+    chunk_rows = STEP_GROUPS * group_block
+    chunks = messages.shape[0] // chunk_rows
+
+    def span(index, size):
+        return pl.ds(pl.multiple_of(index * size, size), size)
+
+    def arriving(chunk):
+        at = span(chunk, chunk_rows)
+        return pltpu.make_async_copy(arrived_hbm.at[at, :], messages.at[at, :], moved.at[0, chunk])
+
+    def leaving(chunk, half):
+        half_rows = group_block // 2
+        for part in range(STEP_GROUPS):
+            group = chunk * STEP_GROUPS + part
+            home = group if half == 0 else groups - 1 - group
+            source = pl.ds(pl.multiple_of((2 * group + half) * half_rows, half_rows), half_rows)
+            to = pl.ds(pl.multiple_of((2 * home + half) * half_rows, half_rows), half_rows)
+            yield pltpu.make_async_copy(
+                messages.at[source, :], out_hbm.at[to, :], left.at[half, group]
+            )
+
+    def weights_in(step):
+        at = span(step, width)
+        return pltpu.make_async_copy(in_hbm.at[at, :], in_ref.at[at, :], landed.at[0, step])
+
+    def weights_down(step):
+        at = span(step, width)
+        return pltpu.make_async_copy(down_hbm.at[:, at], down_ref.at[step], landed.at[1, step])
+
+    for chunk in range(chunks):
+        arriving(chunk).start()
+
+    def unpack(chunk, carry):
+        arriving(chunk).wait()
+        weights_in(chunk).start()
+        for part in range(STEP_GROUPS):
+            group = chunk * STEP_GROUPS + part
+            unpack_group(swap_ref, 2, messages, group * group_block, rows_of, span(group, GROUP_ROWS))
         return carry
 
-    lax.fori_loop(0, groups, unpack, 0, unroll=4)
-    for step in range(steps):
-        weights_in[step].wait()
-        pieces = range(step * STEP_PIECES, (step + 1) * STEP_PIECES)
-        rows = jnp.concatenate([rows_of[piece] for piece in pieces], 1)
-        part = dot_f32(rows, in_ref[columns(step), :])
-        if step == 0:
-            gate_up[...] = part
-        else:
-            gate_up[...] += part
+    def up(step, carry):
+        weights_in(step).wait()
+        weights_down(step).start()
+        first = step * STEP_PIECES
+        rows = jnp.concatenate([rows_of[first + part] for part in range(STEP_PIECES)], 1)
+        gate_up[...] += dot_f32(rows, in_ref[span(step, width), :])
+        return carry
+
+    def down(step, carry):
+        weights_down(step).wait()
+        for part in range(STEP_PIECES):
+            rows_of[step * STEP_PIECES + part] = dot_f32(
+                active[...], down_ref[step, :, part * PIECE : (part + 1) * PIECE]
+            ).astype(jnp.bfloat16)
+        return carry
+
+    def pack(chunk, carry):
+        for part in range(STEP_GROUPS):
+            group = chunk * STEP_GROUPS + part
+            pack_group(swap_ref, rows_of, span(group, GROUP_ROWS), messages, group * group_block)
+        for half in range(2):
+            for copy in leaving(chunk, half):
+                copy.start()
+        return carry
+
+    def leave(chunk, carry):
+        for half in range(2):
+            for copy in leaving(chunk, half):
+                copy.wait()
+        return carry
+
+    lax.fori_loop(0, chunks, unpack, 0)
+    gate_up[...] = jnp.zeros_like(gate_up)
+    lax.fori_loop(0, steps, up, 0)
     active[...] = (jax.nn.silu(gate_up[:, :FF]) * gate_up[:, FF:]).astype(jnp.bfloat16)
-    for step in range(steps):
-        weights_down[step].wait()
-        for piece in range(step * STEP_PIECES, (step + 1) * STEP_PIECES):
-            rows_of[piece] = dot_f32(
-                active[...], down_ref[:, piece * PIECE : (piece + 1) * PIECE]
-            ).astype(jnp.bfloat16)
-
-    def pack(group, carry):
-        at = pl.ds(pl.multiple_of(group * GROUP_ROWS, GROUP_ROWS), GROUP_ROWS)
-        second = (groups - 1 - group) * group_block + group_block // 2
-        pack_group(swap_ref, rows_of, at, out_ref, group * group_block, second)
-        return carry
-
-    lax.fori_loop(0, groups, pack, 0, unroll=4)
+    lax.fori_loop(0, steps, down, 0)
+    lax.fori_loop(0, chunks, pack, 0)
+    lax.fori_loop(0, chunks, leave, 0)
 
 
 def run_expert(arrived, swap, w_in, w_out):
@@ -385,12 +415,15 @@
     return pl.pallas_call(
         expert_kernel,
         out_shape=jax.ShapeDtypeStruct(arrived.shape, jnp.bfloat16),
-        in_specs=[VMEM_SPEC, VMEM_SPEC, any_spec, any_spec],
-        out_specs=VMEM_SPEC,
+        in_specs=[any_spec, VMEM_SPEC, any_spec, any_spec],
+        out_specs=any_spec,
         scratch_shapes=[
             pltpu.VMEM(w_in.shape, jnp.bfloat16),
-            pltpu.VMEM(w_out.shape, jnp.bfloat16),
+            pltpu.VMEM((PIECES // STEP_PIECES, FF, STEP_PIECES * PIECE), jnp.bfloat16),
             pltpu.SemaphoreType.DMA((2, PIECES // STEP_PIECES)),
+            pltpu.VMEM(arrived.shape, jnp.bfloat16),
+            pltpu.SemaphoreType.DMA((1, slots // (GROUP_ROWS * STEP_GROUPS))),
+            pltpu.SemaphoreType.DMA((2, slots // GROUP_ROWS)),
             pltpu.VMEM((PIECES, slots, PIECE), jnp.bfloat16),
             pltpu.VMEM((slots, 2 * FF), jnp.float32),
             pltpu.VMEM((slots, FF), jnp.bfloat16),
@@ -400,7 +433,7 @@
             bytes_accessed=2 * (2 * arrived.size + w_in.size + w_out.size),
             transcendentals=slots * FF,
         ),
-        compiler_params=pltpu.CompilerParams(vmem_limit_bytes=EXPERT_VMEM),
+        compiler_params=pltpu.CompilerParams(vmem_limit_bytes=VMEM_BYTES),
         name="expert",
     )(arrived, swap, w_in, w_out)
 

time: 426 us -> 425 us (level)
    unnamed x27 -> x23, local copies, waits for them, and re-layouts: 9.05 us -> 6.51 us
  transfers between devices with their start and end apart: 9 -> 9, of which waited for: 7 -> 7; matrix products, arithmetic and copies ran while one was open for 1% -> 1% of each run, Pallas kernels for 21% -> 22%
where the time goes in v7:
time: 425 us; the launch traced here: 422 us
  waiting for transfers between devices  171 us (40%)
  Pallas kernels  118 us (28%)
  blocking collectives  83.5 us (20%)
  starting transfers between devices  26.3 us (6%)
  between operations  13.2 us (3%)
  local copies, waits for them, and re-layouts  9.02 us (2%)
    all_to_all x1, blocking collectives, exchange(): lax.all_to_all(shaped, ('ctx', 'tp'), split_axis=0, concat_axis=0, tiled=...  83.5 us
    all_to_all x1, waiting for transfers between devices, exchange(): lax.all_to_all(shaped, ('ctx', 'tp'), split_axis=0, concat_axis=0, tiled=...  74.9 us
    pallas_call x1, Pallas kernels, attend(): pl.pallas_call(attend_kernel, out_shape=jax.ShapeDtypeStruct((2 * rows, c...  67.2 us
    all_gather x1, waiting for transfers between devices, body(): lax.all_gather(own_half(place, keys, values, half), 'ctx', axis=0, tiled=...  34.3 us
    pallas_call x1, Pallas kernels, run_expert(): pl.pallas_call(expert_kernel, out_shape=jax.ShapeDtypeStruct(arrived.shap...  25.2 us
    ppermute x3, waiting for transfers between devices, trade(): return lax.ppermute(array, ('ctx', 'tp'), home)  22.9 us
    reduce_scatter x1, waiting for transfers between devices, body(): lax.psum_scatter(projected, 'tp', scatter_dimension=0, tiled=True)  16.6 us
    ppermute x1, waiting for transfers between devices, body(): swapped = lax.ppermute(queries[half:], 'ctx', opposite)  14.2 us
  transfers between devices with their start and end apart: 9, of which 7 were waited for; matrix products, arithmetic and copies ran while one was open for 1% of the time, Pallas kernels for 22%

profile of v7, /device:TPU:6, one launch (start us, length us, event | category | flops | bytes accessed | tf_op | source)
XLA Modules:
  0.0 422.0 jit_solution(5348854032429451846)
XLA Ops:
  6.5 0.0 all-gather.4.cloned.1.call-start
  6.5 0.7 pad_add_fusion.place_ref
  7.2 2.4 own_half.1
  9.6 0.0 all-gather.4.cloned.1.call-update
  9.6 0.0 all-gather.6.cloned.1.call-start
  9.7 0.7 all-gather.6.cloned.1.call-update
  10.4 0.0 reduce-scatter.2.cloned.1.call-start
  10.4 1.3 fusion.5
  11.7 6.6 %collective-permute-start.1 = (bf16[512,512]{1,0:T(8,128)(2,1)S(1)}, bf16[512,512]{1,0:T(8,128)(2,1)S(1)}, u32[]{:S(2)}, u32[]{:S(2)}) collective-permute-start(bf16[512,512]{1,0:T(8,128)(2,1)S(1)} %get-tuple-element.24), channel_id=1, source_target_pairs={{0,120},{8,112},{16,104},{24,96},{32,88},{40,80},{48,72},{56,64},{... | collective-permute-start | bytes 1572872 | tf_op jit(solution)/shard_map/ppermute | solution.py:516
  18.3 14.2 %collective-permute-done.1.far_ref = bf16[512,512]{1,0:T(8,128)(2,1)S(1)} collective-permute-done((bf16[512,512]{1,0:T(8,128)(2,1)S(1)}, bf16[512,512]{1,0:T(8,128)(2,1)S(1)}, u32[]{:S(2)}, u32[]{:S(2)}) %collective-permute-start.1) | collective-permute-done | bytes 524320 | tf_op jit(solution)/shard_map/ppermute | solution.py:516
  32.4 34.3 %all-gather.4.cloned.1.call-done.mine_ref = bf16[8192,256]{1,0:T(8,128)(2,1)} async-done(((bf16[512,256]{1,0:T(8,128)(2,1)}), bf16[8192,256]{1,0:T(8,128)(2,1)}) %all-gather.4.cloned.1.call-update) | async-done | bytes 4194320 | tf_op jit(solution)/shard_map/all_gather | solution.py:521
  66.7 0.0 collective-permute-start.2
  66.7 7.4 %collective-permute-done.2.other_ref = bf16[8192,256]{1,0:T(8,128)(2,1)S(1)} collective-permute-done((bf16[8192,256]{1,0:T(8,128)(2,1)}, bf16[8192,256]{1,0:T(8,128)(2,1)S(1)}, u32[]{:S(2)}, u32[]{:S(2)}) %collective-permute-start.2) | collective-permute-done | bytes 4194336 | tf_op jit(solution)/shard_map/ppermute | solution.py:523
  74.1 2.2 copy-done
  76.2 0.7 copy-done.2
  76.9 67.2 %attend.1.attended_ref = bf16[1024,512]{1,0:T(8,128)(2,1)S(1)} custom-call(s32[4]{0:T(128)S(1)} %copy-done.2, bf16[512,512]{1,0:T(8,128)(2,1)S(1)} %collective-permute-done.1.far_ref, bf16[512,512]{1,0:T(8,128)(2,1)S(1)} %get-tuple-element.23.near_ref, bf16[8192,256]{1,0:T(8,128)(2,1)S(1)} %copy-done, bf16[8192,256]{1,0:T(8,128)(2,1)S(1)} %collective-permute-done.2.other_ref), custom_call_target="tpu_custom_call" | custom-call | tf_op jit(solution)/shard_map/attend/pallas_call | solution.py:216
  144.1 0.0 copy-start.1
  144.1 1.0 copy-done.1
  145.1 8.6 %project.1 = bf16[1024,4096]{1,0:T(8,128)(2,1)} custom-call(bf16[1024,512]{1,0:T(8,128)(2,1)} %copy-done.1, bf16[16,512,256]{2,1,0:T(8,128)(2,1)} %bitcast.27), custom_call_target="tpu_custom_call" | custom-call | tf_op jit(solution)/shard_map/project/pallas_call | solution.py:240
  153.7 0.0 reduce-scatter.2.cloned.1.call-update
  153.7 0.7 copy-done.6
  154.4 0.1 copy.24
  154.5 0.1 eq.31
  154.6 0.1 eq.27
  154.7 0.1 copy.26
  154.8 0.1 copy-done.8
  155.0 4.9 %collective-permute-start.3 = (bf16[128,4096]{1,0:T(8,128)(2,1)S(1)}, bf16[128,4096]{1,0:T(8,128)(2,1)S(1)}, u32[]{:S(2)}, u32[]{:S(2)}) collective-permute-start(bf16[128,4096]{1,0:T(8,128)(2,1)S(1)} %copy-done.8), channel_id=1, source_target_pairs={{0,0},{1,1},{2,2},{3,3},{4,124},{5,125},{6,126},{7,127},{8,8},{9,9... | collective-permute-start | bytes 3145736 | tf_op jit(solution)/shard_map/ppermute | solution.py:536
  159.9 0.2 fusion.2
  160.2 0.2 fusion.1
  160.4 0.1 reduce_sum.12
  160.6 0.1 copy.28
  160.7 0.0 copy-start.5
  160.7 4.2 %collective-permute-start = (s32[128,4]{1,0:T(8,128)S(1)}, s32[128,4]{1,0:T(8,128)S(1)}, u32[]{:S(2)}, u32[]{:S(2)}) collective-permute-start(s32[128,4]{1,0:T(8,128)S(1)} %add.11.target_ref), channel_id=1, source_target_pairs={{0,0},{1,1},{2,2},{3,3},{4,124},{5,125},{6,126},{7,127},{8,8},{9,9... | collective-permute-start | bytes 6152 | tf_op jit(solution)/shard_map/ppermute | solution.py:536
  164.9 21.8 %collective-permute-done = s32[128,4]{1,0:T(8,128)S(1)} collective-permute-done((s32[128,4]{1,0:T(8,128)S(1)}, s32[128,4]{1,0:T(8,128)S(1)}, u32[]{:S(2)}, u32[]{:S(2)}) %collective-permute-start) | collective-permute-done | bytes 2080 | tf_op jit(solution)/shard_map/ppermute | solution.py:536
  186.7 0.7 copy.29.target_ref
  187.4 0.0 collective-permute-done.3.residual_ref
  187.4 16.6 %reduce-scatter.2.cloned.1.call-done.attn_ref = bf16[128,4096]{1,0:T(8,128)(2,1)} async-done(((bf16[1024,4096]{1,0:T(8,128)(2,1)}), bf16[128,4096]{1,0:T(8,128)(2,1)}) %reduce-scatter.2.cloned.1.call-update) | async-done | bytes 1048592 | tf_op jit(solution)/shard_map/reduce_scatter | solution.py:526
  204.0 6.3 %norm_and_dispatch.1 = (bf16[128,4096]{1,0:T(8,128)(2,1)}, bf16[128,48,512]{2,1,0:T(8,128)(2,1)}) custom-call(s32[4,128]{1,0:T(4,128)} %copy.29.target_ref, bf16[128,4096]{1,0:T(8,128)(2,1)} %reduce-scatter.2.cloned.1.call-done.attn_ref, bf16[128,4096]{1,0:T(8,128)(2,1)} %copy-done.4, f32[1,4096]{1,0:T(1,128)} %bitcast.31), custom_call_target="tpu_custom_call" | custom-call | tf_op jit(solution)/shard_map/norm_and_dispatch/pallas_call | solution.py:302
  210.4 83.5 %all_to_all.10 = bf16[128,48,512]{2,1,0:T(8,128)(2,1)} all-to-all(bf16[128,48,512]{2,1,0:T(8,128)(2,1)} %get-tuple-element.18), channel_id=1, replica_groups=mesh['ctx'=16,'tp'=8] {'ctx','tp'}, dimensions={0} | all-to-all | bytes 12582912 | tf_op jit(solution)/shard_map/all_to_all | solution.py:545
  293.9 0.0 copy-done.5
  293.9 4.1 collective-permute-start.4
  298.0 25.2 %expert.1 = bf16[6144,512]{1,0:T(8,128)(2,1)} custom-call(bf16[6144,512]{1,0:T(8,128)(2,1)} %bitcast.26, bf16[3,192,192]{2,1,0:T(8,128)(2,1)} %constant.48.clone.swap_ref, bf16[4096,1536]{1,0:T(8,128)(2,1)} %bitcast.33, bf16[768,4096]{1,0:T(8,128)(2,1)} %bitcast.34), custom_call_target="tpu_custom_call" | custom-call | flops 14495514624 | bytes 31457280 | tf_op jit(solution)/shard_map/expert/pallas_call | solution.py:415
  323.1 1.1 collective-permute-done.4.hidden_ref
  324.2 1.0 copy-done.3
  325.3 6.4 %all-to-all-start.1 = ((bf16[128,48,512]{2,1,0:T(8,128)(2,1)}), bf16[128,48,512]{2,1,0:T(8,128)(2,1)}, u32[]{:S(2)}, u32[]{:S(2)}) async-start(bf16[128,48,512]{2,1,0:T(8,128)(2,1)} %bitcast.25), calls=%async_computation.2 | async-start | bytes 12582912 | tf_op jit(solution)/shard_map/all_to_all | solution.py:545
  331.7 0.7 copy.30.route_ref
  332.4 74.9 %all-to-all-done.1 = bf16[128,48,512]{2,1,0:T(8,128)(2,1)} async-done(((bf16[128,48,512]{2,1,0:T(8,128)(2,1)}), bf16[128,48,512]{2,1,0:T(8,128)(2,1)}, u32[]{:S(2)}, u32[]{:S(2)}) %all-to-all-start.1) | async-done | bytes 6291488 | tf_op jit(solution)/shard_map/all_to_all | solution.py:545
  407.3 8.2 %combine.1 = bf16[128,4096]{1,0:T(8,128)(2,1)} custom-call(s32[128,4]{1,0:T(8,128)} %copy-done.5, f32[128,4]{1,0:T(8,128)} %copy.30.route_ref, bf16[128,4096]{1,0:T(8,128)(2,1)} %copy-done.3, bf16[3,192,192]{2,1,0:T(8,128)(2,1)} %constant.48.clone.swap_ref, bf16[6144,512]{1,0:T(8,128)(2,1)} %bitcast.14.back_ref), custom_call_target="tpu_custom_call" | custom-call | tf_op jit(solution)/shard_map/combine/pallas_call | solution.py:479
  (20 shorter events, 0.1 us)
Async XLA Ops:
  6.5 60.1 %all-gather.4.cloned.1.call-start = ((), (), s32[]{:S(2)}) async-start(), calls=%async_computation.3 | async-start | bytes 4456448 | tf_op jit(solution)/shard_map/all_gather | solution.py:521
  9.6 135.5 %all-gather.6.cloned.1.call-start = ((), (), s32[]{:S(2)}) async-start(), calls=%async_computation.5 | async-start | bytes 4456448 | tf_op jit(solution)/shard_map/all_gather | solution.py:524
  10.4 193.7 %reduce-scatter.2.cloned.1.call-start = ((), (), s32[]{:S(2)}) async-start(), calls=%async_computation.4 | async-start | bytes 9437184 | tf_op jit(solution)/shard_map/reduce_scatter | solution.py:526
  11.7 20.7 %collective-permute-start.1 = (bf16[512,512]{1,0:T(8,128)(2,1)S(1)}, bf16[512,512]{1,0:T(8,128)(2,1)S(1)}, u32[]{:S(2)}, u32[]{:S(2)}) collective-permute-start(bf16[512,512]{1,0:T(8,128)(2,1)S(1)} %get-tuple-element.24), channel_id=1, source_target_pairs={{0,120},{8,112},{16,104},{24,96},{32,88},{40,80},{48,72},{56,64},{... | collective-permute-start | bytes 1572872 | tf_op jit(solution)/shard_map/ppermute | solution.py:516
  66.7 7.4 %collective-permute-start.2 = (bf16[8192,256]{1,0:T(8,128)(2,1)}, bf16[8192,256]{1,0:T(8,128)(2,1)S(1)}, u32[]{:S(2)}, u32[]{:S(2)}) collective-permute-start(bf16[8192,256]{1,0:T(8,128)(2,1)} %all-gather.4.cloned.1.call-done.mine_ref), channel_id=1, source_target_pairs={{0,1},{1,0},{2,3},{3,2},{4,5},{5,4},{6,7},{7,6},{8,9},{9,8},{10,11... | collective-permute-start | bytes 12582920 | tf_op jit(solution)/shard_map/ppermute | solution.py:523
  74.1 2.2 copy-start
  76.2 0.7 copy-start.2
  144.1 1.0 copy-start.1
  153.7 0.7 copy-start.6
  153.7 1.2 copy-start.8
  155.0 32.5 %collective-permute-start.3 = (bf16[128,4096]{1,0:T(8,128)(2,1)S(1)}, bf16[128,4096]{1,0:T(8,128)(2,1)S(1)}, u32[]{:S(2)}, u32[]{:S(2)}) collective-permute-start(bf16[128,4096]{1,0:T(8,128)(2,1)S(1)} %copy-done.8), channel_id=1, source_target_pairs={{0,0},{1,1},{2,2},{3,3},{4,124},{5,125},{6,126},{7,127},{8,8},{9,9... | collective-permute-start | bytes 3145736 | tf_op jit(solution)/shard_map/ppermute | solution.py:536
  160.7 133.2 %copy-start.5 = (s32[128,4]{1,0:T(8,128)}, s32[128,4]{1,0:T(8,128)S(1)}, u32[]{:S(2)}) copy-start(s32[128,4]{1,0:T(8,128)S(1)} %add.11.target_ref) | copy-start | bytes 6148
  160.7 26.1 %collective-permute-start = (s32[128,4]{1,0:T(8,128)S(1)}, s32[128,4]{1,0:T(8,128)S(1)}, u32[]{:S(2)}, u32[]{:S(2)}) collective-permute-start(s32[128,4]{1,0:T(8,128)S(1)} %add.11.target_ref), channel_id=1, source_target_pairs={{0,0},{1,1},{2,2},{3,3},{4,124},{5,125},{6,126},{7,127},{8,8},{9,9... | collective-permute-start | bytes 6152 | tf_op jit(solution)/shard_map/ppermute | solution.py:536
  187.4 16.6 %copy-start.4 = (bf16[128,4096]{1,0:T(8,128)(2,1)}, bf16[128,4096]{1,0:T(8,128)(2,1)S(1)}, u32[]{:S(2)}) copy-start(bf16[128,4096]{1,0:T(8,128)(2,1)S(1)} %collective-permute-done.3.residual_ref) | copy-start | bytes 3145732
  210.4 83.5 %copy-start.9 = (bf16[128,4096]{1,0:T(8,128)(2,1)S(1)}, bf16[128,4096]{1,0:T(8,128)(2,1)}, u32[]{:S(2)}) copy-start(bf16[128,4096]{1,0:T(8,128)(2,1)} %get-tuple-element.19) | copy-start | bytes 3145732
  293.9 30.4 %collective-permute-start.4 = (bf16[128,4096]{1,0:T(8,128)(2,1)S(1)}, bf16[128,4096]{1,0:T(8,128)(2,1)S(1)}, u32[]{:S(2)}, u32[]{:S(2)}) collective-permute-start(bf16[128,4096]{1,0:T(8,128)(2,1)S(1)} %copy-done.9), channel_id=1, source_target_pairs={{0,0},{1,1},{2,2},{3,3},{4,124},{5,125},{6,126},{7,127},{8,8},{9,9... | collective-permute-start | bytes 3145736 | tf_op jit(solution)/shard_map/ppermute | solution.py:536
  324.2 1.0 copy-start.3
  324.2 7.4 %copy-start.7 = (f32[128,4]{0,1:T(4,128)S(1)}, f32[128,4]{0,1:T(4,128)}, u32[]{:S(2)}) copy-start(f32[128,4]{0,1:T(4,128)} %param.18) | copy-start | bytes 6148
  325.3 82.0 %all-to-all-start.1 = ((bf16[128,48,512]{2,1,0:T(8,128)(2,1)}), bf16[128,48,512]{2,1,0:T(8,128)(2,1)}, u32[]{:S(2)}, u32[]{:S(2)}) async-start(bf16[128,48,512]{2,1,0:T(8,128)(2,1)} %bitcast.25), calls=%async_computation.2 | async-start | bytes 12582912 | tf_op jit(solution)/shard_map/all_to_all | solution.py:545
Sparse Core Ops, SparseCore 0:
  9.7 56.9 all-gather.3
  68.8 51.2 all-gather.5
  153.9 50.1 reduce-scatter.1

commit v8 on v7

--- a/solution.py
+++ b/solution.py
@@ -25,6 +25,7 @@
 GROUP = 8
 GROUP_ROWS = GROUP * CAP
 DISPATCH_GROUPS = 8
+COMBINE_GROUPS = 8
 STEP_GROUPS = 4
 STEP_PIECES = 2
 PROJECT_WIDTH = 2048
@@ -441,8 +442,8 @@
 def combine_kernel(target_ref, route_ref, hidden_ref, swap_ref, back_ref, out_ref, rows_of):
     step = pl.program_id(0)
     group_block = GROUP_ROWS * PIECES
-    for part in range(STEP_GROUPS):
-        to = (step * STEP_GROUPS + part) * GROUP_ROWS
+    for part in range(COMBINE_GROUPS):
+        to = (step * COMBINE_GROUPS + part) * GROUP_ROWS
         to = pl.ds(pl.multiple_of(to, GROUP_ROWS), GROUP_ROWS)
         unpack_group(swap_ref, 0, back_ref, part * group_block, rows_of, to)
 
@@ -478,14 +479,14 @@
 
     return pl.pallas_call(
         combine_kernel,
-        grid=(slots // (GROUP_ROWS * STEP_GROUPS),),
+        grid=(slots // (GROUP_ROWS * COMBINE_GROUPS),),
         out_shape=jax.ShapeDtypeStruct((tokens, model), jnp.bfloat16),
         in_specs=[
             whole((tokens, TOPK)),
             whole((tokens, TOPK)),
             whole((tokens, model)),
             pl.BlockSpec(swap.shape, lambda step: (0, 0, 0)),
-            pl.BlockSpec((STEP_GROUPS * group_block, PIECE), lambda step: (step, 0)),
+            pl.BlockSpec((COMBINE_GROUPS * group_block, PIECE), lambda step: (step, 0)),
         ],
         out_specs=whole((tokens, model)),
         scratch_shapes=[pltpu.VMEM((PIECES, slots, PIECE), jnp.bfloat16)],

time: 425 us -> 425 us (level)
  no operation moved by 1% of the time
where the time goes in v8:
time: 425 us; the launch traced here: 421 us
  waiting for transfers between devices  171 us (40%)
  Pallas kernels  117 us (28%)
  blocking collectives  83.5 us (20%)
  starting transfers between devices  26.3 us (6%)
  between operations  13.2 us (3%)
  local copies, waits for them, and re-layouts  9.02 us (2%)
    all_to_all x1, blocking collectives, exchange(): lax.all_to_all(shaped, ('ctx', 'tp'), split_axis=0, concat_axis=0, tiled=...  83.5 us
    all_to_all x1, waiting for transfers between devices, exchange(): lax.all_to_all(shaped, ('ctx', 'tp'), split_axis=0, concat_axis=0, tiled=...  74.9 us
    pallas_call x1, Pallas kernels, attend(): pl.pallas_call(attend_kernel, out_shape=jax.ShapeDtypeStruct((2 * rows, c...  67.2 us
    all_gather x1, waiting for transfers between devices, body(): lax.all_gather(own_half(place, keys, values, half), 'ctx', axis=0, tiled=...  34.3 us
    pallas_call x1, Pallas kernels, run_expert(): pl.pallas_call(expert_kernel, out_shape=jax.ShapeDtypeStruct(arrived.shap...  25.2 us
    ppermute x3, waiting for transfers between devices, trade(): return lax.ppermute(array, ('ctx', 'tp'), home)  22.9 us
    reduce_scatter x1, waiting for transfers between devices, body(): lax.psum_scatter(projected, 'tp', scatter_dimension=0, tiled=True)  16.6 us
    ppermute x1, waiting for transfers between devices, body(): swapped = lax.ppermute(queries[half:], 'ctx', opposite)  14.2 us
  transfers between devices with their start and end apart: 9, of which 7 were waited for; matrix products, arithmetic and copies ran while one was open for 1% of the time, Pallas kernels for 22%

profile of v8, /device:TPU:6, one launch (start us, length us, event | category | flops | bytes accessed | tf_op | source)
XLA Modules:
  0.0 421.2 jit_solution(16868808218612787376)
XLA Ops:
  6.5 0.0 all-gather.4.cloned.1.call-start
  6.5 0.7 pad_add_fusion.place_ref
  7.2 2.4 own_half.1
  9.6 0.0 all-gather.4.cloned.1.call-update
  9.6 0.0 all-gather.6.cloned.1.call-start
  9.7 0.7 all-gather.6.cloned.1.call-update
  10.4 0.0 reduce-scatter.2.cloned.1.call-start
  10.4 1.3 fusion.5
  11.7 6.6 %collective-permute-start.1 = (bf16[512,512]{1,0:T(8,128)(2,1)S(1)}, bf16[512,512]{1,0:T(8,128)(2,1)S(1)}, u32[]{:S(2)}, u32[]{:S(2)}) collective-permute-start(bf16[512,512]{1,0:T(8,128)(2,1)S(1)} %get-tuple-element.24), channel_id=1, source_target_pairs={{0,120},{8,112},{16,104},{24,96},{32,88},{40,80},{48,72},{56,64},{... | collective-permute-start | bytes 1572872 | tf_op jit(solution)/shard_map/ppermute | solution.py:517
  18.3 14.2 %collective-permute-done.1.far_ref = bf16[512,512]{1,0:T(8,128)(2,1)S(1)} collective-permute-done((bf16[512,512]{1,0:T(8,128)(2,1)S(1)}, bf16[512,512]{1,0:T(8,128)(2,1)S(1)}, u32[]{:S(2)}, u32[]{:S(2)}) %collective-permute-start.1) | collective-permute-done | bytes 524320 | tf_op jit(solution)/shard_map/ppermute | solution.py:517
  32.4 34.3 %all-gather.4.cloned.1.call-done.mine_ref = bf16[8192,256]{1,0:T(8,128)(2,1)} async-done(((bf16[512,256]{1,0:T(8,128)(2,1)}), bf16[8192,256]{1,0:T(8,128)(2,1)}) %all-gather.4.cloned.1.call-update) | async-done | bytes 4194320 | tf_op jit(solution)/shard_map/all_gather | solution.py:522
  66.7 0.0 collective-permute-start.2
  66.7 7.4 %collective-permute-done.2.other_ref = bf16[8192,256]{1,0:T(8,128)(2,1)S(1)} collective-permute-done((bf16[8192,256]{1,0:T(8,128)(2,1)}, bf16[8192,256]{1,0:T(8,128)(2,1)S(1)}, u32[]{:S(2)}, u32[]{:S(2)}) %collective-permute-start.2) | collective-permute-done | bytes 4194336 | tf_op jit(solution)/shard_map/ppermute | solution.py:524
  74.1 2.2 copy-done
  76.2 0.7 copy-done.2
  76.9 67.2 %attend.1.attended_ref = bf16[1024,512]{1,0:T(8,128)(2,1)S(1)} custom-call(s32[4]{0:T(128)S(1)} %copy-done.2, bf16[512,512]{1,0:T(8,128)(2,1)S(1)} %collective-permute-done.1.far_ref, bf16[512,512]{1,0:T(8,128)(2,1)S(1)} %get-tuple-element.23.near_ref, bf16[8192,256]{1,0:T(8,128)(2,1)S(1)} %copy-done, bf16[8192,256]{1,0:T(8,128)(2,1)S(1)} %collective-permute-done.2.other_ref), custom_call_target="tpu_custom_call" | custom-call | tf_op jit(solution)/shard_map/attend/pallas_call | solution.py:217
  144.1 0.0 copy-start.1
  144.1 1.0 copy-done.1
  145.1 8.6 %project.1 = bf16[1024,4096]{1,0:T(8,128)(2,1)} custom-call(bf16[1024,512]{1,0:T(8,128)(2,1)} %copy-done.1, bf16[16,512,256]{2,1,0:T(8,128)(2,1)} %bitcast.27), custom_call_target="tpu_custom_call" | custom-call | tf_op jit(solution)/shard_map/project/pallas_call | solution.py:241
  153.7 0.0 reduce-scatter.2.cloned.1.call-update
  153.7 0.7 copy-done.6
  154.4 0.1 copy.24
  154.5 0.1 eq.31
  154.6 0.1 eq.27
  154.7 0.1 copy.26
  154.8 0.1 copy-done.8
  155.0 4.9 %collective-permute-start.3 = (bf16[128,4096]{1,0:T(8,128)(2,1)S(1)}, bf16[128,4096]{1,0:T(8,128)(2,1)S(1)}, u32[]{:S(2)}, u32[]{:S(2)}) collective-permute-start(bf16[128,4096]{1,0:T(8,128)(2,1)S(1)} %copy-done.8), channel_id=1, source_target_pairs={{0,0},{1,1},{2,2},{3,3},{4,124},{5,125},{6,126},{7,127},{8,8},{9,9... | collective-permute-start | bytes 3145736 | tf_op jit(solution)/shard_map/ppermute | solution.py:537
  159.9 0.2 fusion.2
  160.2 0.2 fusion.1
  160.4 0.1 reduce_sum.12
  160.6 0.1 copy.28
  160.7 4.2 %collective-permute-start = (s32[128,4]{1,0:T(8,128)S(1)}, s32[128,4]{1,0:T(8,128)S(1)}, u32[]{:S(2)}, u32[]{:S(2)}) collective-permute-start(s32[128,4]{1,0:T(8,128)S(1)} %add.11.target_ref), channel_id=1, source_target_pairs={{0,0},{1,1},{2,2},{3,3},{4,124},{5,125},{6,126},{7,127},{8,8},{9,9... | collective-permute-start | bytes 6152 | tf_op jit(solution)/shard_map/ppermute | solution.py:537
  164.9 21.8 %collective-permute-done = s32[128,4]{1,0:T(8,128)S(1)} collective-permute-done((s32[128,4]{1,0:T(8,128)S(1)}, s32[128,4]{1,0:T(8,128)S(1)}, u32[]{:S(2)}, u32[]{:S(2)}) %collective-permute-start) | collective-permute-done | bytes 2080 | tf_op jit(solution)/shard_map/ppermute | solution.py:537
  186.7 0.7 copy.29.target_ref
  187.4 0.0 collective-permute-done.3.residual_ref
  187.4 16.6 %reduce-scatter.2.cloned.1.call-done.attn_ref = bf16[128,4096]{1,0:T(8,128)(2,1)} async-done(((bf16[1024,4096]{1,0:T(8,128)(2,1)}), bf16[128,4096]{1,0:T(8,128)(2,1)}) %reduce-scatter.2.cloned.1.call-update) | async-done | bytes 1048592 | tf_op jit(solution)/shard_map/reduce_scatter | solution.py:527
  204.0 0.0 copy-done.4
  204.0 6.3 %norm_and_dispatch.1 = (bf16[128,4096]{1,0:T(8,128)(2,1)}, bf16[128,48,512]{2,1,0:T(8,128)(2,1)}) custom-call(s32[4,128]{1,0:T(4,128)} %copy.29.target_ref, bf16[128,4096]{1,0:T(8,128)(2,1)} %reduce-scatter.2.cloned.1.call-done.attn_ref, bf16[128,4096]{1,0:T(8,128)(2,1)} %copy-done.4, f32[1,4096]{1,0:T(1,128)} %bitcast.31), custom_call_target="tpu_custom_call" | custom-call | tf_op jit(solution)/shard_map/norm_and_dispatch/pallas_call | solution.py:303
  210.4 83.5 %all_to_all.10 = bf16[128,48,512]{2,1,0:T(8,128)(2,1)} all-to-all(bf16[128,48,512]{2,1,0:T(8,128)(2,1)} %get-tuple-element.18), channel_id=1, replica_groups=mesh['ctx'=16,'tp'=8] {'ctx','tp'}, dimensions={0} | all-to-all | bytes 12582912 | tf_op jit(solution)/shard_map/all_to_all | solution.py:546
  293.9 4.1 collective-permute-start.4
  298.0 25.2 %expert.1 = bf16[6144,512]{1,0:T(8,128)(2,1)} custom-call(bf16[6144,512]{1,0:T(8,128)(2,1)} %bitcast.26, bf16[3,192,192]{2,1,0:T(8,128)(2,1)} %constant.48.clone.swap_ref, bf16[4096,1536]{1,0:T(8,128)(2,1)} %bitcast.33, bf16[768,4096]{1,0:T(8,128)(2,1)} %bitcast.34), custom_call_target="tpu_custom_call" | custom-call | flops 14495514624 | bytes 31457280 | tf_op jit(solution)/shard_map/expert/pallas_call | solution.py:416
  323.1 1.1 collective-permute-done.4.hidden_ref
  324.2 1.0 copy-done.3
  325.3 6.4 %all-to-all-start.1 = ((bf16[128,48,512]{2,1,0:T(8,128)(2,1)}), bf16[128,48,512]{2,1,0:T(8,128)(2,1)}, u32[]{:S(2)}, u32[]{:S(2)}) async-start(bf16[128,48,512]{2,1,0:T(8,128)(2,1)} %bitcast.25), calls=%async_computation.2 | async-start | bytes 12582912 | tf_op jit(solution)/shard_map/all_to_all | solution.py:546
  331.7 0.0 copy-done.7
  331.7 0.7 copy.30.route_ref
  332.4 74.9 %all-to-all-done.1 = bf16[128,48,512]{2,1,0:T(8,128)(2,1)} async-done(((bf16[128,48,512]{2,1,0:T(8,128)(2,1)}), bf16[128,48,512]{2,1,0:T(8,128)(2,1)}, u32[]{:S(2)}, u32[]{:S(2)}) %all-to-all-start.1) | async-done | bytes 6291488 | tf_op jit(solution)/shard_map/all_to_all | solution.py:546
  407.3 7.4 %combine.1 = bf16[128,4096]{1,0:T(8,128)(2,1)} custom-call(s32[128,4]{1,0:T(8,128)} %copy-done.5, f32[128,4]{1,0:T(8,128)} %copy.30.route_ref, bf16[128,4096]{1,0:T(8,128)(2,1)} %copy-done.3, bf16[3,192,192]{2,1,0:T(8,128)(2,1)} %constant.48.clone.swap_ref, bf16[6144,512]{1,0:T(8,128)(2,1)} %bitcast.14.back_ref), custom_call_target="tpu_custom_call" | custom-call | tf_op jit(solution)/shard_map/combine/pallas_call | solution.py:480
  (20 shorter events, 0.1 us)
Async XLA Ops:
  6.5 60.1 %all-gather.4.cloned.1.call-start = ((), (), s32[]{:S(2)}) async-start(), calls=%async_computation.3 | async-start | bytes 4456448 | tf_op jit(solution)/shard_map/all_gather | solution.py:522
  9.6 135.5 %all-gather.6.cloned.1.call-start = ((), (), s32[]{:S(2)}) async-start(), calls=%async_computation.5 | async-start | bytes 4456448 | tf_op jit(solution)/shard_map/all_gather | solution.py:525
  10.4 193.7 %reduce-scatter.2.cloned.1.call-start = ((), (), s32[]{:S(2)}) async-start(), calls=%async_computation.4 | async-start | bytes 9437184 | tf_op jit(solution)/shard_map/reduce_scatter | solution.py:527
  11.7 20.7 %collective-permute-start.1 = (bf16[512,512]{1,0:T(8,128)(2,1)S(1)}, bf16[512,512]{1,0:T(8,128)(2,1)S(1)}, u32[]{:S(2)}, u32[]{:S(2)}) collective-permute-start(bf16[512,512]{1,0:T(8,128)(2,1)S(1)} %get-tuple-element.24), channel_id=1, source_target_pairs={{0,120},{8,112},{16,104},{24,96},{32,88},{40,80},{48,72},{56,64},{... | collective-permute-start | bytes 1572872 | tf_op jit(solution)/shard_map/ppermute | solution.py:517
  66.7 7.4 %collective-permute-start.2 = (bf16[8192,256]{1,0:T(8,128)(2,1)}, bf16[8192,256]{1,0:T(8,128)(2,1)S(1)}, u32[]{:S(2)}, u32[]{:S(2)}) collective-permute-start(bf16[8192,256]{1,0:T(8,128)(2,1)} %all-gather.4.cloned.1.call-done.mine_ref), channel_id=1, source_target_pairs={{0,1},{1,0},{2,3},{3,2},{4,5},{5,4},{6,7},{7,6},{8,9},{9,8},{10,11... | collective-permute-start | bytes 12582920 | tf_op jit(solution)/shard_map/ppermute | solution.py:524
  74.1 2.2 copy-start
  76.2 0.7 copy-start.2
  144.1 1.0 copy-start.1
  153.7 0.7 copy-start.6
  153.7 1.2 copy-start.8
  155.0 32.5 %collective-permute-start.3 = (bf16[128,4096]{1,0:T(8,128)(2,1)S(1)}, bf16[128,4096]{1,0:T(8,128)(2,1)S(1)}, u32[]{:S(2)}, u32[]{:S(2)}) collective-permute-start(bf16[128,4096]{1,0:T(8,128)(2,1)S(1)} %copy-done.8), channel_id=1, source_target_pairs={{0,0},{1,1},{2,2},{3,3},{4,124},{5,125},{6,126},{7,127},{8,8},{9,9... | collective-permute-start | bytes 3145736 | tf_op jit(solution)/shard_map/ppermute | solution.py:537
  160.7 133.2 %copy-start.5 = (s32[128,4]{1,0:T(8,128)}, s32[128,4]{1,0:T(8,128)S(1)}, u32[]{:S(2)}) copy-start(s32[128,4]{1,0:T(8,128)S(1)} %add.11.target_ref) | copy-start | bytes 6148
  160.7 26.1 %collective-permute-start = (s32[128,4]{1,0:T(8,128)S(1)}, s32[128,4]{1,0:T(8,128)S(1)}, u32[]{:S(2)}, u32[]{:S(2)}) collective-permute-start(s32[128,4]{1,0:T(8,128)S(1)} %add.11.target_ref), channel_id=1, source_target_pairs={{0,0},{1,1},{2,2},{3,3},{4,124},{5,125},{6,126},{7,127},{8,8},{9,9... | collective-permute-start | bytes 6152 | tf_op jit(solution)/shard_map/ppermute | solution.py:537
  187.4 16.6 %copy-start.4 = (bf16[128,4096]{1,0:T(8,128)(2,1)}, bf16[128,4096]{1,0:T(8,128)(2,1)S(1)}, u32[]{:S(2)}) copy-start(bf16[128,4096]{1,0:T(8,128)(2,1)S(1)} %collective-permute-done.3.residual_ref) | copy-start | bytes 3145732
  210.4 83.5 %copy-start.9 = (bf16[128,4096]{1,0:T(8,128)(2,1)S(1)}, bf16[128,4096]{1,0:T(8,128)(2,1)}, u32[]{:S(2)}) copy-start(bf16[128,4096]{1,0:T(8,128)(2,1)} %get-tuple-element.19) | copy-start | bytes 3145732
  293.9 30.4 %collective-permute-start.4 = (bf16[128,4096]{1,0:T(8,128)(2,1)S(1)}, bf16[128,4096]{1,0:T(8,128)(2,1)S(1)}, u32[]{:S(2)}, u32[]{:S(2)}) collective-permute-start(bf16[128,4096]{1,0:T(8,128)(2,1)S(1)} %copy-done.9), channel_id=1, source_target_pairs={{0,0},{1,1},{2,2},{3,3},{4,124},{5,125},{6,126},{7,127},{8,8},{9,9... | collective-permute-start | bytes 3145736 | tf_op jit(solution)/shard_map/ppermute | solution.py:537
  324.2 1.0 copy-start.3
  324.2 7.4 %copy-start.7 = (f32[128,4]{0,1:T(4,128)S(1)}, f32[128,4]{0,1:T(4,128)}, u32[]{:S(2)}) copy-start(f32[128,4]{0,1:T(4,128)} %param.18) | copy-start | bytes 6148
  325.3 82.0 %all-to-all-start.1 = ((bf16[128,48,512]{2,1,0:T(8,128)(2,1)}), bf16[128,48,512]{2,1,0:T(8,128)(2,1)}, u32[]{:S(2)}, u32[]{:S(2)}) async-start(bf16[128,48,512]{2,1,0:T(8,128)(2,1)} %bitcast.25), calls=%async_computation.2 | async-start | bytes 12582912 | tf_op jit(solution)/shard_map/all_to_all | solution.py:546
Sparse Core Ops, SparseCore 0:
  9.7 56.9 all-gather.3
  68.8 51.2 all-gather.5
  153.9 50.1 reduce-scatter.1
